TPU v7x, 512 devices: a whole 4x4x16 slice. The times are simulated.
512 devices in a mesh: dp: 16 (over x_lo, y, core), expert: 32 (over z, x_hi).
Axes of the slice: x: 4 (x_hi: 2, x_lo: 2; x = x_hi * 2 + x_lo), y: 4, z: 16, core: 2. Of those that a mesh axis runs over, the one named last changes fastest.
Arguments:
- grad_out: bfloat16 [16384, 2048], P(('dp', 'expert')), may hold values from -6 to 6
- expert_ids: int32 [16384, 8], P(('dp', 'expert')), may hold values from 0 to 31, all different within a row; in each aligned block of 32 rows (0 to 31, 32 to 63, ...) at most 12 rows name the same one
- route_weights: bfloat16 [16384, 8], P(('dp', 'expert')), may hold values from 0.049804688 to 0.5
- saved_pre: bfloat16 [16, 32, 384, 1536], P('dp', 'expert'), may hold values from -6 to 6
- gate_weight: bfloat16 [32, 2048, 768], P('expert', 'dp'), may hold values from -0.125 to 0.125
- up_weight: bfloat16 [32, 2048, 768], P('expert', 'dp'), may hold values from -0.125 to 0.125
- down_weight: bfloat16 [32, 768, 2048], P('expert', 'dp'), may hold values from -0.21875 to 0.21875
Outputs:
- token_grad: bfloat16 [16384, 2048], P(('dp', 'expert'))
- route_grad: bfloat16 [16384, 8], P(('dp', 'expert'))
- down_grad: bfloat16 [32, 768, 2048], P('expert', 'dp')
Inputs may be any that keep to these rules, and one draw needn't show every extreme that they name: `expert_ids`: each row names 8 different experts. Among the 32 rows of one device no expert is named by more than 12 rows, a bound that some block reaches.
All inputs are finite; a program needn't handle non-finite values.
Results may differ from a plain program's by a relative error of at most 0.023.
Values may be sent and summed in bfloat16 or wider, within the bound.
No kernel may reach another device: no remote copies, remote signals or barrier semaphores. Data moves between devices by JAX's collectives and lax.ppermute only.
A program may use at most 64 MiB of HBM per device.

v0:
```python
import jax
import jax.numpy as jnp
from jax import lax
from jax.sharding import PartitionSpec as P


def per_device(grad_out, expert_ids, route_weights, saved_pre, gate_weight, up_weight, down_weight):
    experts = lax.axis_size("expert")
    pre_local = saved_pre[0, 0]
    slot_count = pre_local.shape[0]
    capacity = slot_count // experts
    hidden = pre_local.shape[1] // 2
    tok_count, width = grad_out.shape
    matches = (expert_ids[:, :, None] == jnp.arange(experts, dtype=jnp.int32)).astype(jnp.int32)
    members = jnp.sum(matches, axis=1)
    rank_tok = jnp.cumsum(members, axis=0) - members
    places = jnp.arange(capacity, dtype=jnp.int32)
    onehot = (members.T[:, None, :] == 1) & (rank_tok.T[:, None, :] == places[None, :, None])
    select = onehot.reshape(slot_count, tok_count).astype(jnp.bfloat16)
    send_rows = jnp.dot(select, grad_out, preferred_element_type=jnp.float32).astype(jnp.bfloat16)
    send_rows = send_rows.reshape(experts, capacity, width)
    weight_te = jnp.sum(route_weights.astype(jnp.float32)[:, :, None] * matches, axis=1)
    send_weight = jnp.sum(onehot * weight_te.T[:, None, :], axis=2).astype(jnp.bfloat16)
    got_rows, got_weight = (
        lax.all_to_all(send_rows, "expert", split_axis=0, concat_axis=0, tiled=True),
        lax.all_to_all(send_weight, "expert", split_axis=0, concat_axis=0, tiled=True),
    )
    slot_y = got_rows.reshape(slot_count, width)
    slot_weight = got_weight.reshape(slot_count).astype(jnp.float32)
    down_local = down_weight[0]
    q_slot = lax.dot_general(
        slot_y,
        lax.all_gather(down_local, "dp", axis=0, tiled=True),
        (((1,), (1,)), ((), ())),
        preferred_element_type=jnp.float32,
    )
    gate_pre = pre_local[:, :hidden].astype(jnp.float32)
    up_pre = pre_local[:, hidden:].astype(jnp.float32)
    sigmoid_gate = jax.nn.sigmoid(gate_pre)
    silu_gate = gate_pre * sigmoid_gate
    hidden_act = (silu_gate * up_pre).astype(jnp.bfloat16)
    hidden_f32 = lax.optimization_barrier(hidden_act).astype(jnp.float32)
    scaled = (slot_weight[:, None] * slot_y.astype(jnp.float32)).astype(jnp.bfloat16)
    slot_route = jnp.sum(q_slot * hidden_f32, axis=-1).astype(jnp.bfloat16)
    grad_hidden = slot_weight[:, None] * q_slot
    grad_gate = grad_hidden * up_pre * sigmoid_gate * (1.0 + gate_pre * (1.0 - sigmoid_gate))
    grad_up = grad_hidden * silu_gate
    grad_both = jnp.concatenate([grad_gate, grad_up], axis=1).astype(jnp.bfloat16)
    gate_up = jnp.concatenate([gate_weight[0], up_weight[0]], axis=1)
    slot_dx = lax.dot_general(
        grad_both,
        lax.all_gather(gate_up, "dp", axis=0, tiled=True),
        (((1,), (1,)), ((), ())),
        preferred_element_type=jnp.float32,
    ).astype(jnp.bfloat16)
    down_part = lax.psum_scatter(
        lax.dot_general(
            hidden_act, scaled, (((0,), (0,)), ((), ())), preferred_element_type=jnp.float32
        ).astype(jnp.bfloat16),
        "dp",
        scatter_dimension=0,
        tiled=True,
    )
    back_rows = slot_dx.reshape(experts, capacity, width)
    back_route = slot_route.reshape(experts, capacity)
    ret_rows, ret_route = (
        lax.all_to_all(back_rows, "expert", split_axis=0, concat_axis=0, tiled=True),
        lax.all_to_all(back_route, "expert", split_axis=0, concat_axis=0, tiled=True),
    )
    token_grad = lax.dot_general(
        select,
        ret_rows.reshape(slot_count, width),
        (((0,), (0,)), ((), ())),
        preferred_element_type=jnp.float32,
    )
    route_te = jnp.sum(onehot * ret_route.astype(jnp.float32)[:, :, None], axis=1)
    route_grad = jnp.sum(matches * route_te.T[:, None, :], axis=2)
    down_grad = down_part[None]
    return (token_grad.astype(jnp.bfloat16), route_grad.astype(jnp.bfloat16), down_grad)


def solution(mesh):
    return jax.shard_map(
        per_device,
        mesh=mesh,
        in_specs=(
            P(("dp", "expert"), None),
            P(("dp", "expert"), None),
            P(("dp", "expert"), None),
            P("dp", "expert", None, None),
            P("expert", "dp", None),
            P("expert", "dp", None),
            P("expert", "dp", None),
        ),
        out_specs=(P(("dp", "expert"), None), P(("dp", "expert"), None), P("expert", "dp", None)),
        check_vma=False,
    )
```

profile of v0, /device:TPU:1, one launch (start us, length us, event | category | flops | bytes accessed | tf_op | source)
XLA Modules:
  0.0 291.2 jit_solution(9991133279368327822)
XLA Ops:
  7.2 0.7 all-gather.6.cloned.1.call-update
  8.0 1.8 pad_maximum_fusion
  9.8 0.8 copy.58
  10.5 0.1 convert_reduce_fusion
  10.9 0.1 copy.59
  11.0 0.1 eq.58
  11.2 0.6 convolution_convert_fusion.1
  11.8 1.5 reshape.68
  13.3 18.6 %all-to-all-start.1 = ((bf16[32,12,2048]{2,1,0:T(8,128)(2,1)}), bf16[32,12,2048]{2,1,0:T(8,128)(2,1)S(1)}, u32[]{:S(2)}, u32[]{:S(2)}) async-start(bf16[32,12,2048]{2,1,0:T(8,128)(2,1)} %reshape.68), calls=%async_computation.1 | async-start | bytes 4194304 | tf_op jit(solution)/shard_map/all_to_all | solution.py:25
  31.9 1.2 fusion.8
  33.1 0.1 copy.61
  33.2 95.1 %all-to-all-done.1 = bf16[32,12,2048]{2,1,0:T(8,128)(2,1)S(1)} async-done(((bf16[32,12,2048]{2,1,0:T(8,128)(2,1)}), bf16[32,12,2048]{2,1,0:T(8,128)(2,1)S(1)}, u32[]{:S(2)}, u32[]{:S(2)}) %all-to-all-start.1) | async-done | bytes 1572896 | tf_op jit(solution)/shard_map/all_to_all | solution.py:25
  128.3 1.3 reshape.69
  129.7 4.0 %multiply_reduce_fusion = (bf16[384]{0:T(512)(128)(2,1)S(1)}, f32[384,768]{1,0:T(8,128)S(1)}) fusion(bf16[384,768]{1,0:T(8,128)(2,1)} %fusion.8, bf16[384,2048]{1,0:T(8,128)(2,1)} %reshape.69, bf16[1,768,2048]{2,1,0:T(8,128)(2,1)} %all-gather.6.cloned.1.call-done), kind=kOutput, calls=%fused_computation.26 | convolution fusion | flops 1208843904 | bytes 6488832 | tf_op jit(solution)/shard_map/dot_general | solution.py:31
  133.6 0.7 convert_element_type.118
  134.4 8.3 %all-to-all-start.3 = ((bf16[32,1,12]{2,1,0:T(2,128)(2,1)}), bf16[32,1,12]{2,1,0:T(2,128)(2,1)S(1)}, u32[]{:S(2)}, u32[]{:S(2)}) async-start(bf16[32,1,12]{2,1,0:T(2,128)(2,1)} %convert_element_type.118), calls=%async_computation.3 | async-start | bytes 32768 | tf_op jit(solution)/shard_map/all_to_all | solution.py:68
  142.7 0.1 fusion.22
  142.9 13.3 %all-to-all-done.3 = bf16[32,1,12]{2,1,0:T(2,128)(2,1)S(1)} async-done(((bf16[32,1,12]{2,1,0:T(2,128)(2,1)}), bf16[32,1,12]{2,1,0:T(2,128)(2,1)S(1)}, u32[]{:S(2)}, u32[]{:S(2)}) %all-to-all-start.3) | async-done | bytes 800 | tf_op jit(solution)/shard_map/all_to_all | solution.py:68
  156.2 0.3 select_reduce_fusion
  156.5 0.1 copy.63
  156.6 0.1 copy.64
  156.7 16.5 %all_to_all.22 = bf16[32,1,12]{2,1,0:T(2,128)(2,1)S(1)} all-to-all(bf16[32,1,12]{2,1,0:T(2,128)(2,1)S(1)} %copy.64), channel_id=1, replica_groups=mesh['dp'=16,'expert'=32] {'expert'}, dimensions={0} | all-to-all | bytes 1536 | tf_op jit(solution)/shard_map/all_to_all | solution.py:26
  173.3 0.1 reshape.71
  173.4 1.5 fusion.7
  174.9 5.6 %convolution_convert_fusion.2 = bf16[384,2048]{1,0:T(8,128)(2,1)S(1)} fusion(bf16[2048,1536]{1,0:T(8,128)(2,1)} %all-gather.4.cloned.1.call-done, bf16[384,768]{1,0:T(8,128)(2,1)} %get-tuple-element.12, bf16[384,768]{1,0:T(8,128)(2,1)S(1)} %get-tuple-element.11), kind=kOutput, calls=%fused_computation.5 | convolution fusion | flops 2419064832 | bytes 9043968 | tf_op jit(solution)/shard_map/dot_general | solution.py:50
  180.5 1.6 reshape.70
  182.1 4.1 %all-to-all-start.2 = ((bf16[32,12,2048]{2,1,0:T(8,128)(2,1)}), bf16[32,12,2048]{2,1,0:T(8,128)(2,1)S(1)}, u32[]{:S(2)}, u32[]{:S(2)}) async-start(bf16[32,12,2048]{2,1,0:T(8,128)(2,1)} %reshape.70), calls=%async_computation.2 | async-start | bytes 4194304 | tf_op jit(solution)/shard_map/all_to_all | solution.py:67
  186.3 5.0 %convolution_convert_fusion = bf16[768,2048]{1,0:T(8,128)(2,1)} fusion(bf16[384,768]{1,0:T(8,128)(2,1)S(1)} %copy-done.2, bf16[384,2048]{1,0:T(8,128)(2,1)} %reshape.69, f32[384]{0:T(512)S(1)} %reshape.71), kind=kOutput, calls=%fused_computation | convolution fusion | flops 1211891712 | bytes 5309952 | tf_op jit(solution)/shard_map/dot_general | solution.py:57
  191.4 0.2 fusion.23
  191.6 0.7 copy.69
  192.3 90.7 %all-to-all-done.2 = bf16[32,12,2048]{2,1,0:T(8,128)(2,1)S(1)} async-done(((bf16[32,12,2048]{2,1,0:T(8,128)(2,1)}), bf16[32,12,2048]{2,1,0:T(8,128)(2,1)S(1)}, u32[]{:S(2)}, u32[]{:S(2)}) %all-to-all-start.2) | async-done | bytes 1572896 | tf_op jit(solution)/shard_map/all_to_all | solution.py:67
  283.0 1.7 fusion.2
  (30 shorter events, 0.7 us)
Async XLA Ops:
  7.2 4.0 %copy-start = (bf16[32,2048]{1,0:T(8,128)(2,1)S(1)}, bf16[32,2048]{1,0:T(8,128)(2,1)}, u32[]{:S(2)}) copy-start(bf16[32,2048]{1,0:T(8,128)(2,1)} %param.7) | copy-start | bytes 393220
  7.2 122.5 %all-gather.6.cloned.1.call-start = ((), (), s32[]{:S(2)}) async-start(), calls=%async_computation.7 | async-start | bytes 3342336 | tf_op jit(solution)/shard_map/all_gather | solution.py:33
  7.9 167.0 %all-gather.4.cloned.1.call-start = ((), (), s32[]{:S(2)}) async-start(), calls=%async_computation.5 | async-start | bytes 6684672 | tf_op jit(solution)/shard_map/all_gather | solution.py:52
  13.3 18.6 %copy-start.1 = (bf16[1,1,384,1536]{3,2,1,0:T(8,128)(2,1)S(1)}, bf16[1,1,384,1536]{3,2,1,0:T(8,128)(2,1)}, u32[]{:S(2)}) copy-start(bf16[1,1,384,1536]{3,2,1,0:T(8,128)(2,1)} %param.10) | copy-start | bytes 3538948
  13.3 115.0 %all-to-all-start.1 = ((bf16[32,12,2048]{2,1,0:T(8,128)(2,1)}), bf16[32,12,2048]{2,1,0:T(8,128)(2,1)S(1)}, u32[]{:S(2)}, u32[]{:S(2)}) async-start(bf16[32,12,2048]{2,1,0:T(8,128)(2,1)} %reshape.68), calls=%async_computation.1 | async-start | bytes 4194304 | tf_op jit(solution)/shard_map/all_to_all | solution.py:25
  31.9 1.2 copy-start.3
  134.4 21.8 %all-to-all-start.3 = ((bf16[32,1,12]{2,1,0:T(2,128)(2,1)}), bf16[32,1,12]{2,1,0:T(2,128)(2,1)S(1)}, u32[]{:S(2)}, u32[]{:S(2)}) async-start(bf16[32,1,12]{2,1,0:T(2,128)(2,1)} %convert_element_type.118), calls=%async_computation.3 | async-start | bytes 32768 | tf_op jit(solution)/shard_map/all_to_all | solution.py:68
  182.1 4.2 %copy-start.2 = (bf16[384,768]{1,0:T(8,128)(2,1)S(1)}, bf16[384,768]{1,0:T(8,128)(2,1)}, u32[]{:S(2)}) copy-start(bf16[384,768]{1,0:T(8,128)(2,1)} %fusion.8) | copy-start | bytes 1769476
  182.1 100.9 %all-to-all-start.2 = ((bf16[32,12,2048]{2,1,0:T(8,128)(2,1)}), bf16[32,12,2048]{2,1,0:T(8,128)(2,1)S(1)}, u32[]{:S(2)}, u32[]{:S(2)}) async-start(bf16[32,12,2048]{2,1,0:T(8,128)(2,1)} %reshape.70), calls=%async_computation.2 | async-start | bytes 4194304 | tf_op jit(solution)/shard_map/all_to_all | solution.py:67
  186.2 98.4 %reduce-scatter.2.cloned.1.call-start = ((), (), s32[]{:S(2)}) async-start(), calls=%async_computation.6 | async-start | bytes 3342336 | tf_op jit(solution)/shard_map/reduce_scatter | solution.py:56
Sparse Core Ops, SparseCore 0:
  10.2 52.1 all-gather.5
  64.5 62.1 all-gather.3
  191.4 77.9 reduce-scatter.1
where the time goes:
time: 295 us; the launch traced here: 291 us
  waiting for transfers between devices  200 us (68%)
  starting transfers between devices  31.2 us (11%)
  matrix products  16.9 us (6%)
  blocking collectives  16.5 us (6%)
  between operations  13.9 us (5%)
  local copies, waits for them, and re-layouts  7.51 us (3%)
  other arithmetic  5.36 us (2%)
    all_to_all x1, waiting for transfers between devices, per_device(): lax.all_to_all(send_rows, 'expert', split_axis=0, concat_axis=0, tiled=True)  95.1 us
    all_to_all x1, waiting for transfers between devices, per_device(): lax.all_to_all(back_rows, 'expert', split_axis=0, concat_axis=0, tiled=True)  90.7 us
    all_to_all x1, starting transfers between devices, per_device(): lax.all_to_all(send_rows, 'expert', split_axis=0, concat_axis=0, tiled=True)  18.6 us
    all_to_all x1, blocking collectives, per_device(): lax.all_to_all(send_weight, 'expert', split_axis=0, concat_axis=0, tiled=...  16.5 us
    all_to_all x1, waiting for transfers between devices, per_device(): lax.all_to_all(back_route, 'expert', split_axis=0, concat_axis=0, tiled=T...  13.3 us
    all_to_all x1, starting transfers between devices, per_device(): lax.all_to_all(back_route, 'expert', split_axis=0, concat_axis=0, tiled=T...  8.33 us
  transfers between devices with their start and end apart: 6, of which 3 were waited for; matrix products, arithmetic and copies ran while one was open for 8% of the time, Pallas kernels for 0%

commit v1 on v0

v1 whole, which is shorter than its diff:
```python
import functools

import jax
import jax.numpy as jnp
from jax import lax
from jax.experimental import pallas as pl
from jax.experimental.pallas import tpu as pltpu
from jax.sharding import PartitionSpec as P

BF16, F32 = jnp.bfloat16, jnp.float32
META = 128
STRIDE = 4
VMEM = 48 * 1024 * 1024


def params():
    return pltpu.CompilerParams(vmem_limit_bytes=VMEM)


def prep_kernel(rows_ref, ids_ref, weight_ref, gate_ref, up_ref, down_ref, tok_ref, pack_ref):
    tok, width = rows_ref.shape
    topk = ids_ref.shape[1]
    packed = down_ref.shape[0]
    hidden = gate_ref.shape[1]
    part = 2 * hidden * META // width
    tok_ref[:, :width] = rows_ref[...]
    meta = jnp.concatenate(
        [ids_ref[...].astype(F32), weight_ref[...].astype(F32), jnp.zeros((tok, META - 2 * topk), F32)], axis=1
    )
    tok_ref[:, width:] = meta.astype(BF16)
    for at, ref in enumerate((gate_ref, up_ref)):
        turned = ref[...].astype(F32).T.astype(BF16)
        for g in range(hidden // part):
            lane = (at * (hidden // part) + g) * META
            pack_ref[0:part, lane : lane + META] = turned[g * part : (g + 1) * part]
    pack_ref[part : part + packed, :] = down_ref[...]


def select_kernel(cap, mine_ref, tok_ref, send_ref, select_ref):
    rows, full = tok_ref.shape
    width = full - META
    dests, per, _ = send_ref.shape
    block = rows // STRIDE
    topk = 8
    ids = tok_ref[:, width:].astype(F32).T[0:topk, :]
    member = jnp.concatenate(
        [
            jnp.max((ids == mine_ref[j].astype(F32)).astype(F32), axis=0, keepdims=True)
            for j in range(dests)
        ],
        axis=0,
    )
    before = lax.broadcasted_iota(jnp.int32, (rows, rows), 0)
    after = lax.broadcasted_iota(jnp.int32, (rows, rows), 1)
    earlier = (before < after) & (before // block == after // block)
    rank = jnp.dot(member.astype(BF16), earlier.astype(BF16), preferred_element_type=F32)
    key = jnp.where(member > 0.0, rank, -1.0)
    place = lax.broadcasted_iota(jnp.int32, (per, rows), 0)
    source = lax.broadcasted_iota(jnp.int32, (per, rows), 1) // block
    pattern = jnp.where(place // cap == source, place - source * cap, -2).astype(F32)
    for j in range(dests):
        chosen = (key[j : j + 1, :] == pattern).astype(BF16)
        select_ref[j * per : (j + 1) * per, :] = chosen
    for j in range(dests):
        send_ref[j] = jnp.dot(
            select_ref[j * per : (j + 1) * per, :], tok_ref[...], preferred_element_type=F32
        ).astype(BF16)


def act_kernel(cap, pre_ref, hid_ref, turned_ref, slope_ref, silu_ref):
    slots, both = pre_ref.shape
    hidden = both // 2
    dests = slots // (cap * STRIDE)
    at = lax.broadcasted_iota(jnp.int32, (slots, slots), 0)
    src = lax.broadcasted_iota(jnp.int32, (slots, slots), 1)
    j, rest = at // (STRIDE * cap), at % (STRIDE * cap)
    k, r = rest // cap, rest % cap
    order = (src == (k * dests + j) * cap + r).astype(BF16)
    a = jnp.dot(order, pre_ref[:, :hidden], preferred_element_type=F32)
    u = jnp.dot(order, pre_ref[:, hidden:], preferred_element_type=F32)
    sig = jax.nn.sigmoid(a)
    silu = a * sig
    hid = (silu * u).astype(BF16)
    hid_ref[...] = hid
    turned_ref[...] = hid.astype(F32).T.astype(BF16)
    slope_ref[...] = u * sig * (1.0 + a * (1.0 - sig))
    silu_ref[...] = silu


def slot_weight(meta, expert):
    topk = 8
    meta = meta.astype(F32)
    lane = lax.broadcasted_iota(jnp.int32, meta.shape, 1)
    weight = pltpu.roll(meta, META - topk, 1)
    return jnp.sum(jnp.where((lane < topk) & (meta == expert.astype(F32)), weight, 0.0), axis=1, keepdims=True)


def down_kernel(mine_ref, got_ref, meta_ref, turned_ref, out_ref):
    w = slot_weight(meta_ref[...], mine_ref[0])
    scaled = (w * got_ref[...].astype(F32)).astype(BF16)
    out_ref[...] = jnp.dot(turned_ref[...], scaled, preferred_element_type=F32).astype(BF16)


def mid_kernel(mine_ref, got_ref, hid_ref, slope_ref, silu_ref, down_ref, pack_ref, out_ref, both_ref, wide_ref):
    step = pl.program_id(0)
    width = got_ref.shape[1] - META
    hidden = hid_ref.shape[1]
    pair, part, _ = pack_ref.shape

    @pl.when(step == 0)
    def _():
        w = slot_weight(got_ref[:, width:], mine_ref[0])
        q = lax.dot_general(
            got_ref[:, :width],
            down_ref[...].reshape(hidden, width),
            (((1,), (1,)), ((), ())),
            preferred_element_type=F32,
        )
        route = jnp.sum(q * hid_ref[...].astype(F32), axis=1, keepdims=True)
        grad = w * q
        both_ref[:, :hidden] = (grad * slope_ref[...]).astype(BF16)
        both_ref[:, hidden:] = (grad * silu_ref[...]).astype(BF16)
        lane = lax.broadcasted_iota(jnp.int32, (got_ref.shape[0], META), 1)
        out_ref[:, width:] = jnp.where(lane == mine_ref[0], route, 0.0).astype(BF16)

    @pl.when(step > 0)
    def _():
        for b in range(pair):
            for g in range(2 * hidden // part):
                wide_ref[g * part : (g + 1) * part, b * META : (b + 1) * META] = pack_ref[
                    b, :, g * META : (g + 1) * META
                ]
        at = pl.multiple_of((step - 1) * (pair * META), pair * META)
        out_ref[:, pl.ds(at, pair * META)] = jnp.dot(
            both_ref[...], wide_ref[...], preferred_element_type=F32
        ).astype(BF16)


def combine_kernel(select_ref, back_ref, out_ref):
    total = lax.dot_general(
        select_ref[...], back_ref[...], (((0,), (0,)), ((), ())), preferred_element_type=F32
    )
    out_ref[...] = total.astype(BF16)


def last_kernel(part_ref, ids_ref, tok_ref, route_ref):
    width = tok_ref.shape[1]
    total = part_ref[0].astype(F32)
    for k in range(1, STRIDE):
        total = total + part_ref[k].astype(F32)
    tok_ref[...] = total[:, :width].astype(BF16)
    route = total[:, width:]
    ids = ids_ref[...]
    lane = lax.broadcasted_iota(jnp.int32, route.shape, 1)
    found = [
        jnp.sum(jnp.where(lane == ids[:, k : k + 1], route, 0.0), axis=1, keepdims=True)
        for k in range(ids.shape[1])
    ]
    route_ref[...] = jnp.concatenate(found, axis=1).astype(BF16)


def shape(dims, dtype=BF16):
    return jax.ShapeDtypeStruct(dims, dtype)


def whole(memory=pltpu.VMEM):
    return pl.BlockSpec(memory_space=memory)


def per_device(n_dp, n_expert, grad_out, expert_ids, route_weights, saved_pre, gate_weight, up_weight, down_weight):
    tok, width = grad_out.shape
    pre = saved_pre[0, 0]
    slots, both = pre.shape
    hidden = both // 2
    cap = slots // n_expert
    full = width + META
    n_z = n_expert // 2
    dests = slots // (cap * STRIDE)
    per = STRIDE * cap
    down_rows = down_weight.shape[1]
    part = both * META // width
    axes = ("dp", "expert")

    apart = [
        [d * n_expert + (rho + STRIDE * k) * 2 + h for k in range(n_z // STRIDE)]
        for d in range(n_dp)
        for rho in range(STRIDE)
        for h in range(2)
    ]
    near = [
        [
            d * n_expert + ((STRIDE * a + (rho - 2 * (d % 2)) % STRIDE + 2 * (d % 2)) % n_z) * 2 + h
            for rho in range(STRIDE)
            for h in range(2)
        ]
        for d in range(n_dp)
        for a in range(n_z // STRIDE)
    ]
    core, me = lax.axis_index("dp") % 2, lax.axis_index("expert")
    shift = 2 * core
    quad = ((me // 2 - shift + n_z) % n_z) // STRIDE
    rho = jnp.arange(dests, dtype=jnp.int32) // 2
    members = ((STRIDE * quad + (rho - shift + STRIDE) % STRIDE + shift) % n_z) * 2 + jnp.arange(
        dests, dtype=jnp.int32
    ) % 2
    mine = me.reshape(1).astype(jnp.int32)

    rows, pack = pl.pallas_call(
        prep_kernel,
        out_shape=(shape((tok, full)), shape((part + down_rows, width))),
        in_specs=[whole()] * 6,
        out_specs=(whole(), whole()),
        compiler_params=params(),
        name="prep",
    )(grad_out, expert_ids, route_weights, gate_weight[0], up_weight[0], down_weight[0])
    packs = lax.all_gather(pack, "dp", axis=0, tiled=False)
    blocks = lax.all_gather(rows, axes, axis=0, tiled=True, axis_index_groups=apart)
    send, select = pl.pallas_call(
        functools.partial(select_kernel, cap),
        out_shape=(shape((dests, per, full)), shape((slots, STRIDE * tok))),
        in_specs=[whole(pltpu.SMEM), whole()],
        out_specs=(whole(), whole()),
        compiler_params=params(),
        name="select",
    )(members, blocks)
    got = lax.all_to_all(send, axes, 0, 0, axis_index_groups=near, tiled=True).reshape(slots, full)
    hid, turned, slope, silu = pl.pallas_call(
        functools.partial(act_kernel, cap),
        out_shape=(
            shape((slots, hidden)),
            shape((hidden, slots)),
            shape((slots, hidden), F32),
            shape((slots, hidden), F32),
        ),
        in_specs=[whole()],
        out_specs=(whole(),) * 4,
        compiler_params=params(),
        cost_estimate=pl.CostEstimate(flops=slots * slots * both * 2, bytes_accessed=8 * slots * both, transcendentals=0),
        name="act",
    )(pre)
    columns = 512
    down_part = pl.pallas_call(
        down_kernel,
        out_shape=shape((hidden, width)),
        grid=(width // columns,),
        in_specs=[
            whole(pltpu.SMEM),
            pl.BlockSpec((slots, columns), lambda i: (0, i)),
            pl.BlockSpec((slots, META), lambda i: (0, width // META)),
            pl.BlockSpec((hidden, slots), lambda i: (0, 0)),
        ],
        out_specs=pl.BlockSpec((hidden, columns), lambda i: (0, i)),
        compiler_params=params(),
        cost_estimate=pl.CostEstimate(flops=2 * slots * hidden * width, bytes_accessed=2 * (slots + hidden) * width, transcendentals=0),
        name="down",
    )(mine, got, got, turned)
    down_grad = lax.psum_scatter(down_part, "dp", scatter_dimension=0, tiled=True)
    pair = 2
    back = pl.pallas_call(
        mid_kernel,
        out_shape=shape((slots, full)),
        grid=(1 + n_dp // pair,),
        in_specs=[
            whole(pltpu.SMEM),
            pl.BlockSpec((slots, full), lambda i: (0, 0)),
            pl.BlockSpec((slots, hidden), lambda i: (0, 0)),
            pl.BlockSpec((slots, hidden), lambda i: (0, 0)),
            pl.BlockSpec((slots, hidden), lambda i: (0, 0)),
            pl.BlockSpec((n_dp, down_rows, width), lambda i: (0, part // down_rows, 0)),
            pl.BlockSpec((pair, part, width), lambda i: (jnp.maximum(i - 1, 0), 0, 0)),
        ],
        out_specs=pl.BlockSpec((slots, full), lambda i: (0, 0)),
        scratch_shapes=[pltpu.VMEM((slots, both), BF16), pltpu.VMEM((both, pair * META), BF16)],
        compiler_params=params(),
        cost_estimate=pl.CostEstimate(flops=6 * slots * hidden * width, bytes_accessed=2 * 3 * hidden * width, transcendentals=0),
        name="mid",
    )(mine, got, hid, slope, silu, packs, packs)
    back = lax.all_to_all(
        back.reshape(dests, per, full), axes, 0, 0, axis_index_groups=near, tiled=True
    ).reshape(slots, full)
    partial = pl.pallas_call(
        combine_kernel,
        out_shape=shape((STRIDE * tok, full)),
        in_specs=[whole(), whole()],
        out_specs=whole(),
        compiler_params=params(),
        name="combine",
    )(select, back)
    parts = lax.all_to_all(
        partial.reshape(STRIDE, tok, full), axes, 0, 0, axis_index_groups=apart, tiled=True
    )
    token_grad, route_grad = pl.pallas_call(
        last_kernel,
        out_shape=(shape((tok, width)), shape(expert_ids.shape)),
        in_specs=[whole(), whole()],
        out_specs=(whole(), whole()),
        compiler_params=params(),
        name="last",
    )(parts, expert_ids)
    return token_grad, route_grad, down_grad[None]


def solution(mesh):
    return jax.shard_map(
        functools.partial(per_device, mesh.shape["dp"], mesh.shape["expert"]),
        mesh=mesh,
        in_specs=(
            P(("dp", "expert"), None),
            P(("dp", "expert"), None),
            P(("dp", "expert"), None),
            P("dp", "expert", None, None),
            P("expert", "dp", None),
            P("expert", "dp", None),
            P("expert", "dp", None),
        ),
        out_specs=(P(("dp", "expert"), None), P(("dp", "expert"), None), P("expert", "dp", None)),
        check_vma=False,
    )
```

time: 295 us -> 210 us (0.71)
  waiting for transfers between devices: 200 us -> 76.2 us
  blocking collectives: 16.5 us -> 67.8 us
  Pallas kernels: 0 us -> 21.2 us
  starting transfers between devices: 31.2 us -> 13.3 us
  matrix products: 16.9 us -> 0 us
  local copies, waits for them, and re-layouts: 7.51 us -> 14.2 us
  other arithmetic: 5.36 us -> 0.02 us
    all_to_all x3 -> x2, waiting for transfers between devices: 199 us -> 53.9 us  [the longest x1 27.2 us: per_device(): lax.all_to_all(send, axes, 0, 0, axis_index_groups=near, tiled=True)]
    all_gather x0 -> x1, blocking collectives: none -> 32.4 us  [per_device(): lax.all_gather(rows, axes, axis=0, tiled=True, axis_index_groups=apart)]
    pallas_call x0 -> x7, Pallas kernels: none -> 21.2 us  [the longest x1 11.2 us: per_device(): pl.pallas_call(mid_kernel, out_shape=shape((slots, full)), grid=(1 + n_dp...]
    all_to_all x1, blocking collectives: 16.5 us -> 35.3 us  [per_device(): lax.all_to_all(partial.reshape(STRIDE, tok, full), axes, 0, 0, axis_index...]
    all_to_all x3 -> x2, starting transfers between devices: 31.1 us -> 13.3 us  [the longest x1 8.1 us: per_device(): lax.all_to_all(back.reshape(dests, per, full), axes, 0, 0, axis_index_gro...]
    dot_general x5 -> x0, matrix products: 16.9 us -> none  [the longest x1 5.62 us: per_device(): lax.dot_general(grad_both, lax.all_gather(gate_up, 'dp', axis=0, tiled=Tr...]
    all_gather x2 -> x1, waiting for transfers between devices: 0.01 us -> 16.3 us  [per_device(): packs = lax.all_gather(pack, 'dp', axis=0, tiled=False)]
    unnamed x10 -> x29, local copies, waits for them, and re-layouts: 1.45 us -> 14.2 us
  transfers between devices with their start and end apart: 6 -> 4, of which waited for: 3 -> 4; matrix products, arithmetic and copies ran while one was open for 8% -> 0% of each run, Pallas kernels for 0% -> 4%
where the time goes in v1:
time: 210 us; the launch traced here: 207 us
  waiting for transfers between devices  76.2 us (36%)
  blocking collectives  67.8 us (32%)
  Pallas kernels  21.2 us (10%)
  local copies, waits for them, and re-layouts  14.2 us (7%)
  between operations  14.2 us (7%)
  starting transfers between devices  13.3 us (6%)
    all_to_all x1, blocking collectives, per_device(): lax.all_to_all(partial.reshape(STRIDE, tok, full), axes, 0, 0, axis_index...  35.3 us
    all_gather x1, blocking collectives, per_device(): lax.all_gather(rows, axes, axis=0, tiled=True, axis_index_groups=apart)  32.4 us
    all_to_all x1, waiting for transfers between devices, per_device(): lax.all_to_all(send, axes, 0, 0, axis_index_groups=near, tiled=True)  27.2 us
    all_to_all x1, waiting for transfers between devices, per_device(): lax.all_to_all(back.reshape(dests, per, full), axes, 0, 0, axis_index_gro...  26.7 us
    all_gather x1, waiting for transfers between devices, per_device(): packs = lax.all_gather(pack, 'dp', axis=0, tiled=False)  16.3 us
    unnamed x29, local copies, waits for them, and re-layouts  14.2 us
    pallas_call x1, Pallas kernels, per_device(): pl.pallas_call(mid_kernel, out_shape=shape((slots, full)), grid=(1 + n_dp...  11.2 us
    all_to_all x1, starting transfers between devices, per_device(): lax.all_to_all(back.reshape(dests, per, full), axes, 0, 0, axis_index_gro...  8.1 us
  transfers between devices with their start and end apart: 4, of which 4 were waited for; matrix products, arithmetic and copies ran while one was open for 0% of the time, Pallas kernels for 4%

profile of v1, /device:TPU:1, one launch (start us, length us, event | category | flops | bytes accessed | tf_op | source)
XLA Modules:
  0.0 206.9 jit_solution(16831691955939115459)
XLA Ops:
  7.2 0.0 all-gather.3.cloned.1.call-start
  7.2 0.8 copy.10.ids_ref
  8.0 0.8 copy.11.weight_ref
  8.7 0.9 copy-done.8
  9.7 0.9 copy-done.9
  10.6 0.9 copy-done.10
  11.5 0.9 copy-done.11
  12.4 1.0 prep.1
  13.5 0.0 all-gather.3.cloned.1.call-update
  13.6 32.4 %all_gather.9.tok_ref = bf16[128,2176]{1,0:T(8,128)(2,1)S(1)} all-gather(bf16[32,2176]{1,0:T(8,128)(2,1)S(1)} %get-tuple-element.13), channel_id=1, replica_groups={{0,8,16,24},{1,9,17,25},{2,10,18,26},{3,11,19,27},{4,12,20,28},{5,13,21..., dimensions={0}, use_global_device_ids=true | all-gather | bytes 696320 | tf_op jit(solution)/shard_map/all_gather | solution.py:217
  46.0 2.7 %select.23 = (bf16[8,48,2176]{2,1,0:T(8,128)(2,1)}, bf16[384,128]{1,0:T(8,128)(2,1)S(1)}) custom-call(s32[8]{0:T(128)S(1)} %fusion.mine_ref, bf16[128,2176]{1,0:T(8,128)(2,1)S(1)} %all_gather.9.tok_ref), custom_call_target="tpu_custom_call" | custom-call | tf_op jit(solution)/shard_map/select/pallas_call | solution.py:218
  48.7 5.2 %all-to-all-start = ((bf16[8,48,2176]{2,1,0:T(8,128)(2,1)}), bf16[8,48,2176]{2,1,0:T(8,128)(2,1)S(1)}, u32[]{:S(2)}, u32[]{:S(2)}) async-start(bf16[8,48,2176]{2,1,0:T(8,128)(2,1)} %get-tuple-element.15), calls=%async_computation | async-start | bytes 3342336 | tf_op jit(solution)/shard_map/all_to_all | solution.py:226
  53.8 1.3 copy-done.12
  55.2 1.2 act.1
  56.4 1.0 copy-done.4
  57.5 0.8 copy-done.6
  58.3 27.2 %all-to-all-done = bf16[8,48,2176]{2,1,0:T(8,128)(2,1)S(1)} async-done(((bf16[8,48,2176]{2,1,0:T(8,128)(2,1)}), bf16[8,48,2176]{2,1,0:T(8,128)(2,1)S(1)}, u32[]{:S(2)}, u32[]{:S(2)}) %all-to-all-start) | async-done | bytes 1671200 | tf_op jit(solution)/shard_map/all_to_all | solution.py:226
  85.5 16.3 %all-gather.3.cloned.1.call-done = bf16[2304,2048]{1,0:T(8,128)(2,1)} async-done(((bf16[144,2048]{1,0:T(8,128)(2,1)}), bf16[2304,2048]{1,0:T(8,128)(2,1)}) %all-gather.3.cloned.1.call-update) | async-done | bytes 9437200 | tf_op jit(solution)/shard_map/all_gather | solution.py:216
  101.9 1.3 copy-done.5
  103.1 11.2 %mid.1 = bf16[384,2176]{1,0:T(8,128)(2,1)S(1)} custom-call(s32[1]{0:T(128)} %bitcast.3.mine_ref, bf16[384,2176]{1,0:T(8,128)(2,1)} %bitcast.11, bf16[384,768]{1,0:T(8,128)(2,1)S(1)} %get-tuple-element.16.hid_ref, f32[384,768]{1,0:T(8,128)S(1)} %get-tuple-element.17.slope_ref, f32[384,768]{1,0:T(8,128)S(1)} %copy-done.5, bf16[16,144,2048]{2,1,0:T(8,128)(2,1)} %bitcast.21, ...), custom_call_target="tpu_custom_call" | custom-call | flops 3623878656 | bytes 9437184 | tf_op jit(solution)/shard_map/mid/pallas_call | solution.py:259
  114.4 1.2 copy-done.3
  115.6 8.1 %all-to-all-start.1 = ((bf16[8,48,2176]{2,1,0:T(8,128)(2,1)}), bf16[8,48,2176]{2,1,0:T(8,128)(2,1)S(1)}, u32[]{:S(2)}, u32[]{:S(2)}) async-start(bf16[8,48,2176]{2,1,0:T(8,128)(2,1)} %bitcast.15), calls=%async_computation.1 | async-start | bytes 3342336 | tf_op jit(solution)/shard_map/all_to_all | solution.py:278
  123.7 0.0 reduce-scatter.2.cloned.1.call-start
  123.7 1.1 copy-done.7
  124.8 3.4 %down.1 = bf16[768,2048]{1,0:T(8,128)(2,1)S(1)} custom-call(s32[1]{0:T(128)} %bitcast.3.mine_ref, bf16[384,2176]{1,0:T(8,128)(2,1)S(1)} %bitcast.12, bf16[384,2176]{1,0:T(8,128)(2,1)S(1)} %bitcast.13, bf16[768,384]{1,0:T(8,128)(2,1)S(1)} %copy-done.7), custom_call_target="tpu_custom_call" | custom-call | flops 1207959552 | bytes 4718592 | tf_op jit(solution)/shard_map/down/pallas_call | solution.py:242
  128.2 1.6 copy-done.2
  129.9 26.7 %all-to-all-done.1 = bf16[8,48,2176]{2,1,0:T(8,128)(2,1)S(1)} async-done(((bf16[8,48,2176]{2,1,0:T(8,128)(2,1)}), bf16[8,48,2176]{2,1,0:T(8,128)(2,1)S(1)}, u32[]{:S(2)}, u32[]{:S(2)}) %all-to-all-start.1) | async-done | bytes 1671200 | tf_op jit(solution)/shard_map/all_to_all | solution.py:278
  156.6 0.5 combine.1
  157.1 35.3 %all_to_all.15.part_ref = bf16[4,32,2176]{2,1,0:T(8,128)(2,1)S(1)} all-to-all(bf16[4,32,2176]{2,1,0:T(8,128)(2,1)S(1)} %bitcast.16), channel_id=1, replica_groups={{0,8,16,24},{1,9,17,25},{2,10,18,26},{3,11,19,27},{4,12,20,28},{5,13,21..., dimensions={0} | all-to-all | bytes 1114112 | tf_op jit(solution)/shard_map/all_to_all | solution.py:289
  192.4 1.2 last.1
  193.6 0.7 copy.13
  194.2 5.8 %reduce-scatter.2.cloned.1.call-done = bf16[48,2048]{1,0:T(8,128)(2,1)} async-done(((bf16[768,2048]{1,0:T(8,128)(2,1)}), bf16[48,2048]{1,0:T(8,128)(2,1)}) %reduce-scatter.2.cloned.1.call-update) | async-done | bytes 196624 | tf_op jit(solution)/shard_map/reduce_scatter | solution.py:257
  (17 shorter events, 0.1 us)
Async XLA Ops:
  7.2 94.7 %all-gather.3.cloned.1.call-start = ((), (), s32[]{:S(2)}) async-start(), calls=%async_computation.5 | async-start | bytes 10027008 | tf_op jit(solution)/shard_map/all_gather | solution.py:216
  8.7 0.9 copy-start.8
  9.7 0.9 copy-start.9
  10.6 0.9 copy-start.10
  11.5 0.9 copy-start.11
  48.7 36.8 %all-to-all-start = ((bf16[8,48,2176]{2,1,0:T(8,128)(2,1)}), bf16[8,48,2176]{2,1,0:T(8,128)(2,1)S(1)}, u32[]{:S(2)}, u32[]{:S(2)}) async-start(bf16[8,48,2176]{2,1,0:T(8,128)(2,1)} %get-tuple-element.15), calls=%async_computation | async-start | bytes 3342336 | tf_op jit(solution)/shard_map/all_to_all | solution.py:226
  53.8 1.3 copy-start.12
  56.4 1.0 copy-start.4
  57.5 0.8 copy-start.6
  85.5 16.4 %copy-start = (bf16[8,48,2176]{2,1,0:T(8,128)(2,1)}, bf16[8,48,2176]{2,1,0:T(8,128)(2,1)S(1)}, u32[]{:S(2)}) copy-start(bf16[8,48,2176]{2,1,0:T(8,128)(2,1)S(1)} %all-to-all-done) | copy-start | bytes 5013508
  101.9 1.3 copy-start.5
  114.3 1.2 copy-start.3
  115.6 8.2 %copy-start.1 = (bf16[8,48,2176]{2,1,0:T(8,128)(2,1)S(1)}, bf16[8,48,2176]{2,1,0:T(8,128)(2,1)}, u32[]{:S(2)}) copy-start(bf16[8,48,2176]{2,1,0:T(8,128)(2,1)} %copy-done) | copy-start | bytes 5013508
  115.6 41.0 %all-to-all-start.1 = ((bf16[8,48,2176]{2,1,0:T(8,128)(2,1)}), bf16[8,48,2176]{2,1,0:T(8,128)(2,1)S(1)}, u32[]{:S(2)}, u32[]{:S(2)}) async-start(bf16[8,48,2176]{2,1,0:T(8,128)(2,1)} %bitcast.15), calls=%async_computation.1 | async-start | bytes 3342336 | tf_op jit(solution)/shard_map/all_to_all | solution.py:278
  123.7 76.4 %reduce-scatter.2.cloned.1.call-start = ((), (), s32[]{:S(2)}) async-start(), calls=%async_computation.4 | async-start | bytes 3342336 | tf_op jit(solution)/shard_map/reduce_scatter | solution.py:257
  123.7 1.1 copy-start.7
  128.2 1.6 copy-start.2
Sparse Core Ops, SparseCore 0:
  13.6 88.2 all-gather.2
  130.0 70.0 reduce-scatter.1

commit v2 on v1

v2 whole, which is shorter than its diff:
```python
import functools

import jax
import jax.numpy as jnp
from jax import lax
from jax.experimental import pallas as pl
from jax.experimental.pallas import tpu as pltpu
from jax.sharding import PartitionSpec as P

BF16, F32 = jnp.bfloat16, jnp.float32
META = 128
STRIDE = 4


def params(mib):
    return pltpu.CompilerParams(vmem_limit_bytes=mib * 1024 * 1024)


def turn(values):
    rows, columns = values.shape
    if columns < META:
        values = jnp.concatenate([values, jnp.zeros((rows, META - columns), F32)], axis=1)
    if rows < META:
        values = jnp.concatenate([values, jnp.zeros((META - rows, META), F32)], axis=0)
    return values.T[:columns, :rows] if columns < META else values.T[:, :rows]


def prep_kernel(
    rows_ref, ids_ref, weight_ref, gate_ref, up_ref, down_ref, tok_ref, pack_ref,
    ids_buf, weight_buf, gate_buf, up_buf, sems,
):
    tok, width = rows_ref.shape
    topk = ids_ref.shape[0]
    hidden = gate_ref.shape[1]
    part = 2 * hidden * META // width
    copies = [
        pltpu.make_async_copy(gate_ref, gate_buf, sems.at[0]),
        pltpu.make_async_copy(up_ref, up_buf, sems.at[1]),
        pltpu.make_async_copy(down_ref, pack_ref.at[pl.ds(part, down_ref.shape[0]), :], sems.at[2]),
        pltpu.make_async_copy(ids_ref, ids_buf, sems.at[3]),
        pltpu.make_async_copy(weight_ref, weight_buf, sems.at[4]),
        pltpu.make_async_copy(rows_ref, tok_ref.at[:, pl.ds(0, width)], sems.at[5]),
    ]
    for copy in copies:
        copy.start()
    for at, buf in enumerate((gate_buf, up_buf)):
        copies[at].wait()
        turned = buf[...].astype(F32).T.astype(BF16)
        for g in range(hidden // part):
            lane = (at * (hidden // part) + g) * META
            pack_ref[0:part, lane : lane + META] = turned[g * part : (g + 1) * part]
    copies[3].wait()
    copies[4].wait()
    meta = jnp.concatenate([ids_buf[...].astype(F32), weight_buf[...].astype(F32)], axis=0)
    meta = jnp.concatenate([meta, jnp.zeros((META - 2 * topk, tok), F32)], axis=0)
    tok_ref[:, width:] = turn(meta).astype(BF16)
    copies[2].wait()
    copies[5].wait()


def select_kernel(cap, mine_ref, tok_ref, send_ref, select_ref):
    rows, full = tok_ref.shape
    width = full - META
    dests, per, _ = send_ref.shape
    block = rows // STRIDE
    topk = 8
    ids = tok_ref[:, width:].astype(F32).T[0:topk, :]
    member = jnp.concatenate(
        [
            jnp.max((ids == mine_ref[j].astype(F32)).astype(F32), axis=0, keepdims=True)
            for j in range(dests)
        ],
        axis=0,
    )
    before = lax.broadcasted_iota(jnp.int32, (rows, rows), 0)
    after = lax.broadcasted_iota(jnp.int32, (rows, rows), 1)
    earlier = (before < after) & (before // block == after // block)
    rank = jnp.dot(member.astype(BF16), earlier.astype(BF16), preferred_element_type=F32)
    key = jnp.where(member > 0.0, rank, -1.0)
    place = lax.broadcasted_iota(jnp.int32, (per, rows), 0)
    source = lax.broadcasted_iota(jnp.int32, (per, rows), 1) // block
    pattern = jnp.where(place // cap == source, place - source * cap, -2).astype(F32)
    for j in range(dests):
        chosen = (key[j : j + 1, :] == pattern).astype(BF16)
        select_ref[j * per : (j + 1) * per, :] = chosen
    for j in range(dests):
        send_ref[j] = jnp.dot(
            select_ref[j * per : (j + 1) * per, :], tok_ref[...], preferred_element_type=F32
        ).astype(BF16)


def act_kernel(cap, rows, pre_ref, hid_ref, turned_ref, slope_ref, silu_ref):
    slots, both = pre_ref.shape
    hidden = both // 2
    dests = slots // (cap * STRIDE)
    at = lax.broadcasted_iota(jnp.int32, (slots, slots), 0)
    src = lax.broadcasted_iota(jnp.int32, (slots, slots), 1)
    j, rest = at // (STRIDE * cap), at % (STRIDE * cap)
    k, r = rest // cap, rest % cap
    order = (src == (k * dests + j) * cap + r).astype(BF16)
    a = jnp.dot(order, pre_ref[:, :hidden], preferred_element_type=F32)
    u = jnp.dot(order, pre_ref[:, hidden:], preferred_element_type=F32)
    sig = jax.nn.sigmoid(a)
    silu = a * sig
    hid = (silu * u).astype(BF16)
    hid_ref[...] = hid
    turned = hid.astype(F32).T.astype(BF16)
    for block in range(hidden // rows):
        at = (block % 2) * (hidden // 2) + (block // 2) * rows
        turned_ref[at : at + rows, :] = turned[block * rows : (block + 1) * rows]
    slope_ref[...] = u * sig * (1.0 + a * (1.0 - sig))
    silu_ref[...] = silu


def slot_weight(meta, expert):
    topk = 8
    meta = meta.astype(F32)
    lane = lax.broadcasted_iota(jnp.int32, meta.shape, 1)
    weight = pltpu.roll(meta, META - topk, 1)
    return jnp.sum(jnp.where((lane < topk) & (meta == expert.astype(F32)), weight, 0.0), axis=1, keepdims=True)


def down_kernel(mine_ref, got_ref, turned_ref, keep_ref, send_ref):
    half, width = keep_ref.shape
    core = mine_ref[1]
    w = slot_weight(got_ref[:, width:], mine_ref[0])
    columns = 512
    for at in range(0, width, columns):
        scaled = (w * got_ref[:, at : at + columns].astype(F32)).astype(BF16)
        for ref, which in ((send_ref, 1 - core), (keep_ref, core)):
            begin = pl.multiple_of(which * half, half)
            ref[:, at : at + columns] = jnp.dot(
                turned_ref[pl.ds(begin, half), :], scaled, preferred_element_type=F32
            ).astype(BF16)


def mid_kernel(
    mine_ref, got_ref, hid_ref, slope_ref, silu_ref, pack_ref, out_ref,
    out_buf, both_buf, down_buf, pack_buf, wide_buf, in_sems, out_sems,
):
    width = got_ref.shape[1] - META
    hidden = hid_ref.shape[1]
    pairs, pair, part, _ = pack_buf.shape
    down_rows = down_buf.shape[1]
    down_copy = pltpu.make_async_copy(
        pack_ref.at[:, pl.ds(part, down_rows), :], down_buf, in_sems.at[pairs]
    )
    down_copy.start()
    copies = [
        pltpu.make_async_copy(
            pack_ref.at[pl.ds(p * pair, pair), pl.ds(0, part), :], pack_buf.at[p], in_sems.at[p]
        )
        for p in range(pairs)
    ]
    for copy in copies:
        copy.start()
    w = slot_weight(got_ref[:, width:], mine_ref[0])
    down_copy.wait()
    q = lax.dot_general(
        got_ref[:, :width],
        down_buf[...].reshape(hidden, width),
        (((1,), (1,)), ((), ())),
        preferred_element_type=F32,
    )
    route = jnp.sum(q * hid_ref[...].astype(F32), axis=1, keepdims=True)
    grad = w * q
    both_buf[:, :hidden] = (grad * slope_ref[...]).astype(BF16)
    both_buf[:, hidden:] = (grad * silu_ref[...]).astype(BF16)
    lane = lax.broadcasted_iota(jnp.int32, (got_ref.shape[0], META), 1)
    out_buf[:, width:] = jnp.where(lane == mine_ref[0], route, 0.0).astype(BF16)
    backs = [pltpu.make_async_copy(out_buf.at[:, pl.ds(width, META)], out_ref.at[:, pl.ds(width, META)], out_sems.at[pairs])]
    backs[0].start()
    for p in range(pairs):
        copies[p].wait()
        for b in range(pair):
            for g in range(2 * hidden // part):
                wide_buf[p % 2, g * part : (g + 1) * part, b * META : (b + 1) * META] = pack_buf[
                    p, b, :, g * META : (g + 1) * META
                ]
        at = p * pair * META
        out_buf[:, at : at + pair * META] = jnp.dot(
            both_buf[...], wide_buf[p % 2], preferred_element_type=F32
        ).astype(BF16)
        columns = pl.ds(at, pair * META)
        backs.append(pltpu.make_async_copy(out_buf.at[:, columns], out_ref.at[:, columns], out_sems.at[p]))
        backs[-1].start()
    for copy in backs:
        copy.wait()


def combine_kernel(place_ref, select_ref, back_ref, *refs):
    outs, total_buf = refs[:-1], refs[-1]
    tok = outs[0].shape[0]
    total_buf[...] = lax.dot_general(
        select_ref[...], back_ref[...], (((0,), (0,)), ((), ())), preferred_element_type=F32
    )
    for m, ref in enumerate(outs):
        begin = pl.multiple_of(((place_ref[0] + m) % STRIDE) * tok, tok)
        ref[...] = total_buf[pl.ds(begin, tok), :].astype(ref.dtype)


def last_kernel(ids_ref, *refs):
    parts, (tok_ref, route_ref) = refs[:STRIDE], refs[STRIDE:]
    tok, width = tok_ref.shape
    total = parts[0][...]
    for ref in parts[1:]:
        total = total + ref[...].astype(F32)
    tok_ref[...] = total[:, :width].astype(BF16)
    route = turn(total[:, width:])
    ids = ids_ref[...]
    expert = lax.broadcasted_iota(jnp.int32, route.shape, 0)
    found = [
        jnp.sum(jnp.where(expert == ids[k : k + 1, :], route, 0.0), axis=0, keepdims=True)
        for k in range(ids.shape[0])
    ]
    route_ref[...] = jnp.concatenate(found, axis=0).astype(BF16)


def shape(dims, dtype=BF16):
    return jax.ShapeDtypeStruct(dims, dtype)


def whole(memory=pltpu.VMEM):
    return pl.BlockSpec(memory_space=memory)


def per_device(n_dp, n_expert, grad_out, expert_ids, route_weights, saved_pre, gate_weight, up_weight, down_weight):
    tok, width = grad_out.shape
    pre = saved_pre[0, 0]
    slots, both = pre.shape
    hidden = both // 2
    cap = slots // n_expert
    full = width + META
    n_z = n_expert // 2
    dests = slots // (cap * STRIDE)
    per = STRIDE * cap
    down_rows = down_weight.shape[1]
    part = both * META // width
    axes = ("dp", "expert")

    apart = [
        [d * n_expert + (rho + STRIDE * k) * 2 + h for k in range(n_z // STRIDE)]
        for d in range(n_dp)
        for rho in range(STRIDE)
        for h in range(2)
    ]
    near = [
        [
            d * n_expert + ((STRIDE * a + (rho - 2 * (d % 2)) % STRIDE + 2 * (d % 2)) % n_z) * 2 + h
            for rho in range(STRIDE)
            for h in range(2)
        ]
        for d in range(n_dp)
        for a in range(n_z // STRIDE)
    ]
    core, me = lax.axis_index("dp") % 2, lax.axis_index("expert")
    shift = 2 * core
    quad = ((me // 2 - shift + n_z) % n_z) // STRIDE
    rho = jnp.arange(dests, dtype=jnp.int32) // 2
    members = ((STRIDE * quad + (rho - shift + STRIDE) % STRIDE + shift) % n_z) * 2 + jnp.arange(
        dests, dtype=jnp.int32
    ) % 2
    mine = jnp.stack([me, core]).astype(jnp.int32)

    rows, pack = pl.pallas_call(
        prep_kernel,
        out_shape=(shape((tok, full)), shape((part + down_rows, width))),
        in_specs=[whole(pltpu.HBM)] * 6,
        out_specs=(whole(), whole()),
        scratch_shapes=[
            pltpu.VMEM((expert_ids.shape[1], tok), jnp.int32),
            pltpu.VMEM((expert_ids.shape[1], tok), BF16),
            pltpu.VMEM((META, hidden), BF16),
            pltpu.VMEM((META, hidden), BF16),
            pltpu.SemaphoreType.DMA((6,)),
        ],
        compiler_params=params(12),
        name="prep",
    )(grad_out, expert_ids.T, route_weights.T, gate_weight[0], up_weight[0], down_weight[0])
    packs = lax.all_gather(pack, "dp", axis=0, tiled=False)
    blocks = lax.all_gather(rows, axes, axis=0, tiled=True, axis_index_groups=apart)
    send, select = pl.pallas_call(
        functools.partial(select_kernel, cap),
        out_shape=(shape((dests, per, full)), shape((slots, STRIDE * tok))),
        in_specs=[whole(pltpu.SMEM), whole()],
        out_specs=(whole(), whole()),
        compiler_params=params(16),
        name="select",
    )(members, blocks)
    got = lax.all_to_all(send, axes, 0, 0, axis_index_groups=near, tiled=True).reshape(slots, full)
    hid, turned, slope, silu = pl.pallas_call(
        functools.partial(act_kernel, cap, down_rows),
        out_shape=(
            shape((slots, hidden)),
            shape((hidden, slots)),
            shape((slots, hidden), F32),
            shape((slots, hidden), F32),
        ),
        in_specs=[whole()],
        out_specs=(whole(),) * 4,
        compiler_params=params(24),
        cost_estimate=pl.CostEstimate(flops=slots * slots * both * 2, bytes_accessed=8 * slots * both, transcendentals=0),
        name="act",
    )(pre)
    keep, give = pl.pallas_call(
        down_kernel,
        out_shape=(shape((hidden // 2, width)), shape((hidden // 2, width))),
        in_specs=[whole(pltpu.SMEM), whole(), whole()],
        out_specs=(whole(), whole()),
        compiler_params=params(20),
        cost_estimate=pl.CostEstimate(flops=2 * slots * hidden * width, bytes_accessed=2 * (slots + hidden) * width, transcendentals=0),
        name="down",
    )(mine, got, turned)
    taken = lax.ppermute(give, "dp", [(d, d ^ 1) for d in range(n_dp)])
    chip_part = (keep.astype(F32) + taken.astype(F32)).astype(BF16)
    got, chip_part = lax.optimization_barrier((got, chip_part))
    down_grad = lax.psum_scatter(
        chip_part,
        "dp",
        scatter_dimension=0,
        tiled=True,
        axis_index_groups=[list(range(c, n_dp, 2)) for c in range(2)],
    )
    pair = 2
    back = pl.pallas_call(
        mid_kernel,
        out_shape=shape((slots, full)),
        in_specs=[whole(pltpu.SMEM)] + [whole()] * 4 + [whole(pltpu.HBM)],
        out_specs=whole(pltpu.HBM),
        scratch_shapes=[
            pltpu.VMEM((slots, full), BF16),
            pltpu.VMEM((slots, both), BF16),
            pltpu.VMEM((n_dp, down_rows, width), BF16),
            pltpu.VMEM((n_dp // pair, pair, part, width), BF16),
            pltpu.VMEM((2, both, pair * META), BF16),
            pltpu.SemaphoreType.DMA((n_dp // pair + 1,)),
            pltpu.SemaphoreType.DMA((n_dp // pair + 1,)),
        ],
        compiler_params=params(36),
        cost_estimate=pl.CostEstimate(flops=6 * slots * hidden * width, bytes_accessed=2 * 3 * hidden * width, transcendentals=0),
        name="mid",
    )(mine, got, hid, slope, silu, packs)
    back = lax.all_to_all(
        back.reshape(dests, per, full), axes, 0, 0, axis_index_groups=near, tiled=True
    ).reshape(slots, full)
    place = (me // 2 // STRIDE).reshape(1).astype(jnp.int32)
    own, *sums = pl.pallas_call(
        combine_kernel,
        out_shape=(shape((tok, full), F32),) + (shape((tok, full)),) * (STRIDE - 1),
        in_specs=[whole(pltpu.SMEM), whole(), whole()],
        out_specs=(whole(),) * STRIDE,
        scratch_shapes=[pltpu.VMEM((STRIDE * tok, full), F32)],
        compiler_params=params(12),
        name="combine",
    )(place, select, back)
    parts = [own] + [
        lax.ppermute(
            value,
            "expert",
            [(e, ((e // 2 + STRIDE * (m + 1)) % n_z) * 2 + e % 2) for e in range(n_expert)],
        )
        for m, value in enumerate(sums)
    ]
    token_grad, route_grad = pl.pallas_call(
        last_kernel,
        out_shape=(shape((tok, width)), shape(expert_ids.shape[::-1])),
        in_specs=[whole()] * (1 + STRIDE),
        out_specs=(whole(), whole()),
        compiler_params=params(8),
        name="last",
    )(expert_ids.T, *parts)
    return token_grad, route_grad.T, down_grad[None]


def solution(mesh):
    return jax.shard_map(
        functools.partial(per_device, mesh.shape["dp"], mesh.shape["expert"]),
        mesh=mesh,
        in_specs=(
            P(("dp", "expert"), None),
            P(("dp", "expert"), None),
            P(("dp", "expert"), None),
            P("dp", "expert", None, None),
            P("expert", "dp", None),
            P("expert", "dp", None),
            P("expert", "dp", None),
        ),
        out_specs=(P(("dp", "expert"), None), P(("dp", "expert"), None), P("expert", "dp", None)),
        check_vma=False,
    )
```

time: 210 us -> 207 us (0.986); the launches traced: 207 us -> 206 us
  blocking collectives: 67.8 us -> 32.4 us
  starting transfers between devices: 13.3 us -> 32.2 us
  waiting for transfers between devices: 76.2 us -> 89.3 us
    all_to_all x1 -> x0, blocking collectives: 35.3 us -> none  [per_device(): lax.all_to_all(partial.reshape(STRIDE, tok, full), axes, 0, 0, axis_index...]
    ppermute x0 -> x4, waiting for transfers between devices: none -> 23.9 us  [the longest x3 20.2 us: per_device(): lax.ppermute(value, 'expert', [(e, (e // 2 + STRIDE * (m + 1)) % n_z * 2...]
    ppermute x0 -> x4, starting transfers between devices: none -> 19 us  [the longest x3 17.1 us: per_device(): lax.ppermute(value, 'expert', [(e, (e // 2 + STRIDE * (m + 1)) % n_z * 2...]
    all_gather x1, waiting for transfers between devices: 16.3 us -> 5.43 us  [per_device(): packs = lax.all_gather(pack, 'dp', axis=0, tiled=False)]
    reduce_scatter x1, waiting for transfers between devices: 5.84 us -> 0.01 us  [per_device(): lax.psum_scatter(chip_part, 'dp', scatter_dimension=0, tiled=True, axis_i...]
    all_to_all x1, waiting for transfers between devices: 26.7 us -> 32.3 us  [per_device(): lax.all_to_all(back.reshape(dests, per, full), axes, 0, 0, axis_index_gro...]
    unnamed x29 -> x26, local copies, waits for them, and re-layouts: 14.2 us -> 14.3 us
  transfers between devices with their start and end apart: 4 -> 8, of which waited for: 4 -> 7; matrix products, arithmetic and copies ran while one was open for 0% -> 1% of each run, Pallas kernels for 4% -> 4%
where the time goes in v2:
time: 207 us; the launch traced here: 206 us
  waiting for transfers between devices  89.3 us (43%)
  blocking collectives  32.4 us (16%)
  starting transfers between devices  32.2 us (16%)
  Pallas kernels  20.7 us (10%)
  between operations  15.7 us (8%)
  local copies, waits for them, and re-layouts  14.3 us (7%)
    all_gather x1, blocking collectives, per_device(): lax.all_gather(rows, axes, axis=0, tiled=True, axis_index_groups=apart)  32.4 us
    all_to_all x1, waiting for transfers between devices, per_device(): lax.all_to_all(back.reshape(dests, per, full), axes, 0, 0, axis_index_gro...  32.3 us
    all_to_all x1, waiting for transfers between devices, per_device(): lax.all_to_all(send, axes, 0, 0, axis_index_groups=near, tiled=True)  27.1 us
    ppermute x3, waiting for transfers between devices, per_device(): lax.ppermute(value, 'expert', [(e, (e // 2 + STRIDE * (m + 1)) % n_z * 2...  20.2 us
    ppermute x3, starting transfers between devices, per_device(): lax.ppermute(value, 'expert', [(e, (e // 2 + STRIDE * (m + 1)) % n_z * 2...  17.1 us
    unnamed x26, local copies, waits for them, and re-layouts  14.3 us
    pallas_call x1, Pallas kernels, per_device(): pl.pallas_call(mid_kernel, out_shape=shape((slots, full)), in_specs=[whol...  10.8 us
    all_to_all x1, starting transfers between devices, per_device(): lax.all_to_all(back.reshape(dests, per, full), axes, 0, 0, axis_index_gro...  7.98 us
  transfers between devices with their start and end apart: 8, of which 7 were waited for; matrix products, arithmetic and copies ran while one was open for 1% of the time, Pallas kernels for 4%

profile of v2, /device:TPU:1, one launch (start us, length us, event | category | flops | bytes accessed | tf_op | source)
XLA Modules:
  0.0 206.4 jit_solution(6161647691878381020)
XLA Ops:
  8.1 0.9 copy-done.3
  9.0 0.9 copy-done.4
  9.9 0.9 copy-done.5
  10.8 0.9 copy-done.6
  11.7 0.7 copy-done.7
  13.1 2.0 prep.1
  15.3 32.4 %all_gather.9.tok_ref = bf16[128,2176]{1,0:T(8,128)(2,1)S(1)} all-gather(bf16[32,2176]{1,0:T(8,128)(2,1)S(1)} %get-tuple-element.21), channel_id=1, replica_groups={{0,8,16,24},{1,9,17,25},{2,10,18,26},{3,11,19,27},{4,12,20,28},{5,13,21..., dimensions={0}, use_global_device_ids=true | all-gather | bytes 696320 | tf_op jit(solution)/shard_map/all_gather | solution.py:281
  47.7 2.7 %select.27 = (bf16[8,48,2176]{2,1,0:T(8,128)(2,1)}, bf16[384,128]{1,0:T(8,128)(2,1)S(1)}) custom-call(s32[8]{0:T(128)S(1)} %fusion.mine_ref, bf16[128,2176]{1,0:T(8,128)(2,1)S(1)} %all_gather.9.tok_ref), custom_call_target="tpu_custom_call" | custom-call | tf_op jit(solution)/shard_map/select/pallas_call | solution.py:282
  50.4 5.2 %all-to-all-start = ((bf16[8,48,2176]{2,1,0:T(8,128)(2,1)}), bf16[8,48,2176]{2,1,0:T(8,128)(2,1)S(1)}, u32[]{:S(2)}, u32[]{:S(2)}) async-start(bf16[8,48,2176]{2,1,0:T(8,128)(2,1)} %get-tuple-element.23), calls=%async_computation | async-start | bytes 3342336 | tf_op jit(solution)/shard_map/all_to_all | solution.py:290
  55.5 1.3 copy-done.10
  56.9 1.2 act.1
  58.1 1.0 copy-done.1
  59.1 0.8 copy-done.11
  60.1 27.1 %all-to-all-done = bf16[8,48,2176]{2,1,0:T(8,128)(2,1)S(1)} async-done(((bf16[8,48,2176]{2,1,0:T(8,128)(2,1)}), bf16[8,48,2176]{2,1,0:T(8,128)(2,1)S(1)}, u32[]{:S(2)}, u32[]{:S(2)}) %all-to-all-start) | async-done | bytes 1671200 | tf_op jit(solution)/shard_map/all_to_all | solution.py:290
  87.2 1.1 copy-done.12
  88.3 2.5 %down.1 = (bf16[384,2048]{1,0:T(8,128)(2,1)S(1)}, bf16[384,2048]{1,0:T(8,128)(2,1)S(1)}) custom-call(s32[2]{0:T(128)S(1)} %pad_add_fusion.mine_ref, bf16[384,2176]{1,0:T(8,128)(2,1)S(1)} %bitcast.16, bf16[768,384]{1,0:T(8,128)(2,1)S(1)} %copy-done.12), custom_call_target="tpu_custom_call" | custom-call | flops 1207959552 | bytes 4718592 | tf_op jit(solution)/shard_map/down/pallas_call | solution.py:305
  90.8 1.9 collective-permute-start
  92.7 3.7 %collective-permute-done = bf16[384,2048]{1,0:T(8,128)(2,1)S(1)} collective-permute-done((bf16[384,2048]{1,0:T(8,128)(2,1)S(1)}, bf16[384,2048]{1,0:T(8,128)(2,1)S(1)}, u32[]{:S(2)}, u32[]{:S(2)}) %collective-permute-start) | collective-permute-done | bytes 1572896 | tf_op jit(solution)/shard_map/ppermute | solution.py:314
  96.4 1.8 add_convert_fusion
  98.1 5.4 %all-gather.3.cloned.1.call-done = bf16[2304,2048]{1,0:T(8,128)(2,1)} async-done(((bf16[144,2048]{1,0:T(8,128)(2,1)}), bf16[2304,2048]{1,0:T(8,128)(2,1)}) %all-gather.3.cloned.1.call-update) | async-done | bytes 9437200 | tf_op jit(solution)/shard_map/all_gather | solution.py:280
  103.6 3.7 %copy-done = bf16[2304,2048]{1,0:T(8,128)(2,1)S(1)} copy-done((bf16[2304,2048]{1,0:T(8,128)(2,1)S(1)}, bf16[2304,2048]{1,0:T(8,128)(2,1)}, u32[]{:S(2)}) %copy-start) | copy-done | bytes 9437208
  107.2 1.3 copy-done.2
  108.5 10.8 %mid.1 = bf16[384,2176]{1,0:T(8,128)(2,1)} custom-call(s32[2]{0:T(128)S(1)} %pad_add_fusion.mine_ref, bf16[384,2176]{1,0:T(8,128)(2,1)S(1)} %bitcast.17, bf16[384,768]{1,0:T(8,128)(2,1)S(1)} %get-tuple-element.28.hid_ref, f32[384,768]{1,0:T(8,128)S(1)} %get-tuple-element.29.slope_ref, f32[384,768]{1,0:T(8,128)S(1)} %copy-done.2, ...), custom_call_target="tpu_custom_call" | custom-call | flops 3623878656 | bytes 9437184 | tf_op jit(solution)/shard_map/mid/pallas_call | solution.py:325
  119.3 8.0 %all-to-all-start.1 = ((bf16[8,48,2176]{2,1,0:T(8,128)(2,1)}), bf16[8,48,2176]{2,1,0:T(8,128)(2,1)S(1)}, u32[]{:S(2)}, u32[]{:S(2)}) async-start(bf16[8,48,2176]{2,1,0:T(8,128)(2,1)} %bitcast.11), calls=%async_computation.1 | async-start | bytes 3342336 | tf_op jit(solution)/shard_map/all_to_all | solution.py:343
  127.9 32.3 %all-to-all-done.1 = bf16[8,48,2176]{2,1,0:T(8,128)(2,1)S(1)} async-done(((bf16[8,48,2176]{2,1,0:T(8,128)(2,1)}), bf16[8,48,2176]{2,1,0:T(8,128)(2,1)S(1)}, u32[]{:S(2)}, u32[]{:S(2)}) %all-to-all-start.1) | async-done | bytes 1671200 | tf_op jit(solution)/shard_map/all_to_all | solution.py:343
  160.7 4.2 %collective-permute-start.1 = (bf16[32,2176]{1,0:T(8,128)(2,1)S(1)}, bf16[32,2176]{1,0:T(8,128)(2,1)S(1)}, u32[]{:S(2)}, u32[]{:S(2)}) collective-permute-start(bf16[32,2176]{1,0:T(8,128)(2,1)S(1)} %get-tuple-element.33), channel_id=1, source_target_pairs={{0,8},{1,9},{2,10},{3,11},{4,12},{5,13},{6,14},{7,15},{8,16},{9,17... | collective-permute-start | bytes 417800 | tf_op jit(solution)/shard_map/ppermute | solution.py:357
  165.0 8.9 %collective-permute-start.2 = (bf16[32,2176]{1,0:T(8,128)(2,1)S(1)}, bf16[32,2176]{1,0:T(8,128)(2,1)S(1)}, u32[]{:S(2)}, u32[]{:S(2)}) collective-permute-start(bf16[32,2176]{1,0:T(8,128)(2,1)S(1)} %get-tuple-element.34), channel_id=1, source_target_pairs={{0,16},{1,17},{2,18},{3,19},{4,20},{5,21},{6,22},{7,23},{8,24},{9,... | collective-permute-start | bytes 417800 | tf_op jit(solution)/shard_map/ppermute | solution.py:357
  173.8 4.0 %collective-permute-start.3 = (bf16[32,2176]{1,0:T(8,128)(2,1)S(1)}, bf16[32,2176]{1,0:T(8,128)(2,1)S(1)}, u32[]{:S(2)}, u32[]{:S(2)}) collective-permute-start(bf16[32,2176]{1,0:T(8,128)(2,1)S(1)} %get-tuple-element.35), channel_id=1, source_target_pairs={{0,24},{1,25},{2,26},{3,27},{4,28},{5,29},{6,30},{7,31},{8,0},{9,1... | collective-permute-start | bytes 417800 | tf_op jit(solution)/shard_map/ppermute | solution.py:357
  177.8 6.1 %collective-permute-done.1.refs_1_ = bf16[32,2176]{1,0:T(8,128)(2,1)S(1)} collective-permute-done((bf16[32,2176]{1,0:T(8,128)(2,1)S(1)}, bf16[32,2176]{1,0:T(8,128)(2,1)S(1)}, u32[]{:S(2)}, u32[]{:S(2)}) %collective-permute-start.1) | collective-permute-done | bytes 139296 | tf_op jit(solution)/shard_map/ppermute | solution.py:357
  183.9 8.2 %collective-permute-done.2.refs_2_ = bf16[32,2176]{1,0:T(8,128)(2,1)S(1)} collective-permute-done((bf16[32,2176]{1,0:T(8,128)(2,1)S(1)}, bf16[32,2176]{1,0:T(8,128)(2,1)S(1)}, u32[]{:S(2)}, u32[]{:S(2)}) %collective-permute-start.2) | collective-permute-done | bytes 139296 | tf_op jit(solution)/shard_map/ppermute | solution.py:357
  192.2 5.9 %collective-permute-done.3.refs_3_ = bf16[32,2176]{1,0:T(8,128)(2,1)S(1)} collective-permute-done((bf16[32,2176]{1,0:T(8,128)(2,1)S(1)}, bf16[32,2176]{1,0:T(8,128)(2,1)S(1)}, u32[]{:S(2)}, u32[]{:S(2)}) %collective-permute-start.3) | collective-permute-done | bytes 139296 | tf_op jit(solution)/shard_map/ppermute | solution.py:357
  198.0 0.9 last.1
  (23 shorter events, 2.0 us)
Async XLA Ops:
  8.0 95.6 %all-gather.3.cloned.1.call-start = ((), (), s32[]{:S(2)}) async-start(), calls=%async_computation.4 | async-start | bytes 10027008 | tf_op jit(solution)/shard_map/all_gather | solution.py:280
  8.0 0.9 copy-start.3
  9.0 0.9 copy-start.4
  9.9 0.9 copy-start.5
  10.8 0.9 copy-start.6
  11.7 0.7 copy-start.7
  12.4 0.7 copy-start.9
  50.4 36.8 %all-to-all-start = ((bf16[8,48,2176]{2,1,0:T(8,128)(2,1)}), bf16[8,48,2176]{2,1,0:T(8,128)(2,1)S(1)}, u32[]{:S(2)}, u32[]{:S(2)}) async-start(bf16[8,48,2176]{2,1,0:T(8,128)(2,1)} %get-tuple-element.23), calls=%async_computation | async-start | bytes 3342336 | tf_op jit(solution)/shard_map/all_to_all | solution.py:290
  55.5 1.3 copy-start.10
  58.1 1.0 copy-start.1
  59.1 0.8 copy-start.11
  87.2 1.1 copy-start.12
  90.8 5.6 %collective-permute-start = (bf16[384,2048]{1,0:T(8,128)(2,1)S(1)}, bf16[384,2048]{1,0:T(8,128)(2,1)S(1)}, u32[]{:S(2)}, u32[]{:S(2)}) collective-permute-start(bf16[384,2048]{1,0:T(8,128)(2,1)S(1)} %get-tuple-element.26), channel_id=1, source_target_pairs={{0,32},{32,0},{64,96},{96,64},{128,160},{160,128},{192,224},{224,1... | collective-permute-start | bytes 4718600 | tf_op jit(solution)/shard_map/ppermute | solution.py:314
  103.6 3.7 %copy-start = (bf16[2304,2048]{1,0:T(8,128)(2,1)S(1)}, bf16[2304,2048]{1,0:T(8,128)(2,1)}, u32[]{:S(2)}) copy-start(bf16[2304,2048]{1,0:T(8,128)(2,1)} %all-gather.3.cloned.1.call-done) | copy-start | bytes 28311556
  107.2 1.3 copy-start.2
  119.3 40.9 %all-to-all-start.1 = ((bf16[8,48,2176]{2,1,0:T(8,128)(2,1)}), bf16[8,48,2176]{2,1,0:T(8,128)(2,1)S(1)}, u32[]{:S(2)}, u32[]{:S(2)}) async-start(bf16[8,48,2176]{2,1,0:T(8,128)(2,1)} %bitcast.11), calls=%async_computation.1 | async-start | bytes 3342336 | tf_op jit(solution)/shard_map/all_to_all | solution.py:343
  127.3 70.8 %copy-start.8 = (s32[32,8]{0,1:T(8,128)S(1)}, s32[32,8]{0,1:T(8,128)}, u32[]{:S(2)}) copy-start(s32[32,8]{0,1:T(8,128)} %param.8) | copy-start | bytes 3076
  127.3 71.7 %reduce-scatter.2.cloned.1.call-start = ((), (), s32[]{:S(2)}) async-start(), calls=%async_computation.3 | async-start | bytes 1769472 | tf_op jit(solution)/shard_map/reduce_scatter | solution.py:317
  160.7 23.2 %collective-permute-start.1 = (bf16[32,2176]{1,0:T(8,128)(2,1)S(1)}, bf16[32,2176]{1,0:T(8,128)(2,1)S(1)}, u32[]{:S(2)}, u32[]{:S(2)}) collective-permute-start(bf16[32,2176]{1,0:T(8,128)(2,1)S(1)} %get-tuple-element.33), channel_id=1, source_target_pairs={{0,8},{1,9},{2,10},{3,11},{4,12},{5,13},{6,14},{7,15},{8,16},{9,17... | collective-permute-start | bytes 417800 | tf_op jit(solution)/shard_map/ppermute | solution.py:357
  165.0 27.2 %collective-permute-start.2 = (bf16[32,2176]{1,0:T(8,128)(2,1)S(1)}, bf16[32,2176]{1,0:T(8,128)(2,1)S(1)}, u32[]{:S(2)}, u32[]{:S(2)}) collective-permute-start(bf16[32,2176]{1,0:T(8,128)(2,1)S(1)} %get-tuple-element.34), channel_id=1, source_target_pairs={{0,16},{1,17},{2,18},{3,19},{4,20},{5,21},{6,22},{7,23},{8,24},{9,... | collective-permute-start | bytes 417800 | tf_op jit(solution)/shard_map/ppermute | solution.py:357
  173.8 24.2 %collective-permute-start.3 = (bf16[32,2176]{1,0:T(8,128)(2,1)S(1)}, bf16[32,2176]{1,0:T(8,128)(2,1)S(1)}, u32[]{:S(2)}, u32[]{:S(2)}) collective-permute-start(bf16[32,2176]{1,0:T(8,128)(2,1)S(1)} %get-tuple-element.35), channel_id=1, source_target_pairs={{0,24},{1,25},{2,26},{3,27},{4,28},{5,29},{6,30},{7,31},{8,0},{9,1... | collective-permute-start | bytes 417800 | tf_op jit(solution)/shard_map/ppermute | solution.py:357
Sparse Core Ops, SparseCore 0:
  15.3 88.2 all-gather.2
Sparse Core Ops, SparseCore 1:
  131.2 44.0 reduce-scatter.1

commit v3 on v2

--- a/solution.py
+++ b/solution.py
@@ -9,6 +9,7 @@
 
 BF16, F32 = jnp.bfloat16, jnp.float32
 META = 128
+TILE = 512
 STRIDE = 4
 
 
@@ -26,29 +27,37 @@
 
 
 def prep_kernel(
-    rows_ref, ids_ref, weight_ref, gate_ref, up_ref, down_ref, tok_ref, pack_ref,
+    rows_ref, ids_ref, weight_ref, gate_ref, up_ref, down_ref, tok_ref, first_ref, second_ref,
     ids_buf, weight_buf, gate_buf, up_buf, sems,
 ):
     tok, width = rows_ref.shape
     topk = ids_ref.shape[0]
     hidden = gate_ref.shape[1]
-    part = 2 * hidden * META // width
+    down_rows = down_ref.shape[0]
     copies = [
         pltpu.make_async_copy(gate_ref, gate_buf, sems.at[0]),
         pltpu.make_async_copy(up_ref, up_buf, sems.at[1]),
-        pltpu.make_async_copy(down_ref, pack_ref.at[pl.ds(part, down_ref.shape[0]), :], sems.at[2]),
+        pltpu.make_async_copy(down_ref, first_ref.at[pl.ds(0, down_rows), :], sems.at[2]),
         pltpu.make_async_copy(ids_ref, ids_buf, sems.at[3]),
         pltpu.make_async_copy(weight_ref, weight_buf, sems.at[4]),
         pltpu.make_async_copy(rows_ref, tok_ref.at[:, pl.ds(0, width)], sems.at[5]),
     ]
     for copy in copies:
         copy.start()
-    for at, buf in enumerate((gate_buf, up_buf)):
-        copies[at].wait()
-        turned = buf[...].astype(F32).T.astype(BF16)
-        for g in range(hidden // part):
-            lane = (at * (hidden // part) + g) * META
-            pack_ref[0:part, lane : lane + META] = turned[g * part : (g + 1) * part]
+    copies[0].wait()
+    copies[1].wait()
+    piece = TILE // 2
+    half = gate_ref.shape[0] // 2
+    for which, (ref, base) in enumerate(((first_ref, down_rows), (second_ref, 0))):
+        for i in range(half // 16):
+            for p in range(2 * hidden // piece):
+                n = i * (2 * hidden // TILE) + p // 2
+                row = base + n // (width // TILE) * 16
+                lane = n % (width // TILE) * TILE + p % 2 * piece
+                buf = gate_buf if p * piece < hidden else up_buf
+                src = p * piece % hidden
+                begin = which * half + i * 16
+                ref[row : row + 16, lane : lane + piece] = buf[begin : begin + 16, src : src + piece]
     copies[3].wait()
     copies[4].wait()
     meta = jnp.concatenate([ids_buf[...].astype(F32), weight_buf[...].astype(F32)], axis=0)
@@ -134,26 +143,55 @@
             ).astype(BF16)
 
 
-def mid_kernel(
-    mine_ref, got_ref, hid_ref, slope_ref, silu_ref, pack_ref, out_ref,
-    out_buf, both_buf, down_buf, pack_buf, wide_buf, in_sems, out_sems,
+def fetch(pack_ref, base, wide_buf, sems, first):
+    _, rows, both = wide_buf.shape
+    across, per = both // TILE, pack_ref.shape[2] // TILE
+    copies = []
+    for i in range(rows // 16):
+        for j in range(across):
+            n = i * across + j
+            copies.append(
+                pltpu.make_async_copy(
+                    pack_ref.at[:, pl.ds(base + n // per * 16, 16), pl.ds(n % per * TILE, TILE)],
+                    wide_buf.at[:, pl.ds(i * 16, 16), pl.ds(j * TILE, TILE)],
+                    sems.at[first + n],
+                )
+            )
+    for copy in copies:
+        copy.start()
+    return copies
+
+
+def multiply(both_ref, wide_buf, out_buf, out_ref, sems, backs):
+    columns = 256
+    devices, rows, both = wide_buf.shape
+    group = columns // rows
+    for n in range(devices // group):
+        at = n * columns
+        out_buf[:, at : at + columns] = lax.dot_general(
+            both_ref[...],
+            wide_buf[n * group : (n + 1) * group].reshape(columns, both),
+            (((1,), (1,)), ((), ())),
+            preferred_element_type=F32,
+        ).astype(BF16)
+        part = pl.ds(at, columns)
+        backs.append(pltpu.make_async_copy(out_buf.at[:, part], out_ref.at[:, part], sems.at[n]))
+        backs[-1].start()
+    for copy in backs:
+        copy.wait()
+
+
+def first_kernel(
+    mine_ref, got_ref, hid_ref, slope_ref, silu_ref, pack_ref, out_ref, both_ref,
+    out_buf, down_buf, wide_buf, in_sems, out_sems,
 ):
     width = got_ref.shape[1] - META
     hidden = hid_ref.shape[1]
-    pairs, pair, part, _ = pack_buf.shape
     down_rows = down_buf.shape[1]
-    down_copy = pltpu.make_async_copy(
-        pack_ref.at[:, pl.ds(part, down_rows), :], down_buf, in_sems.at[pairs]
-    )
+    half = out_buf.shape[1] - META
+    down_copy = pltpu.make_async_copy(pack_ref.at[:, pl.ds(0, down_rows), :], down_buf, in_sems.at[0])
     down_copy.start()
-    copies = [
-        pltpu.make_async_copy(
-            pack_ref.at[pl.ds(p * pair, pair), pl.ds(0, part), :], pack_buf.at[p], in_sems.at[p]
-        )
-        for p in range(pairs)
-    ]
-    for copy in copies:
-        copy.start()
+    copies = fetch(pack_ref, down_rows, wide_buf, in_sems, 1)
     w = slot_weight(got_ref[:, width:], mine_ref[0])
     down_copy.wait()
     q = lax.dot_general(
@@ -164,28 +202,23 @@
     )
     route = jnp.sum(q * hid_ref[...].astype(F32), axis=1, keepdims=True)
     grad = w * q
-    both_buf[:, :hidden] = (grad * slope_ref[...]).astype(BF16)
-    both_buf[:, hidden:] = (grad * silu_ref[...]).astype(BF16)
+    both_ref[:, :hidden] = (grad * slope_ref[...]).astype(BF16)
+    both_ref[:, hidden:] = (grad * silu_ref[...]).astype(BF16)
     lane = lax.broadcasted_iota(jnp.int32, (got_ref.shape[0], META), 1)
-    out_buf[:, width:] = jnp.where(lane == mine_ref[0], route, 0.0).astype(BF16)
-    backs = [pltpu.make_async_copy(out_buf.at[:, pl.ds(width, META)], out_ref.at[:, pl.ds(width, META)], out_sems.at[pairs])]
+    out_buf[:, half:] = jnp.where(lane == mine_ref[0], route, 0.0).astype(BF16)
+    extra = pl.ds(half, META)
+    last = out_sems.shape[0] - 1
+    backs = [pltpu.make_async_copy(out_buf.at[:, extra], out_ref.at[:, extra], out_sems.at[last])]
     backs[0].start()
-    for p in range(pairs):
-        copies[p].wait()
-        for b in range(pair):
-            for g in range(2 * hidden // part):
-                wide_buf[p % 2, g * part : (g + 1) * part, b * META : (b + 1) * META] = pack_buf[
-                    p, b, :, g * META : (g + 1) * META
-                ]
-        at = p * pair * META
-        out_buf[:, at : at + pair * META] = jnp.dot(
-            both_buf[...], wide_buf[p % 2], preferred_element_type=F32
-        ).astype(BF16)
-        columns = pl.ds(at, pair * META)
-        backs.append(pltpu.make_async_copy(out_buf.at[:, columns], out_ref.at[:, columns], out_sems.at[p]))
-        backs[-1].start()
-    for copy in backs:
+    for copy in copies:
         copy.wait()
+    multiply(both_ref, wide_buf, out_buf, out_ref, out_sems, backs)
+
+
+def second_kernel(both_ref, pack_ref, out_ref, out_buf, wide_buf, in_sems, out_sems):
+    for copy in fetch(pack_ref, 0, wide_buf, in_sems, 0):
+        copy.wait()
+    multiply(both_ref, wide_buf, out_buf, out_ref, out_sems, [])
 
 
 def combine_kernel(place_ref, select_ref, back_ref, *refs):
@@ -200,13 +233,20 @@
 
 
 def last_kernel(ids_ref, *refs):
-    parts, (tok_ref, route_ref) = refs[:STRIDE], refs[STRIDE:]
+    first, second, (tok_ref, route_ref) = refs[:STRIDE], refs[STRIDE : 2 * STRIDE], refs[2 * STRIDE :]
     tok, width = tok_ref.shape
-    total = parts[0][...]
-    for ref in parts[1:]:
-        total = total + ref[...].astype(F32)
-    tok_ref[...] = total[:, :width].astype(BF16)
-    route = turn(total[:, width:])
+    sums = []
+    for parts in (first, second):
+        total = parts[0][...]
+        for ref in parts[1:]:
+            total = total + ref[...].astype(F32)
+        sums.append(total)
+    low = lax.broadcasted_iota(jnp.int32, (tok, META), 1) < META // 2
+    for j in range(width // META // 2):
+        a, b = (x[:, j * META : (j + 1) * META] for x in sums)
+        tok_ref[:, 2 * j * META : (2 * j + 1) * META] = jnp.where(low, a, pltpu.roll(b, META // 2, 1)).astype(BF16)
+        tok_ref[:, (2 * j + 1) * META : (2 * j + 2) * META] = jnp.where(low, pltpu.roll(a, META // 2, 1), b).astype(BF16)
+    route = turn(sums[0][:, width // 2 :])
     ids = ids_ref[...]
     expert = lax.broadcasted_iota(jnp.int32, route.shape, 0)
     found = [
@@ -222,6 +262,10 @@
 
 def whole(memory=pltpu.VMEM):
     return pl.BlockSpec(memory_space=memory)
+
+
+def exchange(value, axes, groups):
+    return lax.all_to_all(value, axes, 0, 0, axis_index_groups=groups, tiled=True)
 
 
 def per_device(n_dp, n_expert, grad_out, expert_ids, route_weights, saved_pre, gate_weight, up_weight, down_weight):
@@ -235,7 +279,6 @@
     dests = slots // (cap * STRIDE)
     per = STRIDE * cap
     down_rows = down_weight.shape[1]
-    part = both * META // width
     axes = ("dp", "expert")
 
     apart = [
@@ -262,22 +305,25 @@
     ) % 2
     mine = jnp.stack([me, core]).astype(jnp.int32)
 
-    rows, pack = pl.pallas_call(
+    half_rows = gate_weight.shape[1] // 2
+    part = half_rows * both // width
+    rows, pack, pack_b = pl.pallas_call(
         prep_kernel,
-        out_shape=(shape((tok, full)), shape((part + down_rows, width))),
+        out_shape=(shape((tok, full)), shape((down_rows + part, width)), shape((part, width))),
         in_specs=[whole(pltpu.HBM)] * 6,
-        out_specs=(whole(), whole()),
+        out_specs=(whole(),) * 3,
         scratch_shapes=[
             pltpu.VMEM((expert_ids.shape[1], tok), jnp.int32),
             pltpu.VMEM((expert_ids.shape[1], tok), BF16),
-            pltpu.VMEM((META, hidden), BF16),
-            pltpu.VMEM((META, hidden), BF16),
+            pltpu.VMEM((2 * half_rows, hidden), BF16),
+            pltpu.VMEM((2 * half_rows, hidden), BF16),
             pltpu.SemaphoreType.DMA((6,)),
         ],
-        compiler_params=params(12),
+        compiler_params=params(60),
         name="prep",
     )(grad_out, expert_ids.T, route_weights.T, gate_weight[0], up_weight[0], down_weight[0])
     packs = lax.all_gather(pack, "dp", axis=0, tiled=False)
+    packs_b = lax.all_gather(pack_b, "dp", axis=0, tiled=False)
     blocks = lax.all_gather(rows, axes, axis=0, tiled=True, axis_index_groups=apart)
     send, select = pl.pallas_call(
         functools.partial(select_kernel, cap),
@@ -287,7 +333,7 @@
         compiler_params=params(16),
         name="select",
     )(members, blocks)
-    got = lax.all_to_all(send, axes, 0, 0, axis_index_groups=near, tiled=True).reshape(slots, full)
+    got = exchange(send, axes, near).reshape(slots, full)
     hid, turned, slope, silu = pl.pallas_call(
         functools.partial(act_kernel, cap, down_rows),
         out_shape=(
@@ -302,6 +348,27 @@
         cost_estimate=pl.CostEstimate(flops=slots * slots * both * 2, bytes_accessed=8 * slots * both, transcendentals=0),
         name="act",
     )(pre)
+    columns = 256
+    pieces = half_rows // 16 * (both // TILE)
+    back, grads = pl.pallas_call(
+        first_kernel,
+        out_shape=(shape((slots, width // 2 + META)), shape((slots, both))),
+        in_specs=[whole(pltpu.SMEM)] + [whole()] * 4 + [whole(pltpu.HBM)],
+        out_specs=(whole(pltpu.HBM), whole()),
+        scratch_shapes=[
+            pltpu.VMEM((slots, width // 2 + META), BF16),
+            pltpu.VMEM((n_dp, down_rows, width), BF16),
+            pltpu.VMEM((n_dp, half_rows, both), BF16),
+            pltpu.SemaphoreType.DMA((pieces + 1,)),
+            pltpu.SemaphoreType.DMA((width // 2 // columns + 1,)),
+        ],
+        compiler_params=params(54),
+        cost_estimate=pl.CostEstimate(flops=4 * slots * hidden * width, bytes_accessed=4 * hidden * width, transcendentals=0),
+        name="first",
+    )(mine, got, hid, slope, silu, packs)
+    ret = exchange(back.reshape(dests, per, -1), axes, near).reshape(slots, -1)
+
+    got, back = lax.optimization_barrier((got, back))
     keep, give = pl.pallas_call(
         down_kernel,
         out_shape=(shape((hidden // 2, width)), shape((hidden // 2, width))),
@@ -313,7 +380,6 @@
     )(mine, got, turned)
     taken = lax.ppermute(give, "dp", [(d, d ^ 1) for d in range(n_dp)])
     chip_part = (keep.astype(F32) + taken.astype(F32)).astype(BF16)
-    got, chip_part = lax.optimization_barrier((got, chip_part))
     down_grad = lax.psum_scatter(
         chip_part,
         "dp",
@@ -321,50 +387,46 @@
         tiled=True,
         axis_index_groups=[list(range(c, n_dp, 2)) for c in range(2)],
     )
-    pair = 2
-    back = pl.pallas_call(
-        mid_kernel,
-        out_shape=shape((slots, full)),
-        in_specs=[whole(pltpu.SMEM)] + [whole()] * 4 + [whole(pltpu.HBM)],
+
+    back_b = pl.pallas_call(
+        second_kernel,
+        out_shape=shape((slots, width // 2)),
+        in_specs=[whole(), whole(pltpu.HBM)],
         out_specs=whole(pltpu.HBM),
         scratch_shapes=[
-            pltpu.VMEM((slots, full), BF16),
-            pltpu.VMEM((slots, both), BF16),
-            pltpu.VMEM((n_dp, down_rows, width), BF16),
-            pltpu.VMEM((n_dp // pair, pair, part, width), BF16),
-            pltpu.VMEM((2, both, pair * META), BF16),
-            pltpu.SemaphoreType.DMA((n_dp // pair + 1,)),
-            pltpu.SemaphoreType.DMA((n_dp // pair + 1,)),
+            pltpu.VMEM((slots, width // 2), BF16),
+            pltpu.VMEM((n_dp, half_rows, both), BF16),
+            pltpu.SemaphoreType.DMA((pieces,)),
+            pltpu.SemaphoreType.DMA((width // 2 // columns,)),
         ],
-        compiler_params=params(36),
-        cost_estimate=pl.CostEstimate(flops=6 * slots * hidden * width, bytes_accessed=2 * 3 * hidden * width, transcendentals=0),
-        name="mid",
-    )(mine, got, hid, slope, silu, packs)
-    back = lax.all_to_all(
-        back.reshape(dests, per, full), axes, 0, 0, axis_index_groups=near, tiled=True
-    ).reshape(slots, full)
+        compiler_params=params(56),
+        cost_estimate=pl.CostEstimate(flops=2 * slots * hidden * width, bytes_accessed=2 * hidden * width, transcendentals=0),
+        name="second",
+    )(grads, packs_b)
+    ret_b = exchange(back_b.reshape(dests, per, -1), axes, near).reshape(slots, -1)
+    ret, back_b = lax.optimization_barrier((ret, back_b))
+
     place = (me // 2 // STRIDE).reshape(1).astype(jnp.int32)
-    own, *sums = pl.pallas_call(
-        combine_kernel,
-        out_shape=(shape((tok, full), F32),) + (shape((tok, full)),) * (STRIDE - 1),
-        in_specs=[whole(pltpu.SMEM), whole(), whole()],
-        out_specs=(whole(),) * STRIDE,
-        scratch_shapes=[pltpu.VMEM((STRIDE * tok, full), F32)],
-        compiler_params=params(12),
-        name="combine",
-    )(place, select, back)
-    parts = [own] + [
-        lax.ppermute(
-            value,
-            "expert",
-            [(e, ((e // 2 + STRIDE * (m + 1)) % n_z) * 2 + e % 2) for e in range(n_expert)],
-        )
-        for m, value in enumerate(sums)
-    ]
+    parts = []
+    for name, value in (("sum_first", ret), ("sum_second", ret_b)):
+        dims = (tok, value.shape[1])
+        own, *sums = pl.pallas_call(
+            combine_kernel,
+            out_shape=(shape(dims, F32),) + (shape(dims),) * (STRIDE - 1),
+            in_specs=[whole(pltpu.SMEM), whole(), whole()],
+            out_specs=(whole(),) * STRIDE,
+            scratch_shapes=[pltpu.VMEM((STRIDE * tok, value.shape[1]), F32)],
+            compiler_params=params(12),
+            name=name,
+        )(place, select, value)
+        parts.append(own)
+        for m, one in enumerate(sums):
+            perm = [(e, ((e // 2 + STRIDE * (m + 1)) % n_z) * 2 + e % 2) for e in range(n_expert)]
+            parts.append(lax.ppermute(one, "expert", perm))
     token_grad, route_grad = pl.pallas_call(
         last_kernel,
         out_shape=(shape((tok, width)), shape(expert_ids.shape[::-1])),
-        in_specs=[whole()] * (1 + STRIDE),
+        in_specs=[whole()] * (1 + 2 * STRIDE),
         out_specs=(whole(), whole()),
         compiler_params=params(8),
         name="last",

time: 207 us -> 235 us (1.14)
  starting transfers between devices: 32.2 us -> 53.6 us
  local copies, waits for them, and re-layouts: 14.3 us -> 4.91 us
  waiting for transfers between devices: 89.3 us -> 97.3 us
  Pallas kernels: 20.7 us -> 27 us
    all_gather x0 -> x1, waiting for transfers between devices: none -> 36.8 us  [per_device(): packs_b = lax.all_gather(pack_b, 'dp', axis=0, tiled=False)]
    ppermute x3 -> x6, starting transfers between devices: 17.1 us -> 33.9 us  [per_device(): parts.append(lax.ppermute(one, 'expert', perm))]
    ppermute x3 -> x6, waiting for transfers between devices: 20.2 us -> 6.05 us  [per_device(): parts.append(lax.ppermute(one, 'expert', perm))]
    unnamed x26 -> x24, local copies, waits for them, and re-layouts: 14.3 us -> 4.91 us
    all_to_all x2 -> x3, waiting for transfers between devices: 59.4 us -> 51.8 us  [exchange(): lax.all_to_all(value, axes, 0, 0, axis_index_groups=groups, tiled=True)]
    pallas_call x3 -> x5, Pallas kernels: 13.4 us -> 18.8 us  [the longest x1 10.2 us: per_device(): pl.pallas_call(first_kernel, out_shape=(shape((slots, width // 2 + META))...]
    all_to_all x2 -> x3, starting transfers between devices: 13.1 us -> 17.5 us  [exchange(): lax.all_to_all(value, axes, 0, 0, axis_index_groups=groups, tiled=True)]
    ppermute x1, waiting for transfers between devices: 3.67 us -> 0.01 us  [per_device(): taken = lax.ppermute(give, 'dp', [(d, d ^ 1) for d in range(n_dp)])]
  transfers between devices with their start and end apart: 8 -> 13, of which waited for: 7 -> 7; matrix products, arithmetic and copies ran while one was open for 1% -> 2% of each run, Pallas kernels for 4% -> 8%
where the time goes in v3:
time: 235 us; the launch traced here: 233 us
  waiting for transfers between devices  97.3 us (41%)
  starting transfers between devices  53.6 us (23%)
  blocking collectives  32.6 us (14%)
  Pallas kernels  27 us (11%)
  between operations  14 us (6%)
  local copies, waits for them, and re-layouts  4.91 us (2%)
  other arithmetic  3.84 us (2%)
    all_to_all x3, waiting for transfers between devices, exchange(): lax.all_to_all(value, axes, 0, 0, axis_index_groups=groups, tiled=True)  51.8 us
    all_gather x1, waiting for transfers between devices, per_device(): packs_b = lax.all_gather(pack_b, 'dp', axis=0, tiled=False)  36.8 us
    ppermute x6, starting transfers between devices, per_device(): parts.append(lax.ppermute(one, 'expert', perm))  33.9 us
    all_gather x1, blocking collectives, per_device(): lax.all_gather(rows, axes, axis=0, tiled=True, axis_index_groups=apart)  32.6 us
    all_to_all x3, starting transfers between devices, exchange(): lax.all_to_all(value, axes, 0, 0, axis_index_groups=groups, tiled=True)  17.5 us
    pallas_call x1, Pallas kernels, per_device(): pl.pallas_call(first_kernel, out_shape=(shape((slots, width // 2 + META))...  10.2 us
    ppermute x6, waiting for transfers between devices, per_device(): parts.append(lax.ppermute(one, 'expert', perm))  6.05 us
    pallas_call x1, Pallas kernels, per_device(): pl.pallas_call(second_kernel, out_shape=shape((slots, width // 2)), in_sp...  5.64 us
  transfers between devices with their start and end apart: 13, of which 7 were waited for; matrix products, arithmetic and copies ran while one was open for 2% of the time, Pallas kernels for 8%

profile of v3, /device:TPU:1, one launch (start us, length us, event | category | flops | bytes accessed | tf_op | source)
XLA Modules:
  0.0 233.3 jit_solution(4483736855570008695)
XLA Ops:
  7.2 2.1 prep.1
  9.5 32.6 %all_gather.15.tok_ref = bf16[128,2176]{1,0:T(8,128)(2,1)S(1)} all-gather(bf16[32,2176]{1,0:T(8,128)(2,1)} %get-tuple-element.28), channel_id=1, replica_groups={{0,8,16,24},{1,9,17,25},{2,10,18,26},{3,11,19,27},{4,12,20,28},{5,13,21..., dimensions={0}, use_global_device_ids=true | all-gather | bytes 696320 | tf_op jit(solution)/shard_map/all_gather | solution.py:327
  42.1 2.7 %select.27 = (bf16[8,48,2176]{2,1,0:T(8,128)(2,1)}, bf16[384,128]{1,0:T(8,128)(2,1)S(1)}) custom-call(s32[8]{0:T(128)S(1)} %fusion.mine_ref, bf16[128,2176]{1,0:T(8,128)(2,1)S(1)} %all_gather.15.tok_ref), custom_call_target="tpu_custom_call" | custom-call | tf_op jit(solution)/shard_map/select/pallas_call | solution.py:328
  44.8 5.3 %all-to-all-start = ((bf16[8,48,2176]{2,1,0:T(8,128)(2,1)}), bf16[8,48,2176]{2,1,0:T(8,128)(2,1)S(1)}, u32[]{:S(2)}, u32[]{:S(2)}) async-start(bf16[8,48,2176]{2,1,0:T(8,128)(2,1)} %get-tuple-element.30), calls=%async_computation | async-start | bytes 3342336 | tf_op jit(solution)/shard_map/all_to_all | solution.py:268
  50.1 0.7 all-gather.7.cloned.1.call-update
  50.8 1.2 act.1
  52.1 1.0 copy-done.4
  53.1 1.1 copy-done.5
  54.2 0.8 copy-done.6
  55.0 0.8 copy-done.10
  56.5 25.3 %all-to-all-done = bf16[8,48,2176]{2,1,0:T(8,128)(2,1)S(1)} async-done(((bf16[8,48,2176]{2,1,0:T(8,128)(2,1)}), bf16[8,48,2176]{2,1,0:T(8,128)(2,1)S(1)}, u32[]{:S(2)}, u32[]{:S(2)}) %all-to-all-start) | async-done | bytes 1671200 | tf_op jit(solution)/shard_map/all_to_all | solution.py:268
  81.7 1.9 all-gather.5.cloned.1.call-done
  83.6 10.2 %first.1 = (bf16[384,1152]{1,0:T(8,128)(2,1)}, bf16[384,1536]{1,0:T(8,128)(2,1)}) custom-call(s32[2]{0:T(128)} %pad_add_fusion.mine_ref, bf16[384,2176]{1,0:T(8,128)(2,1)} %bitcast.18, bf16[384,768]{1,0:T(8,128)(2,1)} %copy-done.6, f32[384,768]{1,0:T(8,128)} %copy-done.4, f32[384,768]{1,0:T(8,128)} %copy-done.5, bf16[16,96,2048]{2,1,0:T(8,128)(2,1)} %bitcast.25), custom_call_target="tpu_custom_call" | custom-call | flops 2415919104 | bytes 6291456 | tf_op jit(solution)/shard_map/first/pallas_call | solution.py:353
  93.9 36.8 %all-gather.7.cloned.1.call-done = bf16[768,2048]{1,0:T(8,128)(2,1)} async-done(((bf16[48,2048]{1,0:T(8,128)(2,1)}), bf16[768,2048]{1,0:T(8,128)(2,1)}) %all-gather.7.cloned.1.call-update) | async-done | bytes 3145744 | tf_op jit(solution)/shard_map/all_gather | solution.py:326
  130.7 5.6 %second.1 = bf16[384,1024]{1,0:T(8,128)(2,1)} custom-call(bf16[384,1536]{1,0:T(8,128)(2,1)} %get-tuple-element.36.both_ref, bf16[16,48,2048]{2,1,0:T(8,128)(2,1)} %bitcast.27), custom_call_target="tpu_custom_call" | custom-call | flops 1207959552 | bytes 3145728 | tf_op jit(solution)/shard_map/second/pallas_call | solution.py:391
  136.4 8.1 %all-to-all-start.2 = ((bf16[8,48,1024]{2,1,0:T(8,128)(2,1)}), bf16[8,48,1024]{2,1,0:T(8,128)(2,1)S(1)}, u32[]{:S(2)}, u32[]{:S(2)}) async-start(bf16[8,48,1024]{2,1,0:T(8,128)(2,1)} %bitcast.26), calls=%async_computation.2 | async-start | bytes 1572864 | tf_op jit(solution)/shard_map/all_to_all | solution.py:268
  144.5 3.5 %down.1 = (bf16[384,2048]{1,0:T(8,128)(2,1)S(1)}, bf16[384,2048]{1,0:T(8,128)(2,1)}) custom-call(s32[2]{0:T(128)S(1)} %copy-done.8, bf16[384,2176]{1,0:T(8,128)(2,1)S(1)} %bitcast.19, bf16[768,384]{1,0:T(8,128)(2,1)S(1)} %copy-done.11), custom_call_target="tpu_custom_call" | custom-call | flops 1207959552 | bytes 4718592 | tf_op jit(solution)/shard_map/down/pallas_call | solution.py:372
  148.0 1.1 copy-done.2
  149.1 2.0 collective-permute-start.6
  151.2 10.5 %all-to-all-done.2 = bf16[8,48,1024]{2,1,0:T(8,128)(2,1)S(1)} async-done(((bf16[8,48,1024]{2,1,0:T(8,128)(2,1)}), bf16[8,48,1024]{2,1,0:T(8,128)(2,1)S(1)}, u32[]{:S(2)}, u32[]{:S(2)}) %all-to-all-start.2) | async-done | bytes 786464 | tf_op jit(solution)/shard_map/all_to_all | solution.py:268
  161.6 4.1 %all-to-all-start.1 = ((bf16[8,48,1152]{2,1,0:T(8,128)(2,1)}), bf16[8,48,1152]{2,1,0:T(8,128)(2,1)S(1)}, u32[]{:S(2)}, u32[]{:S(2)}) async-start(bf16[8,48,1152]{2,1,0:T(8,128)(2,1)} %bitcast.28), calls=%async_computation.1 | async-start | bytes 1769472 | tf_op jit(solution)/shard_map/all_to_all | solution.py:268
  165.8 3.2 %add_convert_fusion = bf16[384,2048]{1,0:T(8,128)(2,1)} fusion(bf16[384,2048]{1,0:T(8,128)(2,1)} %collective-permute-done.6, bf16[384,2048]{1,0:T(8,128)(2,1)S(1)} %copy-done.3), kind=kLoop, calls=%fused_computation | loop fusion | flops 3145728 | bytes 4718592 | tf_op jit(solution)/shard_map/convert_element_type | solution.py:382
  169.4 3.8 %collective-permute-start.3 = (bf16[32,1024]{1,0:T(8,128)(2,1)S(1)}, bf16[32,1024]{1,0:T(8,128)(2,1)S(1)}, u32[]{:S(2)}, u32[]{:S(2)}) collective-permute-start(bf16[32,1024]{1,0:T(8,128)(2,1)S(1)} %get-tuple-element.44), channel_id=1, source_target_pairs={{0,8},{1,9},{2,10},{3,11},{4,12},{5,13},{6,14},{7,15},{8,16},{9,17... | collective-permute-start | bytes 196616 | tf_op jit(solution)/shard_map/ppermute | solution.py:425
  173.2 16.1 %all-to-all-done.1 = bf16[8,48,1152]{2,1,0:T(8,128)(2,1)S(1)} async-done(((bf16[8,48,1152]{2,1,0:T(8,128)(2,1)}), bf16[8,48,1152]{2,1,0:T(8,128)(2,1)S(1)}, u32[]{:S(2)}, u32[]{:S(2)}) %all-to-all-start.1) | async-done | bytes 884768 | tf_op jit(solution)/shard_map/all_to_all | solution.py:268
  189.7 3.7 %collective-permute-start = (bf16[32,1152]{1,0:T(8,128)(2,1)S(1)}, bf16[32,1152]{1,0:T(8,128)(2,1)S(1)}, u32[]{:S(2)}, u32[]{:S(2)}) collective-permute-start(bf16[32,1152]{1,0:T(8,128)(2,1)S(1)} %get-tuple-element.40), channel_id=1, source_target_pairs={{0,8},{1,9},{2,10},{3,11},{4,12},{5,13},{6,14},{7,15},{8,16},{9,17... | collective-permute-start | bytes 221192 | tf_op jit(solution)/shard_map/ppermute | solution.py:425
  193.4 10.2 %collective-permute-start.1 = (bf16[32,1152]{1,0:T(8,128)(2,1)S(1)}, bf16[32,1152]{1,0:T(8,128)(2,1)S(1)}, u32[]{:S(2)}, u32[]{:S(2)}) collective-permute-start(bf16[32,1152]{1,0:T(8,128)(2,1)S(1)} %get-tuple-element.41), channel_id=1, source_target_pairs={{0,16},{1,17},{2,18},{3,19},{4,20},{5,21},{6,22},{7,23},{8,24},{9,... | collective-permute-start | bytes 221192 | tf_op jit(solution)/shard_map/ppermute | solution.py:425
  203.6 4.0 %collective-permute-start.2 = (bf16[32,1152]{1,0:T(8,128)(2,1)S(1)}, bf16[32,1152]{1,0:T(8,128)(2,1)S(1)}, u32[]{:S(2)}, u32[]{:S(2)}) collective-permute-start(bf16[32,1152]{1,0:T(8,128)(2,1)S(1)} %get-tuple-element.42), channel_id=1, source_target_pairs={{0,24},{1,25},{2,26},{3,27},{4,28},{5,29},{6,30},{7,31},{8,0},{9,1... | collective-permute-start | bytes 221192 | tf_op jit(solution)/shard_map/ppermute | solution.py:425
  207.6 5.3 %collective-permute-start.4 = (bf16[32,1024]{1,0:T(8,128)(2,1)S(1)}, bf16[32,1024]{1,0:T(8,128)(2,1)S(1)}, u32[]{:S(2)}, u32[]{:S(2)}) collective-permute-start(bf16[32,1024]{1,0:T(8,128)(2,1)S(1)} %get-tuple-element.45), channel_id=1, source_target_pairs={{0,16},{1,17},{2,18},{3,19},{4,20},{5,21},{6,22},{7,23},{8,24},{9,... | collective-permute-start | bytes 196616 | tf_op jit(solution)/shard_map/ppermute | solution.py:425
  212.9 6.9 %collective-permute-start.5 = (bf16[32,1024]{1,0:T(8,128)(2,1)S(1)}, bf16[32,1024]{1,0:T(8,128)(2,1)S(1)}, u32[]{:S(2)}, u32[]{:S(2)}) collective-permute-start(bf16[32,1024]{1,0:T(8,128)(2,1)S(1)} %get-tuple-element.46), channel_id=1, source_target_pairs={{0,24},{1,25},{2,26},{3,27},{4,28},{5,29},{6,30},{7,31},{8,0},{9,1... | collective-permute-start | bytes 196616 | tf_op jit(solution)/shard_map/ppermute | solution.py:425
  219.9 2.1 collective-permute-done.4.refs_6_
  221.9 4.0 %collective-permute-done.5.refs_7_ = bf16[32,1024]{1,0:T(8,128)(2,1)S(1)} collective-permute-done((bf16[32,1024]{1,0:T(8,128)(2,1)S(1)}, bf16[32,1024]{1,0:T(8,128)(2,1)S(1)}, u32[]{:S(2)}, u32[]{:S(2)}) %collective-permute-start.5) | collective-permute-done | bytes 65568 | tf_op jit(solution)/shard_map/ppermute | solution.py:425
  225.9 0.9 last.1
  (34 shorter events, 1.6 us)
Async XLA Ops:
  7.2 76.5 %all-gather.5.cloned.1.call-start = ((), (), s32[]{:S(2)}) async-start(), calls=%async_computation.5 | async-start | bytes 6684672 | tf_op jit(solution)/shard_map/all_gather | solution.py:325
  44.8 6.0 %copy-start.9 = (bf16[1,1,384,1536]{3,2,1,0:T(8,128)(2,1)S(1)}, bf16[1,1,384,1536]{3,2,1,0:T(8,128)(2,1)}, u32[]{:S(2)}) copy-start(bf16[1,1,384,1536]{3,2,1,0:T(8,128)(2,1)} %param.10) | copy-start | bytes 3538948
  44.8 37.0 %all-to-all-start = ((bf16[8,48,2176]{2,1,0:T(8,128)(2,1)}), bf16[8,48,2176]{2,1,0:T(8,128)(2,1)S(1)}, u32[]{:S(2)}, u32[]{:S(2)}) async-start(bf16[8,48,2176]{2,1,0:T(8,128)(2,1)} %get-tuple-element.30), calls=%async_computation | async-start | bytes 3342336 | tf_op jit(solution)/shard_map/all_to_all | solution.py:268
  50.1 80.6 %all-gather.7.cloned.1.call-start = ((), (), s32[]{:S(2)}) async-start(), calls=%async_computation.6 | async-start | bytes 3342336 | tf_op jit(solution)/shard_map/all_gather | solution.py:326
  52.1 1.0 copy-start.4
  53.1 1.1 copy-start.5
  54.2 0.8 copy-start.6
  55.0 0.8 copy-start.10
  81.7 1.9 copy-start
  130.7 13.8 %copy-start.1 = (bf16[8,48,2176]{2,1,0:T(8,128)(2,1)S(1)}, bf16[8,48,2176]{2,1,0:T(8,128)(2,1)}, u32[]{:S(2)}) copy-start(bf16[8,48,2176]{2,1,0:T(8,128)(2,1)} %copy-done) | copy-start | bytes 5013508
  136.4 8.1 %copy-start.8 = (s32[2]{0:T(128)S(1)}, s32[2]{0:T(128)}, u32[]{:S(2)}) copy-start(s32[2]{0:T(128)} %pad_add_fusion.mine_ref) | copy-start | bytes 28
  136.4 8.1 %copy-start.11 = (bf16[768,384]{1,0:T(8,128)(2,1)S(1)}, bf16[768,384]{1,0:T(8,128)(2,1)}, u32[]{:S(2)}) copy-start(bf16[768,384]{1,0:T(8,128)(2,1)} %copy-done.10) | copy-start | bytes 1769476
  136.4 25.3 %all-to-all-start.2 = ((bf16[8,48,1024]{2,1,0:T(8,128)(2,1)}), bf16[8,48,1024]{2,1,0:T(8,128)(2,1)S(1)}, u32[]{:S(2)}, u32[]{:S(2)}) async-start(bf16[8,48,1024]{2,1,0:T(8,128)(2,1)} %bitcast.26), calls=%async_computation.2 | async-start | bytes 1572864 | tf_op jit(solution)/shard_map/all_to_all | solution.py:268
  148.0 1.1 copy-start.2
  149.1 16.7 %copy-start.3 = (bf16[384,2048]{1,0:T(8,128)(2,1)S(1)}, bf16[384,2048]{1,0:T(8,128)(2,1)}, u32[]{:S(2)}) copy-start(bf16[384,2048]{1,0:T(8,128)(2,1)} %copy-done.2) | copy-start | bytes 4718596
  149.1 16.6 %collective-permute-start.6 = (bf16[384,2048]{1,0:T(8,128)(2,1)}, bf16[384,2048]{1,0:T(8,128)(2,1)}, u32[]{:S(2)}, u32[]{:S(2)}) collective-permute-start(bf16[384,2048]{1,0:T(8,128)(2,1)} %get-tuple-element.52), channel_id=1, source_target_pairs={{0,32},{32,0},{64,96},{96,64},{128,160},{160,128},{192,224},{224,1... | collective-permute-start | bytes 4718600 | tf_op jit(solution)/shard_map/ppermute | solution.py:381
  161.6 27.6 %all-to-all-start.1 = ((bf16[8,48,1152]{2,1,0:T(8,128)(2,1)}), bf16[8,48,1152]{2,1,0:T(8,128)(2,1)S(1)}, u32[]{:S(2)}, u32[]{:S(2)}) async-start(bf16[8,48,1152]{2,1,0:T(8,128)(2,1)} %bitcast.28), calls=%async_computation.1 | async-start | bytes 1769472 | tf_op jit(solution)/shard_map/all_to_all | solution.py:268
  165.7 61.1 %reduce-scatter.2.cloned.1.call-start = ((), (), s32[]{:S(2)}) async-start(), calls=%async_computation.4 | async-start | bytes 1769472 | tf_op jit(solution)/shard_map/reduce_scatter | solution.py:383
  169.0 57.0 %copy-start.7 = (s32[32,8]{0,1:T(8,128)S(1)}, s32[32,8]{0,1:T(8,128)}, u32[]{:S(2)}) copy-start(s32[32,8]{0,1:T(8,128)} %param.8) | copy-start | bytes 3076
  169.4 43.5 %collective-permute-start.3 = (bf16[32,1024]{1,0:T(8,128)(2,1)S(1)}, bf16[32,1024]{1,0:T(8,128)(2,1)S(1)}, u32[]{:S(2)}, u32[]{:S(2)}) collective-permute-start(bf16[32,1024]{1,0:T(8,128)(2,1)S(1)} %get-tuple-element.44), channel_id=1, source_target_pairs={{0,8},{1,9},{2,10},{3,11},{4,12},{5,13},{6,14},{7,15},{8,16},{9,17... | collective-permute-start | bytes 196616 | tf_op jit(solution)/shard_map/ppermute | solution.py:425
  189.7 36.2 %collective-permute-start = (bf16[32,1152]{1,0:T(8,128)(2,1)S(1)}, bf16[32,1152]{1,0:T(8,128)(2,1)S(1)}, u32[]{:S(2)}, u32[]{:S(2)}) collective-permute-start(bf16[32,1152]{1,0:T(8,128)(2,1)S(1)} %get-tuple-element.40), channel_id=1, source_target_pairs={{0,8},{1,9},{2,10},{3,11},{4,12},{5,13},{6,14},{7,15},{8,16},{9,17... | collective-permute-start | bytes 221192 | tf_op jit(solution)/shard_map/ppermute | solution.py:425
  193.4 32.5 %collective-permute-start.1 = (bf16[32,1152]{1,0:T(8,128)(2,1)S(1)}, bf16[32,1152]{1,0:T(8,128)(2,1)S(1)}, u32[]{:S(2)}, u32[]{:S(2)}) collective-permute-start(bf16[32,1152]{1,0:T(8,128)(2,1)S(1)} %get-tuple-element.41), channel_id=1, source_target_pairs={{0,16},{1,17},{2,18},{3,19},{4,20},{5,21},{6,22},{7,23},{8,24},{9,... | collective-permute-start | bytes 221192 | tf_op jit(solution)/shard_map/ppermute | solution.py:425
  203.6 22.3 %collective-permute-start.2 = (bf16[32,1152]{1,0:T(8,128)(2,1)S(1)}, bf16[32,1152]{1,0:T(8,128)(2,1)S(1)}, u32[]{:S(2)}, u32[]{:S(2)}) collective-permute-start(bf16[32,1152]{1,0:T(8,128)(2,1)S(1)} %get-tuple-element.42), channel_id=1, source_target_pairs={{0,24},{1,25},{2,26},{3,27},{4,28},{5,29},{6,30},{7,31},{8,0},{9,1... | collective-permute-start | bytes 221192 | tf_op jit(solution)/shard_map/ppermute | solution.py:425
  207.6 14.3 %collective-permute-start.4 = (bf16[32,1024]{1,0:T(8,128)(2,1)S(1)}, bf16[32,1024]{1,0:T(8,128)(2,1)S(1)}, u32[]{:S(2)}, u32[]{:S(2)}) collective-permute-start(bf16[32,1024]{1,0:T(8,128)(2,1)S(1)} %get-tuple-element.45), channel_id=1, source_target_pairs={{0,16},{1,17},{2,18},{3,19},{4,20},{5,21},{6,22},{7,23},{8,24},{9,... | collective-permute-start | bytes 196616 | tf_op jit(solution)/shard_map/ppermute | solution.py:425
  212.9 13.0 %collective-permute-start.5 = (bf16[32,1024]{1,0:T(8,128)(2,1)S(1)}, bf16[32,1024]{1,0:T(8,128)(2,1)S(1)}, u32[]{:S(2)}, u32[]{:S(2)}) collective-permute-start(bf16[32,1024]{1,0:T(8,128)(2,1)S(1)} %get-tuple-element.46), channel_id=1, source_target_pairs={{0,24},{1,25},{2,26},{3,27},{4,28},{5,29},{6,30},{7,31},{8,0},{9,1... | collective-permute-start | bytes 196616 | tf_op jit(solution)/shard_map/ppermute | solution.py:425
Sparse Core Ops, SparseCore 0:
  10.1 73.4 all-gather.4
  86.3 44.3 all-gather.6
  170.0 42.9 reduce-scatter.1

commit v4 on v2

--- a/solution.py
+++ b/solution.py
@@ -9,6 +9,7 @@
 
 BF16, F32 = jnp.bfloat16, jnp.float32
 META = 128
+TILE = 512
 STRIDE = 4
 
 
@@ -32,23 +33,28 @@
     tok, width = rows_ref.shape
     topk = ids_ref.shape[0]
     hidden = gate_ref.shape[1]
-    part = 2 * hidden * META // width
+    down_rows = down_ref.shape[0]
     copies = [
         pltpu.make_async_copy(gate_ref, gate_buf, sems.at[0]),
         pltpu.make_async_copy(up_ref, up_buf, sems.at[1]),
-        pltpu.make_async_copy(down_ref, pack_ref.at[pl.ds(part, down_ref.shape[0]), :], sems.at[2]),
+        pltpu.make_async_copy(down_ref, pack_ref.at[pl.ds(0, down_rows), :], sems.at[2]),
         pltpu.make_async_copy(ids_ref, ids_buf, sems.at[3]),
         pltpu.make_async_copy(weight_ref, weight_buf, sems.at[4]),
         pltpu.make_async_copy(rows_ref, tok_ref.at[:, pl.ds(0, width)], sems.at[5]),
     ]
     for copy in copies:
         copy.start()
-    for at, buf in enumerate((gate_buf, up_buf)):
-        copies[at].wait()
-        turned = buf[...].astype(F32).T.astype(BF16)
-        for g in range(hidden // part):
-            lane = (at * (hidden // part) + g) * META
-            pack_ref[0:part, lane : lane + META] = turned[g * part : (g + 1) * part]
+    copies[0].wait()
+    copies[1].wait()
+    piece = TILE // 2
+    for i in range(gate_ref.shape[0] // 16):
+        for p in range(2 * hidden // piece):
+            n = i * (2 * hidden // TILE) + p // 2
+            row = down_rows + n // (width // TILE) * 16
+            lane = n % (width // TILE) * TILE + p % 2 * piece
+            buf = gate_buf if p * piece < hidden else up_buf
+            src = p * piece % hidden
+            pack_ref[row : row + 16, lane : lane + piece] = buf[i * 16 : i * 16 + 16, src : src + piece]
     copies[3].wait()
     copies[4].wait()
     meta = jnp.concatenate([ids_buf[...].astype(F32), weight_buf[...].astype(F32)], axis=0)
@@ -134,26 +140,54 @@
             ).astype(BF16)
 
 
+def fetch(pack_ref, base, wide_buf, sems, first):
+    _, rows, both = wide_buf.shape
+    across, per = both // TILE, pack_ref.shape[2] // TILE
+    copies = []
+    for i in range(rows // 16):
+        for j in range(across):
+            n = i * across + j
+            copies.append(
+                pltpu.make_async_copy(
+                    pack_ref.at[:, pl.ds(base + n // per * 16, 16), pl.ds(n % per * TILE, TILE)],
+                    wide_buf.at[:, pl.ds(i * 16, 16), pl.ds(j * TILE, TILE)],
+                    sems.at[first + n],
+                )
+            )
+    for copy in copies:
+        copy.start()
+    return copies
+
+
+def multiply(both_ref, wide_buf, out_buf, out_ref, sems, backs):
+    columns = 256
+    devices, rows, both = wide_buf.shape
+    group = columns // rows
+    for n in range(devices // group):
+        at = n * columns
+        out_buf[:, at : at + columns] = lax.dot_general(
+            both_ref[...],
+            wide_buf[n * group : (n + 1) * group].reshape(columns, both),
+            (((1,), (1,)), ((), ())),
+            preferred_element_type=F32,
+        ).astype(BF16)
+        part = pl.ds(at, columns)
+        backs.append(pltpu.make_async_copy(out_buf.at[:, part], out_ref.at[:, part], sems.at[n]))
+        backs[-1].start()
+    for copy in backs:
+        copy.wait()
+
+
 def mid_kernel(
     mine_ref, got_ref, hid_ref, slope_ref, silu_ref, pack_ref, out_ref,
-    out_buf, both_buf, down_buf, pack_buf, wide_buf, in_sems, out_sems,
+    out_buf, both_ref, down_buf, wide_buf, in_sems, out_sems,
 ):
     width = got_ref.shape[1] - META
     hidden = hid_ref.shape[1]
-    pairs, pair, part, _ = pack_buf.shape
     down_rows = down_buf.shape[1]
-    down_copy = pltpu.make_async_copy(
-        pack_ref.at[:, pl.ds(part, down_rows), :], down_buf, in_sems.at[pairs]
-    )
+    down_copy = pltpu.make_async_copy(pack_ref.at[:, pl.ds(0, down_rows), :], down_buf, in_sems.at[0])
     down_copy.start()
-    copies = [
-        pltpu.make_async_copy(
-            pack_ref.at[pl.ds(p * pair, pair), pl.ds(0, part), :], pack_buf.at[p], in_sems.at[p]
-        )
-        for p in range(pairs)
-    ]
-    for copy in copies:
-        copy.start()
+    copies = fetch(pack_ref, down_rows, wide_buf, in_sems, 1)
     w = slot_weight(got_ref[:, width:], mine_ref[0])
     down_copy.wait()
     q = lax.dot_general(
@@ -164,43 +198,44 @@
     )
     route = jnp.sum(q * hid_ref[...].astype(F32), axis=1, keepdims=True)
     grad = w * q
-    both_buf[:, :hidden] = (grad * slope_ref[...]).astype(BF16)
-    both_buf[:, hidden:] = (grad * silu_ref[...]).astype(BF16)
+    both_ref[:, :hidden] = (grad * slope_ref[...]).astype(BF16)
+    both_ref[:, hidden:] = (grad * silu_ref[...]).astype(BF16)
     lane = lax.broadcasted_iota(jnp.int32, (got_ref.shape[0], META), 1)
     out_buf[:, width:] = jnp.where(lane == mine_ref[0], route, 0.0).astype(BF16)
-    backs = [pltpu.make_async_copy(out_buf.at[:, pl.ds(width, META)], out_ref.at[:, pl.ds(width, META)], out_sems.at[pairs])]
+    extra = pl.ds(width, META)
+    last = out_sems.shape[0] - 1
+    backs = [pltpu.make_async_copy(out_buf.at[:, extra], out_ref.at[:, extra], out_sems.at[last])]
     backs[0].start()
-    for p in range(pairs):
-        copies[p].wait()
-        for b in range(pair):
-            for g in range(2 * hidden // part):
-                wide_buf[p % 2, g * part : (g + 1) * part, b * META : (b + 1) * META] = pack_buf[
-                    p, b, :, g * META : (g + 1) * META
-                ]
-        at = p * pair * META
-        out_buf[:, at : at + pair * META] = jnp.dot(
-            both_buf[...], wide_buf[p % 2], preferred_element_type=F32
-        ).astype(BF16)
-        columns = pl.ds(at, pair * META)
-        backs.append(pltpu.make_async_copy(out_buf.at[:, columns], out_ref.at[:, columns], out_sems.at[p]))
-        backs[-1].start()
-    for copy in backs:
+    for copy in copies:
         copy.wait()
-
-
-def combine_kernel(place_ref, select_ref, back_ref, *refs):
-    outs, total_buf = refs[:-1], refs[-1]
-    tok = outs[0].shape[0]
+    multiply(both_ref, wide_buf, out_buf, out_ref, out_sems, backs)
+
+
+def combine_kernel(place_ref, select_ref, back_ref, own_ref, next_ref, left_ref, right_ref, before_ref, total_buf):
+    tok = own_ref.shape[0]
+    cut = left_ref.shape[1]
     total_buf[...] = lax.dot_general(
         select_ref[...], back_ref[...], (((0,), (0,)), ((), ())), preferred_element_type=F32
     )
-    for m, ref in enumerate(outs):
-        begin = pl.multiple_of(((place_ref[0] + m) % STRIDE) * tok, tok)
-        ref[...] = total_buf[pl.ds(begin, tok), :].astype(ref.dtype)
+
+    def rows(m):
+        return pl.ds(pl.multiple_of(((place_ref[0] + m) % STRIDE) * tok, tok), tok)
+
+    own_ref[...] = total_buf[rows(0), :]
+    next_ref[...] = total_buf[rows(1), :]
+    before_ref[...] = total_buf[rows(3), :]
+    left_ref[...] = total_buf[rows(2), 0:cut].astype(BF16)
+    right_ref[...] = total_buf[rows(2), cut:].astype(BF16)
+
+
+def pass_kernel(base, part_ref, more_ref, out_ref):
+    size = more_ref.shape[1]
+    out_ref[...] = part_ref[...].astype(BF16)
+    out_ref[:, base : base + size] = (part_ref[:, base : base + size] + more_ref[...].astype(F32)).astype(BF16)
 
 
 def last_kernel(ids_ref, *refs):
-    parts, (tok_ref, route_ref) = refs[:STRIDE], refs[STRIDE:]
+    parts, (tok_ref, route_ref) = refs[:-2], refs[-2:]
     tok, width = tok_ref.shape
     total = parts[0][...]
     for ref in parts[1:]:
@@ -224,6 +259,10 @@
     return pl.BlockSpec(memory_space=memory)
 
 
+def exchange(value, axes, groups):
+    return lax.all_to_all(value, axes, 0, 0, axis_index_groups=groups, tiled=True)
+
+
 def per_device(n_dp, n_expert, grad_out, expert_ids, route_weights, saved_pre, gate_weight, up_weight, down_weight):
     tok, width = grad_out.shape
     pre = saved_pre[0, 0]
@@ -235,7 +274,6 @@
     dests = slots // (cap * STRIDE)
     per = STRIDE * cap
     down_rows = down_weight.shape[1]
-    part = both * META // width
     axes = ("dp", "expert")
 
     apart = [
@@ -262,19 +300,21 @@
     ) % 2
     mine = jnp.stack([me, core]).astype(jnp.int32)
 
+    wide = gate_weight.shape[1]
+    part = wide * both // width
     rows, pack = pl.pallas_call(
         prep_kernel,
-        out_shape=(shape((tok, full)), shape((part + down_rows, width))),
+        out_shape=(shape((tok, full)), shape((down_rows + part, width))),
         in_specs=[whole(pltpu.HBM)] * 6,
-        out_specs=(whole(), whole()),
+        out_specs=(whole(),) * 2,
         scratch_shapes=[
             pltpu.VMEM((expert_ids.shape[1], tok), jnp.int32),
             pltpu.VMEM((expert_ids.shape[1], tok), BF16),
-            pltpu.VMEM((META, hidden), BF16),
-            pltpu.VMEM((META, hidden), BF16),
+            pltpu.VMEM((wide, hidden), BF16),
+            pltpu.VMEM((wide, hidden), BF16),
             pltpu.SemaphoreType.DMA((6,)),
         ],
-        compiler_params=params(12),
+        compiler_params=params(60),
         name="prep",
     )(grad_out, expert_ids.T, route_weights.T, gate_weight[0], up_weight[0], down_weight[0])
     packs = lax.all_gather(pack, "dp", axis=0, tiled=False)
@@ -287,7 +327,7 @@
         compiler_params=params(16),
         name="select",
     )(members, blocks)
-    got = lax.all_to_all(send, axes, 0, 0, axis_index_groups=near, tiled=True).reshape(slots, full)
+    got = exchange(send, axes, near).reshape(slots, full)
     hid, turned, slope, silu = pl.pallas_call(
         functools.partial(act_kernel, cap, down_rows),
         out_shape=(
@@ -321,7 +361,8 @@
         tiled=True,
         axis_index_groups=[list(range(c, n_dp, 2)) for c in range(2)],
     )
-    pair = 2
+    columns = 256
+    pieces = wide // 16 * (both // TILE)
     back = pl.pallas_call(
         mid_kernel,
         out_shape=shape((slots, full)),
@@ -331,40 +372,52 @@
             pltpu.VMEM((slots, full), BF16),
             pltpu.VMEM((slots, both), BF16),
             pltpu.VMEM((n_dp, down_rows, width), BF16),
-            pltpu.VMEM((n_dp // pair, pair, part, width), BF16),
-            pltpu.VMEM((2, both, pair * META), BF16),
-            pltpu.SemaphoreType.DMA((n_dp // pair + 1,)),
-            pltpu.SemaphoreType.DMA((n_dp // pair + 1,)),
+            pltpu.VMEM((n_dp, wide, both), BF16),
+            pltpu.SemaphoreType.DMA((pieces + 1,)),
+            pltpu.SemaphoreType.DMA((width // columns + 1,)),
         ],
-        compiler_params=params(36),
-        cost_estimate=pl.CostEstimate(flops=6 * slots * hidden * width, bytes_accessed=2 * 3 * hidden * width, transcendentals=0),
+        compiler_params=params(54),
+        cost_estimate=pl.CostEstimate(flops=6 * slots * hidden * width, bytes_accessed=6 * hidden * width, transcendentals=0),
         name="mid",
     )(mine, got, hid, slope, silu, packs)
-    back = lax.all_to_all(
-        back.reshape(dests, per, full), axes, 0, 0, axis_index_groups=near, tiled=True
-    ).reshape(slots, full)
+    back = exchange(back.reshape(dests, per, full), axes, near).reshape(slots, full)
     place = (me // 2 // STRIDE).reshape(1).astype(jnp.int32)
-    own, *sums = pl.pallas_call(
+    cut = (full // META + 1) // 2 * META
+    own, after, left, right, before = pl.pallas_call(
         combine_kernel,
-        out_shape=(shape((tok, full), F32),) + (shape((tok, full)),) * (STRIDE - 1),
+        out_shape=(
+            shape((tok, full), F32),
+            shape((tok, full), F32),
+            shape((tok, cut)),
+            shape((tok, full - cut)),
+            shape((tok, full), F32),
+        ),
         in_specs=[whole(pltpu.SMEM), whole(), whole()],
-        out_specs=(whole(),) * STRIDE,
+        out_specs=(whole(),) * 5,
         scratch_shapes=[pltpu.VMEM((STRIDE * tok, full), F32)],
         compiler_params=params(12),
         name="combine",
     )(place, select, back)
-    parts = [own] + [
-        lax.ppermute(
-            value,
-            "expert",
-            [(e, ((e // 2 + STRIDE * (m + 1)) % n_z) * 2 + e % 2) for e in range(n_expert)],
-        )
-        for m, value in enumerate(sums)
-    ]
+
+    def hop(value, step):
+        perm = [(e, ((e // 2 + step) % n_z) * 2 + e % 2) for e in range(n_expert)]
+        return lax.ppermute(value, "expert", perm)
+
+    parts = [own]
+    for name, part, piece, base, step in (("up", after, left, 0, STRIDE), ("down", before, right, cut, -STRIDE)):
+        out = pl.pallas_call(
+            functools.partial(pass_kernel, base),
+            out_shape=shape((tok, full)),
+            in_specs=[whole(), whole()],
+            out_specs=whole(),
+            compiler_params=params(8),
+            name="pass_" + name,
+        )(part, hop(piece, step))
+        parts.append(hop(out, step))
     token_grad, route_grad = pl.pallas_call(
         last_kernel,
         out_shape=(shape((tok, width)), shape(expert_ids.shape[::-1])),
-        in_specs=[whole()] * (1 + STRIDE),
+        in_specs=[whole()] * (1 + len(parts)),
         out_specs=(whole(), whole()),
         compiler_params=params(8),
         name="last",

time: 207 us -> 197 us (0.952)
  local copies, waits for them, and re-layouts: 14.3 us -> 2.87 us
    unnamed x26 -> x14, local copies, waits for them, and re-layouts: 14.3 us -> 2.87 us
    ppermute x3 -> x4, waiting for transfers between devices: 20.2 us -> 18.2 us  [hop(): return lax.ppermute(value, 'expert', perm)]
    ppermute x3 -> x4, starting transfers between devices: 17.1 us -> 18.5 us  [hop(): return lax.ppermute(value, 'expert', perm)]
  transfers between devices with their start and end apart: 8 -> 9, of which waited for: 7 -> 7; matrix products, arithmetic and copies ran while one was open for 1% -> 1% of each run, Pallas kernels for 4% -> 4%
where the time goes in v4:
time: 197 us; the launch traced here: 196 us
  waiting for transfers between devices  89 us (45%)
  starting transfers between devices  33.7 us (17%)
  blocking collectives  32.6 us (17%)
  Pallas kernels  20.6 us (10%)
  between operations  15.7 us (8%)
  local copies, waits for them, and re-layouts  2.87 us (1%)
    all_to_all x2, waiting for transfers between devices, exchange(): lax.all_to_all(value, axes, 0, 0, axis_index_groups=groups, tiled=True)  59.8 us
    all_gather x1, blocking collectives, per_device(): lax.all_gather(rows, axes, axis=0, tiled=True, axis_index_groups=apart)  32.6 us
    ppermute x4, starting transfers between devices, hop(): return lax.ppermute(value, 'expert', perm)  18.5 us
    ppermute x4, waiting for transfers between devices, hop(): return lax.ppermute(value, 'expert', perm)  18.2 us
    all_to_all x2, starting transfers between devices, exchange(): lax.all_to_all(value, axes, 0, 0, axis_index_groups=groups, tiled=True)  13.3 us
    pallas_call x1, Pallas kernels, per_device(): pl.pallas_call(mid_kernel, out_shape=shape((slots, full)), in_specs=[whol...  10.6 us
    all_gather x1, waiting for transfers between devices, per_device(): packs = lax.all_gather(pack, 'dp', axis=0, tiled=False)  6.91 us
  transfers between devices with their start and end apart: 9, of which 7 were waited for; matrix products, arithmetic and copies ran while one was open for 1% of the time, Pallas kernels for 4%

profile of v4, /device:TPU:1, one launch (start us, length us, event | category | flops | bytes accessed | tf_op | source)
XLA Modules:
  0.0 196.3 jit_solution(13984705294655191109)
XLA Ops:
  8.0 0.0 all-gather.3.cloned.1.call-start
  8.0 2.1 %prep.1 = (bf16[32,2176]{1,0:T(8,128)(2,1)}, bf16[144,2048]{1,0:T(8,128)(2,1)}) custom-call(bf16[32,2048]{1,0:T(8,128)(2,1)} %rows_ref.1, s32[8,32]{1,0:T(8,128)} %bitcast.18, bf16[8,32]{1,0:T(8,128)(2,1)} %bitcast.26, bf16[128,768]{1,0:T(8,128)(2,1)} %bitcast.23, bf16[128,768]{1,0:T(8,128)(2,1)} %bitcast.24, bf16[48,2048]{1,0:T(8,128)(2,1)} %bitcast.25), custom_call_target="tpu_custom_call" | custom-call | tf_op jit(solution)/shard_map/prep/pallas_call | solution.py:305
  10.2 0.0 all-gather.3.cloned.1.call-update
  10.3 32.6 %all_gather.9.tok_ref = bf16[128,2176]{1,0:T(8,128)(2,1)S(1)} all-gather(bf16[32,2176]{1,0:T(8,128)(2,1)} %get-tuple-element.22), channel_id=1, replica_groups={{0,8,16,24},{1,9,17,25},{2,10,18,26},{3,11,19,27},{4,12,20,28},{5,13,21..., dimensions={0}, use_global_device_ids=true | all-gather | bytes 696320 | tf_op jit(solution)/shard_map/all_gather | solution.py:321
  42.9 2.7 %select.27 = (bf16[8,48,2176]{2,1,0:T(8,128)(2,1)}, bf16[384,128]{1,0:T(8,128)(2,1)S(1)}) custom-call(s32[8]{0:T(128)S(1)} %fusion.mine_ref, bf16[128,2176]{1,0:T(8,128)(2,1)S(1)} %all_gather.9.tok_ref), custom_call_target="tpu_custom_call" | custom-call | tf_op jit(solution)/shard_map/select/pallas_call | solution.py:322
  45.6 5.3 %all-to-all-start = ((bf16[8,48,2176]{2,1,0:T(8,128)(2,1)}), bf16[8,48,2176]{2,1,0:T(8,128)(2,1)S(1)}, u32[]{:S(2)}, u32[]{:S(2)}) async-start(bf16[8,48,2176]{2,1,0:T(8,128)(2,1)} %get-tuple-element.24), calls=%async_computation | async-start | bytes 3342336 | tf_op jit(solution)/shard_map/all_to_all | solution.py:263
  50.9 1.2 act.1
  52.2 1.0 copy-done.1
  53.2 1.0 copy-done.2
  54.2 0.8 copy-done.3
  55.0 0.1 pad_add_fusion.mine_ref
  55.1 27.5 %all-to-all-done = bf16[8,48,2176]{2,1,0:T(8,128)(2,1)S(1)} async-done(((bf16[8,48,2176]{2,1,0:T(8,128)(2,1)}), bf16[8,48,2176]{2,1,0:T(8,128)(2,1)S(1)}, u32[]{:S(2)}, u32[]{:S(2)}) %all-to-all-start) | async-done | bytes 1671200 | tf_op jit(solution)/shard_map/all_to_all | solution.py:263
  82.6 2.5 %down.1 = (bf16[384,2048]{1,0:T(8,128)(2,1)S(1)}, bf16[384,2048]{1,0:T(8,128)(2,1)S(1)}) custom-call(s32[2]{0:T(128)S(1)} %pad_add_fusion.mine_ref, bf16[384,2176]{1,0:T(8,128)(2,1)S(1)} %bitcast.15, bf16[768,384]{1,0:T(8,128)(2,1)S(1)} %get-tuple-element.25.turned_ref), custom_call_target="tpu_custom_call" | custom-call | flops 1207959552 | bytes 4718592 | tf_op jit(solution)/shard_map/down/pallas_call | solution.py:345
  85.1 1.9 collective-permute-start
  87.0 3.5 %collective-permute-done = bf16[384,2048]{1,0:T(8,128)(2,1)S(1)} collective-permute-done((bf16[384,2048]{1,0:T(8,128)(2,1)S(1)}, bf16[384,2048]{1,0:T(8,128)(2,1)S(1)}, u32[]{:S(2)}, u32[]{:S(2)}) %collective-permute-start) | collective-permute-done | bytes 1572896 | tf_op jit(solution)/shard_map/ppermute | solution.py:354
  90.6 1.8 add_convert_fusion
  92.3 6.9 %all-gather.3.cloned.1.call-done = bf16[2304,2048]{1,0:T(8,128)(2,1)} async-done(((bf16[144,2048]{1,0:T(8,128)(2,1)}), bf16[2304,2048]{1,0:T(8,128)(2,1)}) %all-gather.3.cloned.1.call-update) | async-done | bytes 9437200 | tf_op jit(solution)/shard_map/all_gather | solution.py:320
  99.2 10.6 %mid.1 = bf16[384,2176]{1,0:T(8,128)(2,1)} custom-call(s32[2]{0:T(128)} %copy-done.5, bf16[384,2176]{1,0:T(8,128)(2,1)} %bitcast.16, bf16[384,768]{1,0:T(8,128)(2,1)} %copy-done.3, f32[384,768]{1,0:T(8,128)} %copy-done.1, f32[384,768]{1,0:T(8,128)} %copy-done.2, bf16[16,144,2048]{2,1,0:T(8,128)(2,1)} %bitcast.21), custom_call_target="tpu_custom_call" | custom-call | flops 3623878656 | bytes 9437184 | tf_op jit(solution)/shard_map/mid/pallas_call | solution.py:366
  109.8 8.0 %all-to-all-start.1 = ((bf16[8,48,2176]{2,1,0:T(8,128)(2,1)}), bf16[8,48,2176]{2,1,0:T(8,128)(2,1)S(1)}, u32[]{:S(2)}, u32[]{:S(2)}) async-start(bf16[8,48,2176]{2,1,0:T(8,128)(2,1)} %bitcast.22), calls=%async_computation.1 | async-start | bytes 3342336 | tf_op jit(solution)/shard_map/all_to_all | solution.py:263
  117.8 0.0 reduce-scatter.2.cloned.1.call-start
  117.8 0.5 reduce-scatter.2.cloned.1.call-update
  118.4 0.0 copy-start.4
  118.4 32.3 %all-to-all-done.1 = bf16[8,48,2176]{2,1,0:T(8,128)(2,1)S(1)} async-done(((bf16[8,48,2176]{2,1,0:T(8,128)(2,1)}), bf16[8,48,2176]{2,1,0:T(8,128)(2,1)S(1)}, u32[]{:S(2)}, u32[]{:S(2)}) %all-to-all-start.1) | async-done | bytes 1671200 | tf_op jit(solution)/shard_map/all_to_all | solution.py:263
  150.7 0.6 combine.1
  151.3 4.2 %collective-permute-start.1 = (bf16[32,1152]{1,0:T(8,128)(2,1)S(1)}, bf16[32,1152]{1,0:T(8,128)(2,1)S(1)}, u32[]{:S(2)}, u32[]{:S(2)}) collective-permute-start(bf16[32,1152]{1,0:T(8,128)(2,1)S(1)} %get-tuple-element.35), channel_id=1, source_target_pairs={{0,8},{1,9},{2,10},{3,11},{4,12},{5,13},{6,14},{7,15},{8,16},{9,17... | collective-permute-start | bytes 221192 | tf_op jit(solution)/shard_map/ppermute | solution.py:404
  155.5 5.0 %collective-permute-start.3 = (bf16[32,1024]{1,0:T(8,128)(2,1)S(1)}, bf16[32,1024]{1,0:T(8,128)(2,1)S(1)}, u32[]{:S(2)}, u32[]{:S(2)}) collective-permute-start(bf16[32,1024]{1,0:T(8,128)(2,1)S(1)} %get-tuple-element.37), channel_id=1, source_target_pairs={{0,24},{1,25},{2,26},{3,27},{4,28},{5,29},{6,30},{7,31},{8,0},{9,1... | collective-permute-start | bytes 196616 | tf_op jit(solution)/shard_map/ppermute | solution.py:404
  160.5 4.4 %collective-permute-done.3.more_ref = bf16[32,1024]{1,0:T(8,128)(2,1)S(1)} collective-permute-done((bf16[32,1024]{1,0:T(8,128)(2,1)S(1)}, bf16[32,1024]{1,0:T(8,128)(2,1)S(1)}, u32[]{:S(2)}, u32[]{:S(2)}) %collective-permute-start.3) | collective-permute-done | bytes 65568 | tf_op jit(solution)/shard_map/ppermute | solution.py:404
  164.9 7.4 %collective-permute-start.4 = (bf16[32,2176]{1,0:T(8,128)(2,1)S(1)}, bf16[32,2176]{1,0:T(8,128)(2,1)S(1)}, u32[]{:S(2)}, u32[]{:S(2)}) collective-permute-start(bf16[32,2176]{1,0:T(8,128)(2,1)S(1)} %pass_down.1), channel_id=1, source_target_pairs={{0,24},{1,25},{2,26},{3,27},{4,28},{5,29},{6,30},{7,31},{8,0},{9,1... | collective-permute-start | bytes 417800 | tf_op jit(solution)/shard_map/ppermute | solution.py:404
  172.3 1.9 collective-permute-start.2
  174.2 5.0 %collective-permute-done.4.refs_2_ = bf16[32,2176]{1,0:T(8,128)(2,1)S(1)} collective-permute-done((bf16[32,2176]{1,0:T(8,128)(2,1)S(1)}, bf16[32,2176]{1,0:T(8,128)(2,1)S(1)}, u32[]{:S(2)}, u32[]{:S(2)}) %collective-permute-start.4) | collective-permute-done | bytes 139296 | tf_op jit(solution)/shard_map/ppermute | solution.py:404
  179.3 8.7 %collective-permute-done.2.refs_1_ = bf16[32,2176]{1,0:T(8,128)(2,1)S(1)} collective-permute-done((bf16[32,2176]{1,0:T(8,128)(2,1)S(1)}, bf16[32,2176]{1,0:T(8,128)(2,1)S(1)}, u32[]{:S(2)}, u32[]{:S(2)}) %collective-permute-start.2) | collective-permute-done | bytes 139296 | tf_op jit(solution)/shard_map/ppermute | solution.py:404
  188.0 0.9 last.1
  (15 shorter events, 0.1 us)
Async XLA Ops:
  8.0 91.2 %all-gather.3.cloned.1.call-start = ((), (), s32[]{:S(2)}) async-start(), calls=%async_computation.4 | async-start | bytes 10027008 | tf_op jit(solution)/shard_map/all_gather | solution.py:320
  45.6 5.3 %copy-start.6 = (bf16[1,1,384,1536]{3,2,1,0:T(8,128)(2,1)S(1)}, bf16[1,1,384,1536]{3,2,1,0:T(8,128)(2,1)}, u32[]{:S(2)}) copy-start(bf16[1,1,384,1536]{3,2,1,0:T(8,128)(2,1)} %param.10) | copy-start | bytes 3538948
  45.6 37.0 %all-to-all-start = ((bf16[8,48,2176]{2,1,0:T(8,128)(2,1)}), bf16[8,48,2176]{2,1,0:T(8,128)(2,1)S(1)}, u32[]{:S(2)}, u32[]{:S(2)}) async-start(bf16[8,48,2176]{2,1,0:T(8,128)(2,1)} %get-tuple-element.24), calls=%async_computation | async-start | bytes 3342336 | tf_op jit(solution)/shard_map/all_to_all | solution.py:263
  52.2 1.0 copy-start.1
  53.2 1.0 copy-start.2
  54.2 0.8 copy-start.3
  55.1 30.0 %copy-start.5 = (s32[2]{0:T(128)}, s32[2]{0:T(128)S(1)}, u32[]{:S(2)}) copy-start(s32[2]{0:T(128)S(1)} %pad_add_fusion.mine_ref) | copy-start | bytes 28
  82.6 2.5 %copy-start = (bf16[8,48,2176]{2,1,0:T(8,128)(2,1)}, bf16[8,48,2176]{2,1,0:T(8,128)(2,1)S(1)}, u32[]{:S(2)}) copy-start(bf16[8,48,2176]{2,1,0:T(8,128)(2,1)S(1)} %all-to-all-done) | copy-start | bytes 5013508
  85.1 5.5 %collective-permute-start = (bf16[384,2048]{1,0:T(8,128)(2,1)S(1)}, bf16[384,2048]{1,0:T(8,128)(2,1)S(1)}, u32[]{:S(2)}, u32[]{:S(2)}) collective-permute-start(bf16[384,2048]{1,0:T(8,128)(2,1)S(1)} %get-tuple-element.27), channel_id=1, source_target_pairs={{0,32},{32,0},{64,96},{96,64},{128,160},{160,128},{192,224},{224,1... | collective-permute-start | bytes 4718600 | tf_op jit(solution)/shard_map/ppermute | solution.py:354
  109.8 40.9 %all-to-all-start.1 = ((bf16[8,48,2176]{2,1,0:T(8,128)(2,1)}), bf16[8,48,2176]{2,1,0:T(8,128)(2,1)S(1)}, u32[]{:S(2)}, u32[]{:S(2)}) async-start(bf16[8,48,2176]{2,1,0:T(8,128)(2,1)} %bitcast.22), calls=%async_computation.1 | async-start | bytes 3342336 | tf_op jit(solution)/shard_map/all_to_all | solution.py:263
  117.8 71.1 %reduce-scatter.2.cloned.1.call-start = ((), (), s32[]{:S(2)}) async-start(), calls=%async_computation.3 | async-start | bytes 1769472 | tf_op jit(solution)/shard_map/reduce_scatter | solution.py:357
  118.4 69.7 %copy-start.4 = (s32[32,8]{0,1:T(8,128)S(1)}, s32[32,8]{0,1:T(8,128)}, u32[]{:S(2)}) copy-start(s32[32,8]{0,1:T(8,128)} %param.8) | copy-start | bytes 3076
  151.3 21.0 %collective-permute-start.1 = (bf16[32,1152]{1,0:T(8,128)(2,1)S(1)}, bf16[32,1152]{1,0:T(8,128)(2,1)S(1)}, u32[]{:S(2)}, u32[]{:S(2)}) collective-permute-start(bf16[32,1152]{1,0:T(8,128)(2,1)S(1)} %get-tuple-element.35), channel_id=1, source_target_pairs={{0,8},{1,9},{2,10},{3,11},{4,12},{5,13},{6,14},{7,15},{8,16},{9,17... | collective-permute-start | bytes 221192 | tf_op jit(solution)/shard_map/ppermute | solution.py:404
  155.5 9.4 %collective-permute-start.3 = (bf16[32,1024]{1,0:T(8,128)(2,1)S(1)}, bf16[32,1024]{1,0:T(8,128)(2,1)S(1)}, u32[]{:S(2)}, u32[]{:S(2)}) collective-permute-start(bf16[32,1024]{1,0:T(8,128)(2,1)S(1)} %get-tuple-element.37), channel_id=1, source_target_pairs={{0,24},{1,25},{2,26},{3,27},{4,28},{5,29},{6,30},{7,31},{8,0},{9,1... | collective-permute-start | bytes 196616 | tf_op jit(solution)/shard_map/ppermute | solution.py:404
  164.9 14.4 %collective-permute-start.4 = (bf16[32,2176]{1,0:T(8,128)(2,1)S(1)}, bf16[32,2176]{1,0:T(8,128)(2,1)S(1)}, u32[]{:S(2)}, u32[]{:S(2)}) collective-permute-start(bf16[32,2176]{1,0:T(8,128)(2,1)S(1)} %pass_down.1), channel_id=1, source_target_pairs={{0,24},{1,25},{2,26},{3,27},{4,28},{5,29},{6,30},{7,31},{8,0},{9,1... | collective-permute-start | bytes 417800 | tf_op jit(solution)/shard_map/ppermute | solution.py:404
  172.3 15.7 %collective-permute-start.2 = (bf16[32,2176]{1,0:T(8,128)(2,1)S(1)}, bf16[32,2176]{1,0:T(8,128)(2,1)S(1)}, u32[]{:S(2)}, u32[]{:S(2)}) collective-permute-start(bf16[32,2176]{1,0:T(8,128)(2,1)S(1)} %pass_up.1), channel_id=1, source_target_pairs={{0,8},{1,9},{2,10},{3,11},{4,12},{5,13},{6,14},{7,15},{8,16},{9,17... | collective-permute-start | bytes 417800 | tf_op jit(solution)/shard_map/ppermute | solution.py:404
Sparse Core Ops, SparseCore 0:
  11.0 88.2 all-gather.2
Sparse Core Ops, SparseCore 1:
  121.7 43.9 reduce-scatter.1

commit v5 on v3

--- a/solution.py
+++ b/solution.py
@@ -27,7 +27,7 @@
 
 
 def prep_kernel(
-    rows_ref, ids_ref, weight_ref, gate_ref, up_ref, down_ref, tok_ref, first_ref, second_ref,
+    rows_ref, ids_ref, weight_ref, gate_ref, up_ref, down_ref, tok_ref, pack_ref,
     ids_buf, weight_buf, gate_buf, up_buf, sems,
 ):
     tok, width = rows_ref.shape
@@ -37,7 +37,7 @@
     copies = [
         pltpu.make_async_copy(gate_ref, gate_buf, sems.at[0]),
         pltpu.make_async_copy(up_ref, up_buf, sems.at[1]),
-        pltpu.make_async_copy(down_ref, first_ref.at[pl.ds(0, down_rows), :], sems.at[2]),
+        pltpu.make_async_copy(down_ref, pack_ref.at[pl.ds(0, down_rows), :], sems.at[2]),
         pltpu.make_async_copy(ids_ref, ids_buf, sems.at[3]),
         pltpu.make_async_copy(weight_ref, weight_buf, sems.at[4]),
         pltpu.make_async_copy(rows_ref, tok_ref.at[:, pl.ds(0, width)], sems.at[5]),
@@ -47,17 +47,14 @@
     copies[0].wait()
     copies[1].wait()
     piece = TILE // 2
-    half = gate_ref.shape[0] // 2
-    for which, (ref, base) in enumerate(((first_ref, down_rows), (second_ref, 0))):
-        for i in range(half // 16):
-            for p in range(2 * hidden // piece):
-                n = i * (2 * hidden // TILE) + p // 2
-                row = base + n // (width // TILE) * 16
-                lane = n % (width // TILE) * TILE + p % 2 * piece
-                buf = gate_buf if p * piece < hidden else up_buf
-                src = p * piece % hidden
-                begin = which * half + i * 16
-                ref[row : row + 16, lane : lane + piece] = buf[begin : begin + 16, src : src + piece]
+    for i in range(gate_ref.shape[0] // 16):
+        for p in range(2 * hidden // piece):
+            n = i * (2 * hidden // TILE) + p // 2
+            row = down_rows + n // (width // TILE) * 16
+            lane = n % (width // TILE) * TILE + p % 2 * piece
+            buf = gate_buf if p * piece < hidden else up_buf
+            src = p * piece % hidden
+            pack_ref[row : row + 16, lane : lane + piece] = buf[i * 16 : i * 16 + 16, src : src + piece]
     copies[3].wait()
     copies[4].wait()
     meta = jnp.concatenate([ids_buf[...].astype(F32), weight_buf[...].astype(F32)], axis=0)
@@ -143,8 +140,8 @@
             ).astype(BF16)
 
 
-def fetch(pack_ref, base, wide_buf, sems, first):
-    _, rows, both = wide_buf.shape
+def fetch(pack_ref, begin, base, wide_buf, sems, first):
+    devices, rows, both = wide_buf.shape
     across, per = both // TILE, pack_ref.shape[2] // TILE
     copies = []
     for i in range(rows // 16):
@@ -152,7 +149,7 @@
             n = i * across + j
             copies.append(
                 pltpu.make_async_copy(
-                    pack_ref.at[:, pl.ds(base + n // per * 16, 16), pl.ds(n % per * TILE, TILE)],
+                    pack_ref.at[pl.ds(begin, devices), pl.ds(base + n // per * 16, 16), pl.ds(n % per * TILE, TILE)],
                     wide_buf.at[:, pl.ds(i * 16, 16), pl.ds(j * TILE, TILE)],
                     sems.at[first + n],
                 )
@@ -191,7 +188,7 @@
     half = out_buf.shape[1] - META
     down_copy = pltpu.make_async_copy(pack_ref.at[:, pl.ds(0, down_rows), :], down_buf, in_sems.at[0])
     down_copy.start()
-    copies = fetch(pack_ref, down_rows, wide_buf, in_sems, 1)
+    copies = fetch(pack_ref, 0, down_rows, wide_buf, in_sems, 1)
     w = slot_weight(got_ref[:, width:], mine_ref[0])
     down_copy.wait()
     q = lax.dot_general(
@@ -215,8 +212,9 @@
     multiply(both_ref, wide_buf, out_buf, out_ref, out_sems, backs)
 
 
-def second_kernel(both_ref, pack_ref, out_ref, out_buf, wide_buf, in_sems, out_sems):
-    for copy in fetch(pack_ref, 0, wide_buf, in_sems, 0):
+def second_kernel(down_rows, both_ref, pack_ref, out_ref, out_buf, wide_buf, in_sems, out_sems):
+    devices = wide_buf.shape[0]
+    for copy in fetch(pack_ref, pack_ref.shape[0] - devices, down_rows, wide_buf, in_sems, 0):
         copy.wait()
     multiply(both_ref, wide_buf, out_buf, out_ref, out_sems, [])
 
@@ -234,19 +232,16 @@
 
 def last_kernel(ids_ref, *refs):
     first, second, (tok_ref, route_ref) = refs[:STRIDE], refs[STRIDE : 2 * STRIDE], refs[2 * STRIDE :]
-    tok, width = tok_ref.shape
+    half = tok_ref.shape[1] // 2
     sums = []
     for parts in (first, second):
         total = parts[0][...]
         for ref in parts[1:]:
             total = total + ref[...].astype(F32)
         sums.append(total)
-    low = lax.broadcasted_iota(jnp.int32, (tok, META), 1) < META // 2
-    for j in range(width // META // 2):
-        a, b = (x[:, j * META : (j + 1) * META] for x in sums)
-        tok_ref[:, 2 * j * META : (2 * j + 1) * META] = jnp.where(low, a, pltpu.roll(b, META // 2, 1)).astype(BF16)
-        tok_ref[:, (2 * j + 1) * META : (2 * j + 2) * META] = jnp.where(low, pltpu.roll(a, META // 2, 1), b).astype(BF16)
-    route = turn(sums[0][:, width // 2 :])
+    tok_ref[:, :half] = sums[0][:, :half].astype(BF16)
+    tok_ref[:, half:] = sums[1].astype(BF16)
+    route = turn(sums[0][:, half:])
     ids = ids_ref[...]
     expert = lax.broadcasted_iota(jnp.int32, route.shape, 0)
     found = [
@@ -305,25 +300,24 @@
     ) % 2
     mine = jnp.stack([me, core]).astype(jnp.int32)
 
-    half_rows = gate_weight.shape[1] // 2
-    part = half_rows * both // width
-    rows, pack, pack_b = pl.pallas_call(
+    wide = gate_weight.shape[1]
+    part = wide * both // width
+    rows, pack = pl.pallas_call(
         prep_kernel,
-        out_shape=(shape((tok, full)), shape((down_rows + part, width)), shape((part, width))),
+        out_shape=(shape((tok, full)), shape((down_rows + part, width))),
         in_specs=[whole(pltpu.HBM)] * 6,
-        out_specs=(whole(),) * 3,
+        out_specs=(whole(),) * 2,
         scratch_shapes=[
             pltpu.VMEM((expert_ids.shape[1], tok), jnp.int32),
             pltpu.VMEM((expert_ids.shape[1], tok), BF16),
-            pltpu.VMEM((2 * half_rows, hidden), BF16),
-            pltpu.VMEM((2 * half_rows, hidden), BF16),
+            pltpu.VMEM((wide, hidden), BF16),
+            pltpu.VMEM((wide, hidden), BF16),
             pltpu.SemaphoreType.DMA((6,)),
         ],
         compiler_params=params(60),
         name="prep",
     )(grad_out, expert_ids.T, route_weights.T, gate_weight[0], up_weight[0], down_weight[0])
     packs = lax.all_gather(pack, "dp", axis=0, tiled=False)
-    packs_b = lax.all_gather(pack_b, "dp", axis=0, tiled=False)
     blocks = lax.all_gather(rows, axes, axis=0, tiled=True, axis_index_groups=apart)
     send, select = pl.pallas_call(
         functools.partial(select_kernel, cap),
@@ -349,26 +343,42 @@
         name="act",
     )(pre)
     columns = 256
-    pieces = half_rows // 16 * (both // TILE)
+    half = width // 2
+    pieces = wide // 16 * (both // TILE)
     back, grads = pl.pallas_call(
         first_kernel,
-        out_shape=(shape((slots, width // 2 + META)), shape((slots, both))),
+        out_shape=(shape((slots, half + META)), shape((slots, both))),
         in_specs=[whole(pltpu.SMEM)] + [whole()] * 4 + [whole(pltpu.HBM)],
         out_specs=(whole(pltpu.HBM), whole()),
         scratch_shapes=[
-            pltpu.VMEM((slots, width // 2 + META), BF16),
+            pltpu.VMEM((slots, half + META), BF16),
             pltpu.VMEM((n_dp, down_rows, width), BF16),
-            pltpu.VMEM((n_dp, half_rows, both), BF16),
+            pltpu.VMEM((n_dp // 2, wide, both), BF16),
             pltpu.SemaphoreType.DMA((pieces + 1,)),
-            pltpu.SemaphoreType.DMA((width // 2 // columns + 1,)),
+            pltpu.SemaphoreType.DMA((half // columns + 1,)),
         ],
         compiler_params=params(54),
         cost_estimate=pl.CostEstimate(flops=4 * slots * hidden * width, bytes_accessed=4 * hidden * width, transcendentals=0),
         name="first",
     )(mine, got, hid, slope, silu, packs)
     ret = exchange(back.reshape(dests, per, -1), axes, near).reshape(slots, -1)
-
-    got, back = lax.optimization_barrier((got, back))
+    back_b = pl.pallas_call(
+        functools.partial(second_kernel, down_rows),
+        out_shape=shape((slots, half)),
+        in_specs=[whole(), whole(pltpu.HBM)],
+        out_specs=whole(pltpu.HBM),
+        scratch_shapes=[
+            pltpu.VMEM((slots, half), BF16),
+            pltpu.VMEM((n_dp // 2, wide, both), BF16),
+            pltpu.SemaphoreType.DMA((pieces,)),
+            pltpu.SemaphoreType.DMA((half // columns,)),
+        ],
+        compiler_params=params(54),
+        cost_estimate=pl.CostEstimate(flops=2 * slots * hidden * width, bytes_accessed=2 * hidden * width, transcendentals=0),
+        name="second",
+    )(grads, packs)
+
+    got, back_b = lax.optimization_barrier((got, back_b))
     keep, give = pl.pallas_call(
         down_kernel,
         out_shape=(shape((hidden // 2, width)), shape((hidden // 2, width))),
@@ -380,6 +390,7 @@
     )(mine, got, turned)
     taken = lax.ppermute(give, "dp", [(d, d ^ 1) for d in range(n_dp)])
     chip_part = (keep.astype(F32) + taken.astype(F32)).astype(BF16)
+    ret, _ = lax.optimization_barrier((ret, chip_part))
     down_grad = lax.psum_scatter(
         chip_part,
         "dp",
@@ -387,24 +398,8 @@
         tiled=True,
         axis_index_groups=[list(range(c, n_dp, 2)) for c in range(2)],
     )
-
-    back_b = pl.pallas_call(
-        second_kernel,
-        out_shape=shape((slots, width // 2)),
-        in_specs=[whole(), whole(pltpu.HBM)],
-        out_specs=whole(pltpu.HBM),
-        scratch_shapes=[
-            pltpu.VMEM((slots, width // 2), BF16),
-            pltpu.VMEM((n_dp, half_rows, both), BF16),
-            pltpu.SemaphoreType.DMA((pieces,)),
-            pltpu.SemaphoreType.DMA((width // 2 // columns,)),
-        ],
-        compiler_params=params(56),
-        cost_estimate=pl.CostEstimate(flops=2 * slots * hidden * width, bytes_accessed=2 * hidden * width, transcendentals=0),
-        name="second",
-    )(grads, packs_b)
+    ret, back_b = lax.optimization_barrier((ret, back_b))
     ret_b = exchange(back_b.reshape(dests, per, -1), axes, near).reshape(slots, -1)
-    ret, back_b = lax.optimization_barrier((ret, back_b))
 
     place = (me // 2 // STRIDE).reshape(1).astype(jnp.int32)
     parts = []
@@ -426,7 +421,7 @@
     token_grad, route_grad = pl.pallas_call(
         last_kernel,
         out_shape=(shape((tok, width)), shape(expert_ids.shape[::-1])),
-        in_specs=[whole()] * (1 + 2 * STRIDE),
+        in_specs=[whole()] * (1 + len(parts)),
         out_specs=(whole(), whole()),
         compiler_params=params(8),
         name="last",

time: 235 us -> 202 us (0.86)
  waiting for transfers between devices: 97.3 us -> 63.3 us
  starting transfers between devices: 53.6 us -> 57 us
    all_gather x1 -> x0, waiting for transfers between devices: 36.8 us -> none  [per_device(): packs_b = lax.all_gather(pack_b, 'dp', axis=0, tiled=False)]
    all_gather x1, waiting for transfers between devices: 1.87 us -> 16.6 us  [per_device(): packs = lax.all_gather(pack, 'dp', axis=0, tiled=False)]
    all_to_all x3, waiting for transfers between devices: 51.8 us -> 37.8 us  [exchange(): lax.all_to_all(value, axes, 0, 0, axis_index_groups=groups, tiled=True)]
    ppermute x6, starting transfers between devices: 33.9 us -> 37.7 us  [per_device(): parts.append(lax.ppermute(one, 'expert', perm))]
    ppermute x1, waiting for transfers between devices: 0.01 us -> 3.38 us  [per_device(): taken = lax.ppermute(give, 'dp', [(d, d ^ 1) for d in range(n_dp)])]
    unnamed x24 -> x16, local copies, waits for them, and re-layouts: 4.91 us -> 2.95 us
  transfers between devices with their start and end apart: 13 -> 12, of which waited for: 7 -> 7; matrix products, arithmetic and copies ran while one was open for 2% -> 1% of each run, Pallas kernels for 8% -> 7%
where the time goes in v5:
time: 202 us; the launch traced here: 199 us
  waiting for transfers between devices  63.3 us (31%)
  starting transfers between devices  57 us (28%)
  blocking collectives  32.6 us (16%)
  Pallas kernels  26.3 us (13%)
  between operations  14.3 us (7%)
  local copies, waits for them, and re-layouts  2.95 us (1%)
  other arithmetic  2.4 us (1%)
    all_to_all x3, waiting for transfers between devices, exchange(): lax.all_to_all(value, axes, 0, 0, axis_index_groups=groups, tiled=True)  37.8 us
    ppermute x6, starting transfers between devices, per_device(): parts.append(lax.ppermute(one, 'expert', perm))  37.7 us
    all_gather x1, blocking collectives, per_device(): lax.all_gather(rows, axes, axis=0, tiled=True, axis_index_groups=apart)  32.6 us
    all_to_all x3, starting transfers between devices, exchange(): lax.all_to_all(value, axes, 0, 0, axis_index_groups=groups, tiled=True)  17.3 us
    all_gather x1, waiting for transfers between devices, per_device(): packs = lax.all_gather(pack, 'dp', axis=0, tiled=False)  16.6 us
    pallas_call x1, Pallas kernels, per_device(): pl.pallas_call(first_kernel, out_shape=(shape((slots, half + META)), shap...  10.3 us
    pallas_call x1, Pallas kernels, per_device(): pl.pallas_call(functools.partial(second_kernel, down_rows), out_shape=sha...  5.78 us
    ppermute x6, waiting for transfers between devices, per_device(): parts.append(lax.ppermute(one, 'expert', perm))  5.49 us
  transfers between devices with their start and end apart: 12, of which 7 were waited for; matrix products, arithmetic and copies ran while one was open for 1% of the time, Pallas kernels for 7%

profile of v5, /device:TPU:1, one launch (start us, length us, event | category | flops | bytes accessed | tf_op | source)
XLA Modules:
  0.0 199.0 jit_solution(2862727687389404331)
XLA Ops:
  7.2 2.1 %prep.1 = (bf16[32,2176]{1,0:T(8,128)(2,1)}, bf16[144,2048]{1,0:T(8,128)(2,1)}) custom-call(bf16[32,2048]{1,0:T(8,128)(2,1)} %rows_ref.1, s32[8,32]{1,0:T(8,128)} %bitcast.21, bf16[8,32]{1,0:T(8,128)(2,1)} %bitcast.30, bf16[128,768]{1,0:T(8,128)(2,1)} %bitcast.27, bf16[128,768]{1,0:T(8,128)(2,1)} %bitcast.28, bf16[48,2048]{1,0:T(8,128)(2,1)} %bitcast.29), custom_call_target="tpu_custom_call" | custom-call | tf_op jit(solution)/shard_map/prep/pallas_call | solution.py:305
  9.5 32.6 %all_gather.9.tok_ref = bf16[128,2176]{1,0:T(8,128)(2,1)S(1)} all-gather(bf16[32,2176]{1,0:T(8,128)(2,1)} %get-tuple-element.30), channel_id=1, replica_groups={{0,8,16,24},{1,9,17,25},{2,10,18,26},{3,11,19,27},{4,12,20,28},{5,13,21..., dimensions={0}, use_global_device_ids=true | all-gather | bytes 696320 | tf_op jit(solution)/shard_map/all_gather | solution.py:321
  42.1 2.7 %select.27 = (bf16[8,48,2176]{2,1,0:T(8,128)(2,1)}, bf16[384,128]{1,0:T(8,128)(2,1)S(1)}) custom-call(s32[8]{0:T(128)S(1)} %fusion.mine_ref, bf16[128,2176]{1,0:T(8,128)(2,1)S(1)} %all_gather.9.tok_ref), custom_call_target="tpu_custom_call" | custom-call | tf_op jit(solution)/shard_map/select/pallas_call | solution.py:322
  44.8 5.3 %all-to-all-start = ((bf16[8,48,2176]{2,1,0:T(8,128)(2,1)}), bf16[8,48,2176]{2,1,0:T(8,128)(2,1)S(1)}, u32[]{:S(2)}, u32[]{:S(2)}) async-start(bf16[8,48,2176]{2,1,0:T(8,128)(2,1)} %get-tuple-element.32), calls=%async_computation | async-start | bytes 3342336 | tf_op jit(solution)/shard_map/all_to_all | solution.py:263
  50.1 1.2 act.1
  51.4 1.0 copy-done.2
  52.4 1.1 copy-done.3
  53.5 0.8 copy-done.4
  54.3 0.6 pad_add_fusion.mine_ref
  54.9 26.9 %all-to-all-done = bf16[8,48,2176]{2,1,0:T(8,128)(2,1)S(1)} async-done(((bf16[8,48,2176]{2,1,0:T(8,128)(2,1)}), bf16[8,48,2176]{2,1,0:T(8,128)(2,1)S(1)}, u32[]{:S(2)}, u32[]{:S(2)}) %all-to-all-start) | async-done | bytes 1671200 | tf_op jit(solution)/shard_map/all_to_all | solution.py:263
  81.8 16.6 %all-gather.3.cloned.1.call-done = bf16[2304,2048]{1,0:T(8,128)(2,1)} async-done(((bf16[144,2048]{1,0:T(8,128)(2,1)}), bf16[2304,2048]{1,0:T(8,128)(2,1)}) %all-gather.3.cloned.1.call-update) | async-done | bytes 9437200 | tf_op jit(solution)/shard_map/all_gather | solution.py:320
  98.4 10.3 %first.1 = (bf16[384,1152]{1,0:T(8,128)(2,1)}, bf16[384,1536]{1,0:T(8,128)(2,1)}) custom-call(s32[2]{0:T(128)} %pad_add_fusion.mine_ref, bf16[384,2176]{1,0:T(8,128)(2,1)} %bitcast.17, bf16[384,768]{1,0:T(8,128)(2,1)} %copy-done.4, f32[384,768]{1,0:T(8,128)} %copy-done.2, f32[384,768]{1,0:T(8,128)} %copy-done.3, bf16[16,144,2048]{2,1,0:T(8,128)(2,1)} %bitcast.24), custom_call_target="tpu_custom_call" | custom-call | flops 2415919104 | bytes 6291456 | tf_op jit(solution)/shard_map/first/pallas_call | solution.py:348
  108.7 8.0 %all-to-all-start.1 = ((bf16[8,48,1152]{2,1,0:T(8,128)(2,1)}), bf16[8,48,1152]{2,1,0:T(8,128)(2,1)S(1)}, u32[]{:S(2)}, u32[]{:S(2)}) async-start(bf16[8,48,1152]{2,1,0:T(8,128)(2,1)} %bitcast.26), calls=%async_computation.1 | async-start | bytes 1769472 | tf_op jit(solution)/shard_map/all_to_all | solution.py:263
  116.8 5.8 %second.1 = bf16[384,1024]{1,0:T(8,128)(2,1)} custom-call(bf16[384,1536]{1,0:T(8,128)(2,1)} %get-tuple-element.38.both_ref, bf16[16,144,2048]{2,1,0:T(8,128)(2,1)} %bitcast.25), custom_call_target="tpu_custom_call" | custom-call | flops 1207959552 | bytes 3145728 | tf_op jit(solution)/shard_map/second/pallas_call | solution.py:365
  122.6 2.5 %down.1 = (bf16[384,2048]{1,0:T(8,128)(2,1)S(1)}, bf16[384,2048]{1,0:T(8,128)(2,1)S(1)}) custom-call(s32[2]{0:T(128)S(1)} %copy-done.6, bf16[384,2176]{1,0:T(8,128)(2,1)S(1)} %bitcast.18, bf16[768,384]{1,0:T(8,128)(2,1)S(1)} %get-tuple-element.40.turned_ref), custom_call_target="tpu_custom_call" | custom-call | flops 1207959552 | bytes 4718592 | tf_op jit(solution)/shard_map/down/pallas_call | solution.py:382
  125.1 1.9 collective-permute-start
  127.0 3.4 %collective-permute-done = bf16[384,2048]{1,0:T(8,128)(2,1)S(1)} collective-permute-done((bf16[384,2048]{1,0:T(8,128)(2,1)S(1)}, bf16[384,2048]{1,0:T(8,128)(2,1)S(1)}, u32[]{:S(2)}, u32[]{:S(2)}) %collective-permute-start) | collective-permute-done | bytes 1572896 | tf_op jit(solution)/shard_map/ppermute | solution.py:391
  130.4 1.8 add_convert_fusion
  132.2 3.4 %all-to-all-done.1 = bf16[8,48,1152]{2,1,0:T(8,128)(2,1)S(1)} async-done(((bf16[8,48,1152]{2,1,0:T(8,128)(2,1)}), bf16[8,48,1152]{2,1,0:T(8,128)(2,1)S(1)}, u32[]{:S(2)}, u32[]{:S(2)}) %all-to-all-start.1) | async-done | bytes 884768 | tf_op jit(solution)/shard_map/all_to_all | solution.py:263
  135.6 4.1 %all-to-all-start.2 = ((bf16[8,48,1024]{2,1,0:T(8,128)(2,1)}), bf16[8,48,1024]{2,1,0:T(8,128)(2,1)S(1)}, u32[]{:S(2)}, u32[]{:S(2)}) async-start(bf16[8,48,1024]{2,1,0:T(8,128)(2,1)} %bitcast.13), calls=%async_computation.2 | async-start | bytes 1572864 | tf_op jit(solution)/shard_map/all_to_all | solution.py:263
  139.7 0.4 sum_first.1
  140.1 4.2 %collective-permute-start.1 = (bf16[32,1152]{1,0:T(8,128)(2,1)S(1)}, bf16[32,1152]{1,0:T(8,128)(2,1)S(1)}, u32[]{:S(2)}, u32[]{:S(2)}) collective-permute-start(bf16[32,1152]{1,0:T(8,128)(2,1)S(1)} %get-tuple-element.47), channel_id=1, source_target_pairs={{0,8},{1,9},{2,10},{3,11},{4,12},{5,13},{6,14},{7,15},{8,16},{9,17... | collective-permute-start | bytes 221192 | tf_op jit(solution)/shard_map/ppermute | solution.py:420
  144.3 9.4 %collective-permute-start.2 = (bf16[32,1152]{1,0:T(8,128)(2,1)S(1)}, bf16[32,1152]{1,0:T(8,128)(2,1)S(1)}, u32[]{:S(2)}, u32[]{:S(2)}) collective-permute-start(bf16[32,1152]{1,0:T(8,128)(2,1)S(1)} %get-tuple-element.48), channel_id=1, source_target_pairs={{0,16},{1,17},{2,18},{3,19},{4,20},{5,21},{6,22},{7,23},{8,24},{9,... | collective-permute-start | bytes 221192 | tf_op jit(solution)/shard_map/ppermute | solution.py:420
  153.7 4.0 %collective-permute-start.3 = (bf16[32,1152]{1,0:T(8,128)(2,1)S(1)}, bf16[32,1152]{1,0:T(8,128)(2,1)S(1)}, u32[]{:S(2)}, u32[]{:S(2)}) collective-permute-start(bf16[32,1152]{1,0:T(8,128)(2,1)S(1)} %get-tuple-element.49), channel_id=1, source_target_pairs={{0,24},{1,25},{2,26},{3,27},{4,28},{5,29},{6,30},{7,31},{8,0},{9,1... | collective-permute-start | bytes 221192 | tf_op jit(solution)/shard_map/ppermute | solution.py:420
  157.7 7.5 %all-to-all-done.2 = bf16[8,48,1024]{2,1,0:T(8,128)(2,1)S(1)} async-done(((bf16[8,48,1024]{2,1,0:T(8,128)(2,1)}), bf16[8,48,1024]{2,1,0:T(8,128)(2,1)S(1)}, u32[]{:S(2)}, u32[]{:S(2)}) %all-to-all-start.2) | async-done | bytes 786464 | tf_op jit(solution)/shard_map/all_to_all | solution.py:263
  165.3 0.4 sum_second.1
  165.6 5.8 %collective-permute-start.4 = (bf16[32,1024]{1,0:T(8,128)(2,1)S(1)}, bf16[32,1024]{1,0:T(8,128)(2,1)S(1)}, u32[]{:S(2)}, u32[]{:S(2)}) collective-permute-start(bf16[32,1024]{1,0:T(8,128)(2,1)S(1)} %get-tuple-element.52), channel_id=1, source_target_pairs={{0,8},{1,9},{2,10},{3,11},{4,12},{5,13},{6,14},{7,15},{8,16},{9,17... | collective-permute-start | bytes 196616 | tf_op jit(solution)/shard_map/ppermute | solution.py:420
  171.5 9.7 %collective-permute-start.5 = (bf16[32,1024]{1,0:T(8,128)(2,1)S(1)}, bf16[32,1024]{1,0:T(8,128)(2,1)S(1)}, u32[]{:S(2)}, u32[]{:S(2)}) collective-permute-start(bf16[32,1024]{1,0:T(8,128)(2,1)S(1)} %get-tuple-element.53), channel_id=1, source_target_pairs={{0,16},{1,17},{2,18},{3,19},{4,20},{5,21},{6,22},{7,23},{8,24},{9,... | collective-permute-start | bytes 196616 | tf_op jit(solution)/shard_map/ppermute | solution.py:420
  181.2 4.5 %collective-permute-start.6 = (bf16[32,1024]{1,0:T(8,128)(2,1)S(1)}, bf16[32,1024]{1,0:T(8,128)(2,1)S(1)}, u32[]{:S(2)}, u32[]{:S(2)}) collective-permute-start(bf16[32,1024]{1,0:T(8,128)(2,1)S(1)} %get-tuple-element.54), channel_id=1, source_target_pairs={{0,24},{1,25},{2,26},{3,27},{4,28},{5,29},{6,30},{7,31},{8,0},{9,1... | collective-permute-start | bytes 196616 | tf_op jit(solution)/shard_map/ppermute | solution.py:420
  185.8 3.4 %collective-permute-done.5.refs_6_ = bf16[32,1024]{1,0:T(8,128)(2,1)S(1)} collective-permute-done((bf16[32,1024]{1,0:T(8,128)(2,1)S(1)}, bf16[32,1024]{1,0:T(8,128)(2,1)S(1)}, u32[]{:S(2)}, u32[]{:S(2)}) %collective-permute-start.5) | collective-permute-done | bytes 65568 | tf_op jit(solution)/shard_map/ppermute | solution.py:420
  189.1 2.1 %collective-permute-done.6.refs_7_ = bf16[32,1024]{1,0:T(8,128)(2,1)S(1)} collective-permute-done((bf16[32,1024]{1,0:T(8,128)(2,1)S(1)}, bf16[32,1024]{1,0:T(8,128)(2,1)S(1)}, u32[]{:S(2)}, u32[]{:S(2)}) %collective-permute-start.6) | collective-permute-done | bytes 65568 | tf_op jit(solution)/shard_map/ppermute | solution.py:420
  191.2 0.9 last.1
  (23 shorter events, 0.2 us)
Async XLA Ops:
  7.2 91.2 %all-gather.3.cloned.1.call-start = ((), (), s32[]{:S(2)}) async-start(), calls=%async_computation.5 | async-start | bytes 10027008 | tf_op jit(solution)/shard_map/all_gather | solution.py:320
  44.8 5.3 %copy-start.7 = (bf16[1,1,384,1536]{3,2,1,0:T(8,128)(2,1)S(1)}, bf16[1,1,384,1536]{3,2,1,0:T(8,128)(2,1)}, u32[]{:S(2)}) copy-start(bf16[1,1,384,1536]{3,2,1,0:T(8,128)(2,1)} %param.10) | copy-start | bytes 3538948
  44.8 37.0 %all-to-all-start = ((bf16[8,48,2176]{2,1,0:T(8,128)(2,1)}), bf16[8,48,2176]{2,1,0:T(8,128)(2,1)S(1)}, u32[]{:S(2)}, u32[]{:S(2)}) async-start(bf16[8,48,2176]{2,1,0:T(8,128)(2,1)} %get-tuple-element.32), calls=%async_computation | async-start | bytes 3342336 | tf_op jit(solution)/shard_map/all_to_all | solution.py:263
  51.3 1.0 copy-start.2
  52.4 1.1 copy-start.3
  53.5 0.8 copy-start.4
  81.8 16.6 %copy-start = (bf16[8,48,2176]{2,1,0:T(8,128)(2,1)}, bf16[8,48,2176]{2,1,0:T(8,128)(2,1)S(1)}, u32[]{:S(2)}) copy-start(bf16[8,48,2176]{2,1,0:T(8,128)(2,1)S(1)} %all-to-all-done) | copy-start | bytes 5013508
  108.7 26.8 %all-to-all-start.1 = ((bf16[8,48,1152]{2,1,0:T(8,128)(2,1)}), bf16[8,48,1152]{2,1,0:T(8,128)(2,1)S(1)}, u32[]{:S(2)}, u32[]{:S(2)}) async-start(bf16[8,48,1152]{2,1,0:T(8,128)(2,1)} %bitcast.26), calls=%async_computation.1 | async-start | bytes 1769472 | tf_op jit(solution)/shard_map/all_to_all | solution.py:263
  116.7 75.4 %reduce-scatter.2.cloned.1.call-start = ((), (), s32[]{:S(2)}) async-start(), calls=%async_computation.4 | async-start | bytes 1769472 | tf_op jit(solution)/shard_map/reduce_scatter | solution.py:394
  116.8 5.8 %copy-start.1 = (bf16[8,48,2176]{2,1,0:T(8,128)(2,1)S(1)}, bf16[8,48,2176]{2,1,0:T(8,128)(2,1)}, u32[]{:S(2)}) copy-start(bf16[8,48,2176]{2,1,0:T(8,128)(2,1)} %copy-done) | copy-start | bytes 5013508
  116.8 5.8 %copy-start.6 = (s32[2]{0:T(128)S(1)}, s32[2]{0:T(128)}, u32[]{:S(2)}) copy-start(s32[2]{0:T(128)} %pad_add_fusion.mine_ref) | copy-start | bytes 28
  125.1 5.3 %collective-permute-start = (bf16[384,2048]{1,0:T(8,128)(2,1)S(1)}, bf16[384,2048]{1,0:T(8,128)(2,1)S(1)}, u32[]{:S(2)}, u32[]{:S(2)}) collective-permute-start(bf16[384,2048]{1,0:T(8,128)(2,1)S(1)} %get-tuple-element.42), channel_id=1, source_target_pairs={{0,32},{32,0},{64,96},{96,64},{128,160},{160,128},{192,224},{224,1... | collective-permute-start | bytes 4718600 | tf_op jit(solution)/shard_map/ppermute | solution.py:391
  135.6 55.7 %copy-start.5 = (s32[32,8]{0,1:T(8,128)S(1)}, s32[32,8]{0,1:T(8,128)}, u32[]{:S(2)}) copy-start(s32[32,8]{0,1:T(8,128)} %param.8) | copy-start | bytes 3076
  135.6 29.7 %all-to-all-start.2 = ((bf16[8,48,1024]{2,1,0:T(8,128)(2,1)}), bf16[8,48,1024]{2,1,0:T(8,128)(2,1)S(1)}, u32[]{:S(2)}, u32[]{:S(2)}) async-start(bf16[8,48,1024]{2,1,0:T(8,128)(2,1)} %bitcast.13), calls=%async_computation.2 | async-start | bytes 1572864 | tf_op jit(solution)/shard_map/all_to_all | solution.py:263
  140.1 41.1 %collective-permute-start.1 = (bf16[32,1152]{1,0:T(8,128)(2,1)S(1)}, bf16[32,1152]{1,0:T(8,128)(2,1)S(1)}, u32[]{:S(2)}, u32[]{:S(2)}) collective-permute-start(bf16[32,1152]{1,0:T(8,128)(2,1)S(1)} %get-tuple-element.47), channel_id=1, source_target_pairs={{0,8},{1,9},{2,10},{3,11},{4,12},{5,13},{6,14},{7,15},{8,16},{9,17... | collective-permute-start | bytes 221192 | tf_op jit(solution)/shard_map/ppermute | solution.py:420
  144.3 41.5 %collective-permute-start.2 = (bf16[32,1152]{1,0:T(8,128)(2,1)S(1)}, bf16[32,1152]{1,0:T(8,128)(2,1)S(1)}, u32[]{:S(2)}, u32[]{:S(2)}) collective-permute-start(bf16[32,1152]{1,0:T(8,128)(2,1)S(1)} %get-tuple-element.48), channel_id=1, source_target_pairs={{0,16},{1,17},{2,18},{3,19},{4,20},{5,21},{6,22},{7,23},{8,24},{9,... | collective-permute-start | bytes 221192 | tf_op jit(solution)/shard_map/ppermute | solution.py:420
  153.7 32.0 %collective-permute-start.3 = (bf16[32,1152]{1,0:T(8,128)(2,1)S(1)}, bf16[32,1152]{1,0:T(8,128)(2,1)S(1)}, u32[]{:S(2)}, u32[]{:S(2)}) collective-permute-start(bf16[32,1152]{1,0:T(8,128)(2,1)S(1)} %get-tuple-element.49), channel_id=1, source_target_pairs={{0,24},{1,25},{2,26},{3,27},{4,28},{5,29},{6,30},{7,31},{8,0},{9,1... | collective-permute-start | bytes 221192 | tf_op jit(solution)/shard_map/ppermute | solution.py:420
  165.6 20.1 %collective-permute-start.4 = (bf16[32,1024]{1,0:T(8,128)(2,1)S(1)}, bf16[32,1024]{1,0:T(8,128)(2,1)S(1)}, u32[]{:S(2)}, u32[]{:S(2)}) collective-permute-start(bf16[32,1024]{1,0:T(8,128)(2,1)S(1)} %get-tuple-element.52), channel_id=1, source_target_pairs={{0,8},{1,9},{2,10},{3,11},{4,12},{5,13},{6,14},{7,15},{8,16},{9,17... | collective-permute-start | bytes 196616 | tf_op jit(solution)/shard_map/ppermute | solution.py:420
  171.5 17.6 %collective-permute-start.5 = (bf16[32,1024]{1,0:T(8,128)(2,1)S(1)}, bf16[32,1024]{1,0:T(8,128)(2,1)S(1)}, u32[]{:S(2)}, u32[]{:S(2)}) collective-permute-start(bf16[32,1024]{1,0:T(8,128)(2,1)S(1)} %get-tuple-element.53), channel_id=1, source_target_pairs={{0,16},{1,17},{2,18},{3,19},{4,20},{5,21},{6,22},{7,23},{8,24},{9,... | collective-permute-start | bytes 196616 | tf_op jit(solution)/shard_map/ppermute | solution.py:420
  181.2 10.1 %collective-permute-start.6 = (bf16[32,1024]{1,0:T(8,128)(2,1)S(1)}, bf16[32,1024]{1,0:T(8,128)(2,1)S(1)}, u32[]{:S(2)}, u32[]{:S(2)}) collective-permute-start(bf16[32,1024]{1,0:T(8,128)(2,1)S(1)} %get-tuple-element.54), channel_id=1, source_target_pairs={{0,24},{1,25},{2,26},{3,27},{4,28},{5,29},{6,30},{7,31},{8,0},{9,1... | collective-permute-start | bytes 196616 | tf_op jit(solution)/shard_map/ppermute | solution.py:420
Sparse Core Ops, SparseCore 0:
  10.1 88.2 all-gather.2
  132.3 42.0 reduce-scatter.1

commit v6 on v4

--- a/solution.py
+++ b/solution.py
@@ -9,7 +9,6 @@
 
 BF16, F32 = jnp.bfloat16, jnp.float32
 META = 128
-TILE = 512
 STRIDE = 4
 
 
@@ -27,41 +26,35 @@
 
 
 def prep_kernel(
-    rows_ref, ids_ref, weight_ref, gate_ref, up_ref, down_ref, tok_ref, pack_ref,
-    ids_buf, weight_buf, gate_buf, up_buf, sems,
+    rows_ref, ids_ref, weight_ref, gate_ref, up_ref, down_ref, tok_ref, pack_ref, downs_ref,
+    ids_buf, weight_buf, down_buf, sems,
 ):
     tok, width = rows_ref.shape
     topk = ids_ref.shape[0]
     hidden = gate_ref.shape[1]
-    down_rows = down_ref.shape[0]
     copies = [
-        pltpu.make_async_copy(gate_ref, gate_buf, sems.at[0]),
-        pltpu.make_async_copy(up_ref, up_buf, sems.at[1]),
-        pltpu.make_async_copy(down_ref, pack_ref.at[pl.ds(0, down_rows), :], sems.at[2]),
-        pltpu.make_async_copy(ids_ref, ids_buf, sems.at[3]),
-        pltpu.make_async_copy(weight_ref, weight_buf, sems.at[4]),
-        pltpu.make_async_copy(rows_ref, tok_ref.at[:, pl.ds(0, width)], sems.at[5]),
+        pltpu.make_async_copy(gate_ref, pack_ref.at[:, pl.ds(0, hidden)], sems.at[0]),
+        pltpu.make_async_copy(up_ref, pack_ref.at[:, pl.ds(hidden, hidden)], sems.at[1]),
+        pltpu.make_async_copy(ids_ref, ids_buf, sems.at[2]),
+        pltpu.make_async_copy(weight_ref, weight_buf, sems.at[3]),
+        pltpu.make_async_copy(rows_ref, tok_ref.at[:, pl.ds(0, width)], sems.at[4]),
+        pltpu.make_async_copy(down_ref, down_buf, sems.at[5]),
     ]
     for copy in copies:
         copy.start()
-    copies[0].wait()
-    copies[1].wait()
-    piece = TILE // 2
-    for i in range(gate_ref.shape[0] // 16):
-        for p in range(2 * hidden // piece):
-            n = i * (2 * hidden // TILE) + p // 2
-            row = down_rows + n // (width // TILE) * 16
-            lane = n % (width // TILE) * TILE + p % 2 * piece
-            buf = gate_buf if p * piece < hidden else up_buf
-            src = p * piece % hidden
-            pack_ref[row : row + 16, lane : lane + piece] = buf[i * 16 : i * 16 + 16, src : src + piece]
+    copies[5].wait()
+    outs = [
+        pltpu.make_async_copy(down_buf, downs_ref.at[i], sems.at[6 + i]) for i in range(downs_ref.shape[0])
+    ]
+    for copy in outs:
+        copy.start()
+    copies[2].wait()
     copies[3].wait()
-    copies[4].wait()
     meta = jnp.concatenate([ids_buf[...].astype(F32), weight_buf[...].astype(F32)], axis=0)
     meta = jnp.concatenate([meta, jnp.zeros((META - 2 * topk, tok), F32)], axis=0)
     tok_ref[:, width:] = turn(meta).astype(BF16)
-    copies[2].wait()
-    copies[5].wait()
+    for copy in copies[:2] + copies[4:5] + outs:
+        copy.wait()
 
 
 def select_kernel(cap, mine_ref, tok_ref, send_ref, select_ref):
@@ -89,10 +82,8 @@
     for j in range(dests):
         chosen = (key[j : j + 1, :] == pattern).astype(BF16)
         select_ref[j * per : (j + 1) * per, :] = chosen
-    for j in range(dests):
-        send_ref[j] = jnp.dot(
-            select_ref[j * per : (j + 1) * per, :], tok_ref[...], preferred_element_type=F32
-        ).astype(BF16)
+    sent = jnp.dot(select_ref[...], tok_ref[...], preferred_element_type=F32).astype(BF16)
+    send_ref[...] = sent.reshape(send_ref.shape)
 
 
 def act_kernel(cap, rows, pre_ref, hid_ref, turned_ref, slope_ref, silu_ref):
@@ -140,56 +131,24 @@
             ).astype(BF16)
 
 
-def fetch(pack_ref, base, wide_buf, sems, first):
-    _, rows, both = wide_buf.shape
-    across, per = both // TILE, pack_ref.shape[2] // TILE
-    copies = []
-    for i in range(rows // 16):
-        for j in range(across):
-            n = i * across + j
-            copies.append(
-                pltpu.make_async_copy(
-                    pack_ref.at[:, pl.ds(base + n // per * 16, 16), pl.ds(n % per * TILE, TILE)],
-                    wide_buf.at[:, pl.ds(i * 16, 16), pl.ds(j * TILE, TILE)],
-                    sems.at[first + n],
-                )
-            )
-    for copy in copies:
-        copy.start()
-    return copies
-
-
-def multiply(both_ref, wide_buf, out_buf, out_ref, sems, backs):
-    columns = 256
-    devices, rows, both = wide_buf.shape
-    group = columns // rows
-    for n in range(devices // group):
-        at = n * columns
-        out_buf[:, at : at + columns] = lax.dot_general(
-            both_ref[...],
-            wide_buf[n * group : (n + 1) * group].reshape(columns, both),
-            (((1,), (1,)), ((), ())),
-            preferred_element_type=F32,
-        ).astype(BF16)
-        part = pl.ds(at, columns)
-        backs.append(pltpu.make_async_copy(out_buf.at[:, part], out_ref.at[:, part], sems.at[n]))
-        backs[-1].start()
-    for copy in backs:
-        copy.wait()
-
-
 def mid_kernel(
-    mine_ref, got_ref, hid_ref, slope_ref, silu_ref, pack_ref, out_ref,
-    out_buf, both_ref, down_buf, wide_buf, in_sems, out_sems,
+    mine_ref, got_ref, hid_ref, slope_ref, silu_ref, own_ref, other_ref, pack_ref, out_ref,
+    out_buf, both_buf, down_buf, wide_buf, in_sems, out_sems,
 ):
     width = got_ref.shape[1] - META
     hidden = hid_ref.shape[1]
-    down_rows = down_buf.shape[1]
-    down_copy = pltpu.make_async_copy(pack_ref.at[:, pl.ds(0, down_rows), :], down_buf, in_sems.at[0])
-    down_copy.start()
-    copies = fetch(pack_ref, down_rows, wide_buf, in_sems, 1)
+    devices, wide, both = wide_buf.shape
+    core = mine_ref[1]
+    copies = [
+        pltpu.make_async_copy(own_ref, down_buf.at[:, core], in_sems.at[0]),
+        pltpu.make_async_copy(other_ref, down_buf.at[:, 1 - core], in_sems.at[1]),
+        pltpu.make_async_copy(pack_ref, wide_buf, in_sems.at[2]),
+    ]
+    for copy in copies:
+        copy.start()
     w = slot_weight(got_ref[:, width:], mine_ref[0])
-    down_copy.wait()
+    copies[0].wait()
+    copies[1].wait()
     q = lax.dot_general(
         got_ref[:, :width],
         down_buf[...].reshape(hidden, width),
@@ -198,17 +157,27 @@
     )
     route = jnp.sum(q * hid_ref[...].astype(F32), axis=1, keepdims=True)
     grad = w * q
-    both_ref[:, :hidden] = (grad * slope_ref[...]).astype(BF16)
-    both_ref[:, hidden:] = (grad * silu_ref[...]).astype(BF16)
+    both_buf[:, :hidden] = (grad * slope_ref[...]).astype(BF16)
+    both_buf[:, hidden:] = (grad * silu_ref[...]).astype(BF16)
     lane = lax.broadcasted_iota(jnp.int32, (got_ref.shape[0], META), 1)
     out_buf[:, width:] = jnp.where(lane == mine_ref[0], route, 0.0).astype(BF16)
-    extra = pl.ds(width, META)
-    last = out_sems.shape[0] - 1
-    backs = [pltpu.make_async_copy(out_buf.at[:, extra], out_ref.at[:, extra], out_sems.at[last])]
-    backs[0].start()
-    for copy in copies:
+    copies[2].wait()
+    backs = []
+    steps = out_sems.shape[0]
+    group = devices // steps
+    for n in range(steps):
+        at, size = n * group * wide, group * wide
+        out_buf[:, at : at + size] = lax.dot_general(
+            both_buf[...],
+            wide_buf[n * group : (n + 1) * group].reshape(size, both),
+            (((1,), (1,)), ((), ())),
+            preferred_element_type=F32,
+        ).astype(BF16)
+        part = pl.ds(at, size + META if n == steps - 1 else size)
+        backs.append(pltpu.make_async_copy(out_buf.at[:, part], out_ref.at[:, part], out_sems.at[n]))
+        backs[-1].start()
+    for copy in backs:
         copy.wait()
-    multiply(both_ref, wide_buf, out_buf, out_ref, out_sems, backs)
 
 
 def combine_kernel(place_ref, select_ref, back_ref, own_ref, next_ref, left_ref, right_ref, before_ref, total_buf):
@@ -301,23 +270,27 @@
     mine = jnp.stack([me, core]).astype(jnp.int32)
 
     wide = gate_weight.shape[1]
-    part = wide * both // width
-    rows, pack = pl.pallas_call(
+    chips = n_dp // 2
+    rows, pack, downs = pl.pallas_call(
         prep_kernel,
-        out_shape=(shape((tok, full)), shape((down_rows + part, width))),
+        out_shape=(shape((tok, full)), shape((wide, both)), shape((chips, down_rows, width))),
         in_specs=[whole(pltpu.HBM)] * 6,
-        out_specs=(whole(),) * 2,
+        out_specs=(whole(), whole(), whole(pltpu.HBM)),
         scratch_shapes=[
             pltpu.VMEM((expert_ids.shape[1], tok), jnp.int32),
             pltpu.VMEM((expert_ids.shape[1], tok), BF16),
-            pltpu.VMEM((wide, hidden), BF16),
-            pltpu.VMEM((wide, hidden), BF16),
-            pltpu.SemaphoreType.DMA((6,)),
+            pltpu.VMEM((down_rows, width), BF16),
+            pltpu.SemaphoreType.DMA((6 + chips,)),
         ],
         compiler_params=params(60),
         name="prep",
     )(grad_out, expert_ids.T, route_weights.T, gate_weight[0], up_weight[0], down_weight[0])
     packs = lax.all_gather(pack, "dp", axis=0, tiled=False)
+    same_core = [
+        [d * n_expert + e for d in range(c, n_dp, 2)] for c in range(2) for e in range(n_expert)
+    ]
+    swap = [(d, d ^ 1) for d in range(n_dp)]
+    own_down = exchange(downs, axes, same_core)
     blocks = lax.all_gather(rows, axes, axis=0, tiled=True, axis_index_groups=apart)
     send, select = pl.pallas_call(
         functools.partial(select_kernel, cap),
@@ -327,6 +300,8 @@
         compiler_params=params(16),
         name="select",
     )(members, blocks)
+    own_down, send = lax.optimization_barrier((own_down, send))
+    other_down = lax.ppermute(own_down, "dp", swap)
     got = exchange(send, axes, near).reshape(slots, full)
     hid, turned, slope, silu = pl.pallas_call(
         functools.partial(act_kernel, cap, down_rows),
@@ -342,6 +317,24 @@
         cost_estimate=pl.CostEstimate(flops=slots * slots * both * 2, bytes_accessed=8 * slots * both, transcendentals=0),
         name="act",
     )(pre)
+    back = pl.pallas_call(
+        mid_kernel,
+        out_shape=shape((slots, full)),
+        in_specs=[whole(pltpu.SMEM)] + [whole()] * 4 + [whole(pltpu.HBM)] * 3,
+        out_specs=whole(pltpu.HBM),
+        scratch_shapes=[
+            pltpu.VMEM((slots, full), BF16),
+            pltpu.VMEM((slots, both), BF16),
+            pltpu.VMEM((chips, 2, down_rows, width), BF16),
+            pltpu.VMEM((n_dp, wide, both), BF16),
+            pltpu.SemaphoreType.DMA((3,)),
+            pltpu.SemaphoreType.DMA((4,)),
+        ],
+        compiler_params=params(54),
+        cost_estimate=pl.CostEstimate(flops=6 * slots * hidden * width, bytes_accessed=6 * hidden * width, transcendentals=0),
+        name="mid",
+    )(mine, got, hid, slope, silu, own_down, other_down, packs)
+    got, _ = lax.optimization_barrier((got, back))
     keep, give = pl.pallas_call(
         down_kernel,
         out_shape=(shape((hidden // 2, width)), shape((hidden // 2, width))),
@@ -351,9 +344,8 @@
         cost_estimate=pl.CostEstimate(flops=2 * slots * hidden * width, bytes_accessed=2 * (slots + hidden) * width, transcendentals=0),
         name="down",
     )(mine, got, turned)
-    taken = lax.ppermute(give, "dp", [(d, d ^ 1) for d in range(n_dp)])
+    taken = lax.ppermute(give, "dp", swap)
     chip_part = (keep.astype(F32) + taken.astype(F32)).astype(BF16)
-    got, chip_part = lax.optimization_barrier((got, chip_part))
     down_grad = lax.psum_scatter(
         chip_part,
         "dp",
@@ -361,26 +353,8 @@
         tiled=True,
         axis_index_groups=[list(range(c, n_dp, 2)) for c in range(2)],
     )
-    columns = 256
-    pieces = wide // 16 * (both // TILE)
-    back = pl.pallas_call(
-        mid_kernel,
-        out_shape=shape((slots, full)),
-        in_specs=[whole(pltpu.SMEM)] + [whole()] * 4 + [whole(pltpu.HBM)],
-        out_specs=whole(pltpu.HBM),
-        scratch_shapes=[
-            pltpu.VMEM((slots, full), BF16),
-            pltpu.VMEM((slots, both), BF16),
-            pltpu.VMEM((n_dp, down_rows, width), BF16),
-            pltpu.VMEM((n_dp, wide, both), BF16),
-            pltpu.SemaphoreType.DMA((pieces + 1,)),
-            pltpu.SemaphoreType.DMA((width // columns + 1,)),
-        ],
-        compiler_params=params(54),
-        cost_estimate=pl.CostEstimate(flops=6 * slots * hidden * width, bytes_accessed=6 * hidden * width, transcendentals=0),
-        name="mid",
-    )(mine, got, hid, slope, silu, packs)
     back = exchange(back.reshape(dests, per, full), axes, near).reshape(slots, full)
+    back, _ = lax.optimization_barrier((back, chip_part))
     place = (me // 2 // STRIDE).reshape(1).astype(jnp.int32)
     cut = (full // META + 1) // 2 * META
     own, after, left, right, before = pl.pallas_call(

time: 197 us -> 187 us (0.949); the launches traced: 196 us -> 184 us
  waiting for transfers between devices: 89 us -> 60 us
  starting transfers between devices: 33.7 us -> 47.4 us
  local copies, waits for them, and re-layouts: 2.87 us -> 7.1 us
    all_to_all x2 -> x3, waiting for transfers between devices: 59.8 us -> 41.4 us  [exchange(): lax.all_to_all(value, axes, 0, 0, axis_index_groups=groups, tiled=True)]
    all_gather x1, waiting for transfers between devices: 6.91 us -> 0.01 us  [per_device(): packs = lax.all_gather(pack, 'dp', axis=0, tiled=False)]
    all_to_all x2 -> x3, starting transfers between devices: 13.3 us -> 20.2 us  [exchange(): lax.all_to_all(value, axes, 0, 0, axis_index_groups=groups, tiled=True)]
    ppermute x1 -> x2, starting transfers between devices: 1.92 us -> 8.53 us  [the longest x1 6.61 us: per_device(): other_down = lax.ppermute(own_down, 'dp', swap)]
    unnamed x14 -> x24, local copies, waits for them, and re-layouts: 2.87 us -> 7.1 us
    ppermute x4, waiting for transfers between devices: 18.2 us -> 15.3 us  [hop(): return lax.ppermute(value, 'expert', perm)]
  transfers between devices with their start and end apart: 9 -> 11, of which waited for: 7 -> 6; matrix products, arithmetic and copies ran while one was open for 1% -> 1% of each run, Pallas kernels for 4% -> 4%
where the time goes in v6:
time: 187 us; the launch traced here: 184 us
  waiting for transfers between devices  60 us (32%)
  starting transfers between devices  47.4 us (25%)
  blocking collectives  31.5 us (17%)
  Pallas kernels  21.6 us (12%)
  between operations  14.3 us (8%)
  local copies, waits for them, and re-layouts  7.1 us (4%)
  other arithmetic  2.4 us (1%)
    all_to_all x3, waiting for transfers between devices, exchange(): lax.all_to_all(value, axes, 0, 0, axis_index_groups=groups, tiled=True)  41.4 us
    all_gather x1, blocking collectives, per_device(): lax.all_gather(rows, axes, axis=0, tiled=True, axis_index_groups=apart)  31.5 us
    all_to_all x3, starting transfers between devices, exchange(): lax.all_to_all(value, axes, 0, 0, axis_index_groups=groups, tiled=True)  20.2 us
    ppermute x4, starting transfers between devices, hop(): return lax.ppermute(value, 'expert', perm)  18.6 us
    ppermute x4, waiting for transfers between devices, hop(): return lax.ppermute(value, 'expert', perm)  15.3 us
    pallas_call x1, Pallas kernels, per_device(): pl.pallas_call(mid_kernel, out_shape=shape((slots, full)), in_specs=[whol...  10.5 us
    unnamed x24, local copies, waits for them, and re-layouts  7.1 us
    ppermute x1, starting transfers between devices, per_device(): other_down = lax.ppermute(own_down, 'dp', swap)  6.61 us
  transfers between devices with their start and end apart: 11, of which 6 were waited for; matrix products, arithmetic and copies ran while one was open for 1% of the time, Pallas kernels for 4%

profile of v6, /device:TPU:1, one launch (start us, length us, event | category | flops | bytes accessed | tf_op | source)
XLA Modules:
  0.0 184.3 jit_solution(11030389387950685119)
XLA Ops:
  7.2 3.3 %prep.1 = (bf16[32,2176]{1,0:T(8,128)(2,1)}, bf16[128,1536]{1,0:T(8,128)(2,1)}, bf16[8,48,2048]{2,1,0:T(8,128)(2,1)}) custom-call(bf16[32,2048]{1,0:T(8,128)(2,1)} %rows_ref.1, s32[8,32]{1,0:T(8,128)} %bitcast.18, bf16[8,32]{1,0:T(8,128)(2,1)} %bitcast.26, bf16[128,768]{1,0:T(8,128)(2,1)} %bitcast.23, bf16[128,768]{1,0:T(8,128)(2,1)} %bitcast.24, ...), custom_call_target="tpu_custom_call" | custom-call | tf_op jit(solution)/shard_map/prep/pallas_call | solution.py:274
  10.6 6.1 %all-to-all-start = ((bf16[8,48,2048]{2,1,0:T(8,128)(2,1)}), bf16[8,48,2048]{2,1,0:T(8,128)(2,1)S(1)}, u32[]{:S(2)}, u32[]{:S(2)}) async-start(bf16[8,48,2048]{2,1,0:T(8,128)(2,1)} %get-tuple-element.27), calls=%async_computation | async-start | bytes 3145728 | tf_op jit(solution)/shard_map/all_to_all | solution.py:232
  16.7 31.5 %all_gather.9.tok_ref = bf16[128,2176]{1,0:T(8,128)(2,1)S(1)} all-gather(bf16[32,2176]{1,0:T(8,128)(2,1)S(1)} %copy-done.11), channel_id=1, replica_groups={{0,8,16,24},{1,9,17,25},{2,10,18,26},{3,11,19,27},{4,12,20,28},{5,13,21..., dimensions={0}, use_global_device_ids=true | all-gather | bytes 696320 | tf_op jit(solution)/shard_map/all_gather | solution.py:294
  48.3 2.5 %select.27 = (bf16[8,48,2176]{2,1,0:T(8,128)(2,1)}, bf16[384,128]{1,0:T(8,128)(2,1)S(1)}) custom-call(s32[8]{0:T(128)S(1)} %fusion.mine_ref, bf16[128,2176]{1,0:T(8,128)(2,1)S(1)} %all_gather.9.tok_ref), custom_call_target="tpu_custom_call" | custom-call | tf_op jit(solution)/shard_map/select/pallas_call | solution.py:295
  50.8 1.1 copy-done.10
  51.9 4.5 %all-to-all-start.1 = ((bf16[8,48,2176]{2,1,0:T(8,128)(2,1)}), bf16[8,48,2176]{2,1,0:T(8,128)(2,1)S(1)}, u32[]{:S(2)}, u32[]{:S(2)}) async-start(bf16[8,48,2176]{2,1,0:T(8,128)(2,1)} %get-tuple-element.29), calls=%async_computation.1 | async-start | bytes 3342336 | tf_op jit(solution)/shard_map/all_to_all | solution.py:232
  56.5 6.6 %collective-permute-start = (bf16[8,48,2048]{2,1,0:T(8,128)(2,1)}, bf16[8,48,2048]{2,1,0:T(8,128)(2,1)}, u32[]{:S(2)}, u32[]{:S(2)}) collective-permute-start(bf16[8,48,2048]{2,1,0:T(8,128)(2,1)} %copy-done.10), channel_id=1, source_target_pairs={{0,32},{32,0},{64,96},{96,64},{128,160},{160,128},{192,224},{224,1... | collective-permute-start | bytes 4718600 | tf_op jit(solution)/shard_map/ppermute | solution.py:304
  63.1 1.2 act.1
  64.3 1.0 copy-done.2
  65.3 1.0 copy-done.3
  66.4 0.8 copy-done.4
  67.2 0.8 copy-done.8
  68.0 0.6 pad_add_fusion.mine_ref
  68.6 19.6 %all-to-all-done.1 = bf16[8,48,2176]{2,1,0:T(8,128)(2,1)S(1)} async-done(((bf16[8,48,2176]{2,1,0:T(8,128)(2,1)}), bf16[8,48,2176]{2,1,0:T(8,128)(2,1)S(1)}, u32[]{:S(2)}, u32[]{:S(2)}) %all-to-all-start.1) | async-done | bytes 1671200 | tf_op jit(solution)/shard_map/all_to_all | solution.py:232
  88.1 1.2 copy-done
  89.4 10.5 %mid.1 = bf16[384,2176]{1,0:T(8,128)(2,1)} custom-call(s32[2]{0:T(128)} %pad_add_fusion.mine_ref, bf16[384,2176]{1,0:T(8,128)(2,1)} %bitcast.15, bf16[384,768]{1,0:T(8,128)(2,1)} %copy-done.4, f32[384,768]{1,0:T(8,128)} %copy-done.2, f32[384,768]{1,0:T(8,128)} %copy-done.3, bf16[8,48,2048]{2,1,0:T(8,128)(2,1)} %copy-done.10, ...), custom_call_target="tpu_custom_call" | custom-call | flops 3623878656 | bytes 9437184 | tf_op jit(solution)/shard_map/mid/pallas_call | solution.py:320
  99.9 9.6 %all-to-all-start.2 = ((bf16[8,48,2176]{2,1,0:T(8,128)(2,1)}), bf16[8,48,2176]{2,1,0:T(8,128)(2,1)S(1)}, u32[]{:S(2)}, u32[]{:S(2)}) async-start(bf16[8,48,2176]{2,1,0:T(8,128)(2,1)} %bitcast.21), calls=%async_computation.2 | async-start | bytes 3342336 | tf_op jit(solution)/shard_map/all_to_all | solution.py:232
  109.5 1.1 copy-done.9
  110.6 2.5 %down.1 = (bf16[384,2048]{1,0:T(8,128)(2,1)S(1)}, bf16[384,2048]{1,0:T(8,128)(2,1)S(1)}) custom-call(s32[2]{0:T(128)S(1)} %copy-done.6, bf16[384,2176]{1,0:T(8,128)(2,1)S(1)} %bitcast.16, bf16[768,384]{1,0:T(8,128)(2,1)S(1)} %copy-done.9), custom_call_target="tpu_custom_call" | custom-call | flops 1207959552 | bytes 4718592 | tf_op jit(solution)/shard_map/down/pallas_call | solution.py:338
  113.1 1.9 %collective-permute-start.1 = (bf16[384,2048]{1,0:T(8,128)(2,1)S(1)}, bf16[384,2048]{1,0:T(8,128)(2,1)S(1)}, u32[]{:S(2)}, u32[]{:S(2)}) collective-permute-start(bf16[384,2048]{1,0:T(8,128)(2,1)S(1)} %get-tuple-element.38), channel_id=1, source_target_pairs={{0,32},{32,0},{64,96},{96,64},{128,160},{160,128},{192,224},{224,1... | collective-permute-start | bytes 4718600 | tf_op jit(solution)/shard_map/ppermute | solution.py:347
  115.0 3.4 %collective-permute-done.1 = bf16[384,2048]{1,0:T(8,128)(2,1)S(1)} collective-permute-done((bf16[384,2048]{1,0:T(8,128)(2,1)S(1)}, bf16[384,2048]{1,0:T(8,128)(2,1)S(1)}, u32[]{:S(2)}, u32[]{:S(2)}) %collective-permute-start.1) | collective-permute-done | bytes 1572896 | tf_op jit(solution)/shard_map/ppermute | solution.py:347
  118.4 1.8 add_convert_fusion
  120.2 21.8 %all-to-all-done.2 = bf16[8,48,2176]{2,1,0:T(8,128)(2,1)S(1)} async-done(((bf16[8,48,2176]{2,1,0:T(8,128)(2,1)}), bf16[8,48,2176]{2,1,0:T(8,128)(2,1)S(1)}, u32[]{:S(2)}, u32[]{:S(2)}) %all-to-all-start.2) | async-done | bytes 1671200 | tf_op jit(solution)/shard_map/all_to_all | solution.py:232
  142.0 0.6 combine.1
  142.6 1.9 %collective-permute-start.2 = (bf16[32,1152]{1,0:T(8,128)(2,1)S(1)}, bf16[32,1152]{1,0:T(8,128)(2,1)S(1)}, u32[]{:S(2)}, u32[]{:S(2)}) collective-permute-start(bf16[32,1152]{1,0:T(8,128)(2,1)S(1)} %get-tuple-element.42), channel_id=1, source_target_pairs={{0,8},{1,9},{2,10},{3,11},{4,12},{5,13},{6,14},{7,15},{8,16},{9,17... | collective-permute-start | bytes 221192 | tf_op jit(solution)/shard_map/ppermute | solution.py:378
  144.5 7.3 %collective-permute-start.4 = (bf16[32,1024]{1,0:T(8,128)(2,1)S(1)}, bf16[32,1024]{1,0:T(8,128)(2,1)S(1)}, u32[]{:S(2)}, u32[]{:S(2)}) collective-permute-start(bf16[32,1024]{1,0:T(8,128)(2,1)S(1)} %get-tuple-element.44), channel_id=1, source_target_pairs={{0,24},{1,25},{2,26},{3,27},{4,28},{5,29},{6,30},{7,31},{8,0},{9,1... | collective-permute-start | bytes 196616 | tf_op jit(solution)/shard_map/ppermute | solution.py:378
  151.8 2.4 %collective-permute-done.4.more_ref = bf16[32,1024]{1,0:T(8,128)(2,1)S(1)} collective-permute-done((bf16[32,1024]{1,0:T(8,128)(2,1)S(1)}, bf16[32,1024]{1,0:T(8,128)(2,1)S(1)}, u32[]{:S(2)}, u32[]{:S(2)}) %collective-permute-start.4) | collective-permute-done | bytes 65568 | tf_op jit(solution)/shard_map/ppermute | solution.py:378
  154.3 7.5 %collective-permute-start.5 = (bf16[32,2176]{1,0:T(8,128)(2,1)S(1)}, bf16[32,2176]{1,0:T(8,128)(2,1)S(1)}, u32[]{:S(2)}, u32[]{:S(2)}) collective-permute-start(bf16[32,2176]{1,0:T(8,128)(2,1)S(1)} %pass_down.1), channel_id=1, source_target_pairs={{0,24},{1,25},{2,26},{3,27},{4,28},{5,29},{6,30},{7,31},{8,0},{9,1... | collective-permute-start | bytes 417800 | tf_op jit(solution)/shard_map/ppermute | solution.py:378
  161.8 1.9 %collective-permute-start.3 = (bf16[32,2176]{1,0:T(8,128)(2,1)S(1)}, bf16[32,2176]{1,0:T(8,128)(2,1)S(1)}, u32[]{:S(2)}, u32[]{:S(2)}) collective-permute-start(bf16[32,2176]{1,0:T(8,128)(2,1)S(1)} %pass_up.1), channel_id=1, source_target_pairs={{0,8},{1,9},{2,10},{3,11},{4,12},{5,13},{6,14},{7,15},{8,16},{9,17... | collective-permute-start | bytes 417800 | tf_op jit(solution)/shard_map/ppermute | solution.py:378
  163.8 3.8 %collective-permute-done.5.refs_2_ = bf16[32,2176]{1,0:T(8,128)(2,1)S(1)} collective-permute-done((bf16[32,2176]{1,0:T(8,128)(2,1)S(1)}, bf16[32,2176]{1,0:T(8,128)(2,1)S(1)}, u32[]{:S(2)}, u32[]{:S(2)}) %collective-permute-start.5) | collective-permute-done | bytes 139296 | tf_op jit(solution)/shard_map/ppermute | solution.py:378
  167.5 9.0 %collective-permute-done.3.refs_1_ = bf16[32,2176]{1,0:T(8,128)(2,1)S(1)} collective-permute-done((bf16[32,2176]{1,0:T(8,128)(2,1)S(1)}, bf16[32,2176]{1,0:T(8,128)(2,1)S(1)}, u32[]{:S(2)}, u32[]{:S(2)}) %collective-permute-start.3) | collective-permute-done | bytes 139296 | tf_op jit(solution)/shard_map/ppermute | solution.py:378
  176.6 0.9 last.1
  (29 shorter events, 0.2 us)
Async XLA Ops:
  7.2 81.0 %all-gather.3.cloned.1.call-start = ((), (), s32[]{:S(2)}) async-start(), calls=%async_computation.5 | async-start | bytes 6684672 | tf_op jit(solution)/shard_map/all_gather | solution.py:288
  10.6 6.1 %copy-start.11 = (bf16[32,2176]{1,0:T(8,128)(2,1)S(1)}, bf16[32,2176]{1,0:T(8,128)(2,1)}, u32[]{:S(2)}) copy-start(bf16[32,2176]{1,0:T(8,128)(2,1)} %get-tuple-element.25) | copy-start | bytes 417796
  10.6 40.2 %all-to-all-start = ((bf16[8,48,2048]{2,1,0:T(8,128)(2,1)}), bf16[8,48,2048]{2,1,0:T(8,128)(2,1)S(1)}, u32[]{:S(2)}, u32[]{:S(2)}) async-start(bf16[8,48,2048]{2,1,0:T(8,128)(2,1)} %get-tuple-element.27), calls=%async_computation | async-start | bytes 3145728 | tf_op jit(solution)/shard_map/all_to_all | solution.py:232
  50.8 1.1 copy-start.10
  50.8 12.3 %copy-start.7 = (bf16[1,1,384,1536]{3,2,1,0:T(8,128)(2,1)S(1)}, bf16[1,1,384,1536]{3,2,1,0:T(8,128)(2,1)}, u32[]{:S(2)}) copy-start(bf16[1,1,384,1536]{3,2,1,0:T(8,128)(2,1)} %param.10) | copy-start | bytes 3538948
  51.9 36.2 %all-to-all-start.1 = ((bf16[8,48,2176]{2,1,0:T(8,128)(2,1)}), bf16[8,48,2176]{2,1,0:T(8,128)(2,1)S(1)}, u32[]{:S(2)}, u32[]{:S(2)}) async-start(bf16[8,48,2176]{2,1,0:T(8,128)(2,1)} %get-tuple-element.29), calls=%async_computation.1 | async-start | bytes 3342336 | tf_op jit(solution)/shard_map/all_to_all | solution.py:232
  56.5 12.1 %collective-permute-start = (bf16[8,48,2048]{2,1,0:T(8,128)(2,1)}, bf16[8,48,2048]{2,1,0:T(8,128)(2,1)}, u32[]{:S(2)}, u32[]{:S(2)}) collective-permute-start(bf16[8,48,2048]{2,1,0:T(8,128)(2,1)} %copy-done.10), channel_id=1, source_target_pairs={{0,32},{32,0},{64,96},{96,64},{128,160},{160,128},{192,224},{224,1... | collective-permute-start | bytes 4718600 | tf_op jit(solution)/shard_map/ppermute | solution.py:304
  64.3 1.0 copy-start.2
  65.3 1.0 copy-start.3
  66.4 0.8 copy-start.4
  67.2 0.8 copy-start.8
  88.1 1.2 copy-start
  99.8 9.6 %copy-start.1 = (bf16[8,48,2176]{2,1,0:T(8,128)(2,1)S(1)}, bf16[8,48,2176]{2,1,0:T(8,128)(2,1)}, u32[]{:S(2)}) copy-start(bf16[8,48,2176]{2,1,0:T(8,128)(2,1)} %copy-done) | copy-start | bytes 5013508
  99.9 9.6 %copy-start.6 = (s32[2]{0:T(128)S(1)}, s32[2]{0:T(128)}, u32[]{:S(2)}) copy-start(s32[2]{0:T(128)} %pad_add_fusion.mine_ref) | copy-start | bytes 28
  99.9 42.2 %all-to-all-start.2 = ((bf16[8,48,2176]{2,1,0:T(8,128)(2,1)}), bf16[8,48,2176]{2,1,0:T(8,128)(2,1)S(1)}, u32[]{:S(2)}, u32[]{:S(2)}) async-start(bf16[8,48,2176]{2,1,0:T(8,128)(2,1)} %bitcast.21), calls=%async_computation.2 | async-start | bytes 3342336 | tf_op jit(solution)/shard_map/all_to_all | solution.py:232
  109.4 68.0 %reduce-scatter.2.cloned.1.call-start = ((), (), s32[]{:S(2)}) async-start(), calls=%async_computation.4 | async-start | bytes 1769472 | tf_op jit(solution)/shard_map/reduce_scatter | solution.py:349
  109.5 1.1 copy-start.9
  113.1 5.3 %collective-permute-start.1 = (bf16[384,2048]{1,0:T(8,128)(2,1)S(1)}, bf16[384,2048]{1,0:T(8,128)(2,1)S(1)}, u32[]{:S(2)}, u32[]{:S(2)}) collective-permute-start(bf16[384,2048]{1,0:T(8,128)(2,1)S(1)} %get-tuple-element.38), channel_id=1, source_target_pairs={{0,32},{32,0},{64,96},{96,64},{128,160},{160,128},{192,224},{224,1... | collective-permute-start | bytes 4718600 | tf_op jit(solution)/shard_map/ppermute | solution.py:347
  120.2 56.4 %copy-start.5 = (s32[32,8]{0,1:T(8,128)S(1)}, s32[32,8]{0,1:T(8,128)}, u32[]{:S(2)}) copy-start(s32[32,8]{0,1:T(8,128)} %param.8) | copy-start | bytes 3076
  142.6 19.2 %collective-permute-start.2 = (bf16[32,1152]{1,0:T(8,128)(2,1)S(1)}, bf16[32,1152]{1,0:T(8,128)(2,1)S(1)}, u32[]{:S(2)}, u32[]{:S(2)}) collective-permute-start(bf16[32,1152]{1,0:T(8,128)(2,1)S(1)} %get-tuple-element.42), channel_id=1, source_target_pairs={{0,8},{1,9},{2,10},{3,11},{4,12},{5,13},{6,14},{7,15},{8,16},{9,17... | collective-permute-start | bytes 221192 | tf_op jit(solution)/shard_map/ppermute | solution.py:378
  144.5 9.7 %collective-permute-start.4 = (bf16[32,1024]{1,0:T(8,128)(2,1)S(1)}, bf16[32,1024]{1,0:T(8,128)(2,1)S(1)}, u32[]{:S(2)}, u32[]{:S(2)}) collective-permute-start(bf16[32,1024]{1,0:T(8,128)(2,1)S(1)} %get-tuple-element.44), channel_id=1, source_target_pairs={{0,24},{1,25},{2,26},{3,27},{4,28},{5,29},{6,30},{7,31},{8,0},{9,1... | collective-permute-start | bytes 196616 | tf_op jit(solution)/shard_map/ppermute | solution.py:378
  154.3 13.3 %collective-permute-start.5 = (bf16[32,2176]{1,0:T(8,128)(2,1)S(1)}, bf16[32,2176]{1,0:T(8,128)(2,1)S(1)}, u32[]{:S(2)}, u32[]{:S(2)}) collective-permute-start(bf16[32,2176]{1,0:T(8,128)(2,1)S(1)} %pass_down.1), channel_id=1, source_target_pairs={{0,24},{1,25},{2,26},{3,27},{4,28},{5,29},{6,30},{7,31},{8,0},{9,1... | collective-permute-start | bytes 417800 | tf_op jit(solution)/shard_map/ppermute | solution.py:378
  161.8 14.7 %collective-permute-start.3 = (bf16[32,2176]{1,0:T(8,128)(2,1)S(1)}, bf16[32,2176]{1,0:T(8,128)(2,1)S(1)}, u32[]{:S(2)}, u32[]{:S(2)}) collective-permute-start(bf16[32,2176]{1,0:T(8,128)(2,1)S(1)} %pass_up.1), channel_id=1, source_target_pairs={{0,8},{1,9},{2,10},{3,11},{4,12},{5,13},{6,14},{7,15},{8,16},{9,17... | collective-permute-start | bytes 417800 | tf_op jit(solution)/shard_map/ppermute | solution.py:378
Sparse Core Ops, SparseCore 0:
  10.7 72.7 all-gather.2
  120.3 41.9 reduce-scatter.1

commit v7 on v6

--- a/solution.py
+++ b/solution.py
@@ -27,33 +27,40 @@
 
 def prep_kernel(
     rows_ref, ids_ref, weight_ref, gate_ref, up_ref, down_ref, tok_ref, pack_ref, downs_ref,
-    ids_buf, weight_buf, down_buf, sems,
+    tok_buf, pack_buf, down_buf, ids_buf, weight_buf, in_sems, out_sems,
 ):
     tok, width = rows_ref.shape
     topk = ids_ref.shape[0]
     hidden = gate_ref.shape[1]
     copies = [
-        pltpu.make_async_copy(gate_ref, pack_ref.at[:, pl.ds(0, hidden)], sems.at[0]),
-        pltpu.make_async_copy(up_ref, pack_ref.at[:, pl.ds(hidden, hidden)], sems.at[1]),
-        pltpu.make_async_copy(ids_ref, ids_buf, sems.at[2]),
-        pltpu.make_async_copy(weight_ref, weight_buf, sems.at[3]),
-        pltpu.make_async_copy(rows_ref, tok_ref.at[:, pl.ds(0, width)], sems.at[4]),
-        pltpu.make_async_copy(down_ref, down_buf, sems.at[5]),
+        pltpu.make_async_copy(ids_ref, ids_buf, in_sems.at[0]),
+        pltpu.make_async_copy(weight_ref, weight_buf, in_sems.at[1]),
+        pltpu.make_async_copy(down_ref, down_buf, in_sems.at[2]),
+        pltpu.make_async_copy(rows_ref, tok_buf.at[:, pl.ds(0, width)], in_sems.at[3]),
+        pltpu.make_async_copy(gate_ref, pack_buf.at[:, pl.ds(0, hidden)], in_sems.at[4]),
+        pltpu.make_async_copy(up_ref, pack_buf.at[:, pl.ds(hidden, hidden)], in_sems.at[5]),
     ]
     for copy in copies:
         copy.start()
-    copies[5].wait()
+    copies[0].wait()
+    copies[1].wait()
+    meta = jnp.concatenate([ids_buf[...].astype(F32), weight_buf[...].astype(F32)], axis=0)
+    meta = jnp.concatenate([meta, jnp.zeros((META - 2 * topk, tok), F32)], axis=0)
+    tok_buf[:, width:] = turn(meta).astype(BF16)
+    copies[2].wait()
     outs = [
-        pltpu.make_async_copy(down_buf, downs_ref.at[i], sems.at[6 + i]) for i in range(downs_ref.shape[0])
+        pltpu.make_async_copy(down_buf, downs_ref.at[i], out_sems.at[2 + i]) for i in range(downs_ref.shape[0])
     ]
     for copy in outs:
         copy.start()
-    copies[2].wait()
     copies[3].wait()
-    meta = jnp.concatenate([ids_buf[...].astype(F32), weight_buf[...].astype(F32)], axis=0)
-    meta = jnp.concatenate([meta, jnp.zeros((META - 2 * topk, tok), F32)], axis=0)
-    tok_ref[:, width:] = turn(meta).astype(BF16)
-    for copy in copies[:2] + copies[4:5] + outs:
+    outs.append(pltpu.make_async_copy(tok_buf, tok_ref, out_sems.at[0]))
+    outs[-1].start()
+    copies[4].wait()
+    copies[5].wait()
+    outs.append(pltpu.make_async_copy(pack_buf, pack_ref, out_sems.at[1]))
+    outs[-1].start()
+    for copy in outs:
         copy.wait()
 
 
@@ -117,36 +124,42 @@
     return jnp.sum(jnp.where((lane < topk) & (meta == expert.astype(F32)), weight, 0.0), axis=1, keepdims=True)
 
 
-def down_kernel(mine_ref, got_ref, turned_ref, keep_ref, send_ref):
+def down_kernel(mine_ref, scaled_ref, turned_ref, keep_ref, send_ref):
     half, width = keep_ref.shape
     core = mine_ref[1]
-    w = slot_weight(got_ref[:, width:], mine_ref[0])
     columns = 512
     for at in range(0, width, columns):
-        scaled = (w * got_ref[:, at : at + columns].astype(F32)).astype(BF16)
         for ref, which in ((send_ref, 1 - core), (keep_ref, core)):
             begin = pl.multiple_of(which * half, half)
             ref[:, at : at + columns] = jnp.dot(
-                turned_ref[pl.ds(begin, half), :], scaled, preferred_element_type=F32
+                turned_ref[pl.ds(begin, half), :], scaled_ref[:, at : at + columns], preferred_element_type=F32
             ).astype(BF16)
 
 
 def mid_kernel(
-    mine_ref, got_ref, hid_ref, slope_ref, silu_ref, own_ref, other_ref, pack_ref, out_ref,
-    out_buf, both_buf, down_buf, wide_buf, in_sems, out_sems,
+    mine_ref, got_ref, own_ref, other_ref, hid_ref, slope_ref, silu_ref, pack_ref, out_ref, scaled_ref,
+    out_buf, both_buf, scaled_buf, down_buf, hid_buf, slope_buf, silu_buf, wide_buf, in_sems, out_sems,
 ):
     width = got_ref.shape[1] - META
     hidden = hid_ref.shape[1]
     devices, wide, both = wide_buf.shape
     core = mine_ref[1]
-    copies = [
-        pltpu.make_async_copy(own_ref, down_buf.at[:, core], in_sems.at[0]),
-        pltpu.make_async_copy(other_ref, down_buf.at[:, 1 - core], in_sems.at[1]),
-        pltpu.make_async_copy(pack_ref, wide_buf, in_sems.at[2]),
-    ]
+    places = (
+        (own_ref, down_buf.at[:, core]),
+        (other_ref, down_buf.at[:, 1 - core]),
+        (hid_ref, hid_buf),
+        (slope_ref, slope_buf),
+        (silu_ref, silu_buf),
+        (pack_ref, wide_buf),
+    )
+    copies = [pltpu.make_async_copy(src, dst, in_sems.at[n]) for n, (src, dst) in enumerate(places)]
     for copy in copies:
         copy.start()
     w = slot_weight(got_ref[:, width:], mine_ref[0])
+    scaled_buf[...] = (w * got_ref[:, :width].astype(F32)).astype(BF16)
+    steps = out_sems.shape[0] - 1
+    backs = [pltpu.make_async_copy(scaled_buf, scaled_ref, out_sems.at[steps])]
+    backs[0].start()
     copies[0].wait()
     copies[1].wait()
     q = lax.dot_general(
@@ -155,15 +168,15 @@
         (((1,), (1,)), ((), ())),
         preferred_element_type=F32,
     )
-    route = jnp.sum(q * hid_ref[...].astype(F32), axis=1, keepdims=True)
+    for copy in copies[2:5]:
+        copy.wait()
+    route = jnp.sum(q * hid_buf[...].astype(F32), axis=1, keepdims=True)
     grad = w * q
-    both_buf[:, :hidden] = (grad * slope_ref[...]).astype(BF16)
-    both_buf[:, hidden:] = (grad * silu_ref[...]).astype(BF16)
+    both_buf[:, :hidden] = (grad * slope_buf[...]).astype(BF16)
+    both_buf[:, hidden:] = (grad * silu_buf[...]).astype(BF16)
     lane = lax.broadcasted_iota(jnp.int32, (got_ref.shape[0], META), 1)
     out_buf[:, width:] = jnp.where(lane == mine_ref[0], route, 0.0).astype(BF16)
-    copies[2].wait()
-    backs = []
-    steps = out_sems.shape[0]
+    copies[5].wait()
     group = devices // steps
     for n in range(steps):
         at, size = n * group * wide, group * wide
@@ -275,12 +288,15 @@
         prep_kernel,
         out_shape=(shape((tok, full)), shape((wide, both)), shape((chips, down_rows, width))),
         in_specs=[whole(pltpu.HBM)] * 6,
-        out_specs=(whole(), whole(), whole(pltpu.HBM)),
+        out_specs=(whole(pltpu.HBM),) * 3,
         scratch_shapes=[
+            pltpu.VMEM((tok, full), BF16),
+            pltpu.VMEM((wide, both), BF16),
+            pltpu.VMEM((down_rows, width), BF16),
             pltpu.VMEM((expert_ids.shape[1], tok), jnp.int32),
             pltpu.VMEM((expert_ids.shape[1], tok), BF16),
-            pltpu.VMEM((down_rows, width), BF16),
-            pltpu.SemaphoreType.DMA((6 + chips,)),
+            pltpu.SemaphoreType.DMA((6,)),
+            pltpu.SemaphoreType.DMA((2 + chips,)),
         ],
         compiler_params=params(60),
         name="prep",
@@ -317,24 +333,28 @@
         cost_estimate=pl.CostEstimate(flops=slots * slots * both * 2, bytes_accessed=8 * slots * both, transcendentals=0),
         name="act",
     )(pre)
-    back = pl.pallas_call(
+    back, scaled = pl.pallas_call(
         mid_kernel,
-        out_shape=shape((slots, full)),
-        in_specs=[whole(pltpu.SMEM)] + [whole()] * 4 + [whole(pltpu.HBM)] * 3,
-        out_specs=whole(pltpu.HBM),
+        out_shape=(shape((slots, full)), shape((slots, width))),
+        in_specs=[whole(pltpu.SMEM), whole()] + [whole(pltpu.HBM)] * 6,
+        out_specs=(whole(pltpu.HBM),) * 2,
         scratch_shapes=[
             pltpu.VMEM((slots, full), BF16),
             pltpu.VMEM((slots, both), BF16),
+            pltpu.VMEM((slots, width), BF16),
             pltpu.VMEM((chips, 2, down_rows, width), BF16),
+            pltpu.VMEM((slots, hidden), BF16),
+            pltpu.VMEM((slots, hidden), F32),
+            pltpu.VMEM((slots, hidden), F32),
             pltpu.VMEM((n_dp, wide, both), BF16),
-            pltpu.SemaphoreType.DMA((3,)),
-            pltpu.SemaphoreType.DMA((4,)),
+            pltpu.SemaphoreType.DMA((6,)),
+            pltpu.SemaphoreType.DMA((5,)),
         ],
-        compiler_params=params(54),
+        compiler_params=params(50),
         cost_estimate=pl.CostEstimate(flops=6 * slots * hidden * width, bytes_accessed=6 * hidden * width, transcendentals=0),
         name="mid",
-    )(mine, got, hid, slope, silu, own_down, other_down, packs)
-    got, _ = lax.optimization_barrier((got, back))
+    )(mine, got, own_down, other_down, hid, slope, silu, packs)
+    scaled, _ = lax.optimization_barrier((scaled, back))
     keep, give = pl.pallas_call(
         down_kernel,
         out_shape=(shape((hidden // 2, width)), shape((hidden // 2, width))),
@@ -343,7 +363,7 @@
         compiler_params=params(20),
         cost_estimate=pl.CostEstimate(flops=2 * slots * hidden * width, bytes_accessed=2 * (slots + hidden) * width, transcendentals=0),
         name="down",
-    )(mine, got, turned)
+    )(mine, scaled, turned)
     taken = lax.ppermute(give, "dp", swap)
     chip_part = (keep.astype(F32) + taken.astype(F32)).astype(BF16)
     down_grad = lax.psum_scatter(

time: 187 us -> 185 us (0.989)
  local copies, waits for them, and re-layouts: 7.1 us -> 3.49 us
  starting transfers between devices: 47.4 us -> 49.6 us
  waiting for transfers between devices: 60 us -> 62 us
    unnamed x24 -> x12, local copies, waits for them, and re-layouts: 7.1 us -> 3.49 us
    all_to_all x3, starting transfers between devices: 20.2 us -> 22.4 us  [exchange(): lax.all_to_all(value, axes, 0, 0, axis_index_groups=groups, tiled=True)]
    all_to_all x3, waiting for transfers between devices: 41.4 us -> 43.3 us  [exchange(): lax.all_to_all(value, axes, 0, 0, axis_index_groups=groups, tiled=True)]
where the time goes in v7:
time: 185 us; the launch traced here: 183 us
  waiting for transfers between devices  62 us (34%)
  starting transfers between devices  49.6 us (27%)
  blocking collectives  31.5 us (17%)
  Pallas kernels  20.2 us (11%)
  between operations  14.2 us (8%)
  local copies, waits for them, and re-layouts  3.49 us (2%)
  other arithmetic  1.88 us (1%)
    all_to_all x3, waiting for transfers between devices, exchange(): lax.all_to_all(value, axes, 0, 0, axis_index_groups=groups, tiled=True)  43.3 us
    all_gather x1, blocking collectives, per_device(): lax.all_gather(rows, axes, axis=0, tiled=True, axis_index_groups=apart)  31.5 us
    all_to_all x3, starting transfers between devices, exchange(): lax.all_to_all(value, axes, 0, 0, axis_index_groups=groups, tiled=True)  22.4 us
    ppermute x4, starting transfers between devices, hop(): return lax.ppermute(value, 'expert', perm)  18.6 us
    ppermute x4, waiting for transfers between devices, hop(): return lax.ppermute(value, 'expert', perm)  15.2 us
    pallas_call x1, Pallas kernels, per_device(): pl.pallas_call(mid_kernel, out_shape=(shape((slots, full)), shape((slots,...  10.1 us
    ppermute x1, starting transfers between devices, per_device(): other_down = lax.ppermute(own_down, 'dp', swap)  6.62 us
  transfers between devices with their start and end apart: 11, of which 6 were waited for; matrix products, arithmetic and copies ran while one was open for 1% of the time, Pallas kernels for 4%

profile of v7, /device:TPU:1, one launch (start us, length us, event | category | flops | bytes accessed | tf_op | source)
XLA Modules:
  0.0 183.0 jit_solution(18280731121153172835)
XLA Ops:
  7.2 0.0 all-gather.3.cloned.1.call-start
  7.2 2.4 %prep.1 = (bf16[32,2176]{1,0:T(8,128)(2,1)}, bf16[128,1536]{1,0:T(8,128)(2,1)}, bf16[8,48,2048]{2,1,0:T(8,128)(2,1)}) custom-call(bf16[32,2048]{1,0:T(8,128)(2,1)} %rows_ref.1, s32[8,32]{1,0:T(8,128)} %bitcast.16, bf16[8,32]{1,0:T(8,128)(2,1)} %bitcast.24, bf16[128,768]{1,0:T(8,128)(2,1)} %bitcast.21, bf16[128,768]{1,0:T(8,128)(2,1)} %bitcast.22, ...), custom_call_target="tpu_custom_call" | custom-call | tf_op jit(solution)/shard_map/prep/pallas_call | solution.py:287
  9.6 0.0 all-gather.3.cloned.1.call-update
  9.7 6.1 %all-to-all-start = ((bf16[8,48,2048]{2,1,0:T(8,128)(2,1)}), bf16[8,48,2048]{2,1,0:T(8,128)(2,1)}, u32[]{:S(2)}, u32[]{:S(2)}) async-start(bf16[8,48,2048]{2,1,0:T(8,128)(2,1)} %get-tuple-element.29), calls=%async_computation | async-start | bytes 3145728 | tf_op jit(solution)/shard_map/all_to_all | solution.py:245
  15.8 31.5 %all_gather.9.tok_ref = bf16[128,2176]{1,0:T(8,128)(2,1)S(1)} all-gather(bf16[32,2176]{1,0:T(8,128)(2,1)S(1)} %copy-done.5), channel_id=1, replica_groups={{0,8,16,24},{1,9,17,25},{2,10,18,26},{3,11,19,27},{4,12,20,28},{5,13,21..., dimensions={0}, use_global_device_ids=true | all-gather | bytes 696320 | tf_op jit(solution)/shard_map/all_gather | solution.py:310
  47.3 2.6 %select.27 = (bf16[8,48,2176]{2,1,0:T(8,128)(2,1)}, bf16[384,128]{1,0:T(8,128)(2,1)S(1)}) custom-call(s32[8]{0:T(128)S(1)} %fusion.mine_ref, bf16[128,2176]{1,0:T(8,128)(2,1)S(1)} %all_gather.9.tok_ref), custom_call_target="tpu_custom_call" | custom-call | tf_op jit(solution)/shard_map/select/pallas_call | solution.py:311
  49.9 4.5 %all-to-all-start.1 = ((bf16[8,48,2176]{2,1,0:T(8,128)(2,1)}), bf16[8,48,2176]{2,1,0:T(8,128)(2,1)}, u32[]{:S(2)}, u32[]{:S(2)}) async-start(bf16[8,48,2176]{2,1,0:T(8,128)(2,1)} %get-tuple-element.31), calls=%async_computation.1 | async-start | bytes 3342336 | tf_op jit(solution)/shard_map/all_to_all | solution.py:245
  54.4 6.6 %collective-permute-start = (bf16[8,48,2048]{2,1,0:T(8,128)(2,1)}, bf16[8,48,2048]{2,1,0:T(8,128)(2,1)}, u32[]{:S(2)}, u32[]{:S(2)}) collective-permute-start(bf16[8,48,2048]{2,1,0:T(8,128)(2,1)} %all-to-all-done.own_ref), channel_id=1, source_target_pairs={{0,32},{32,0},{64,96},{96,64},{128,160},{160,128},{192,224},{224,1... | collective-permute-start | bytes 4718600 | tf_op jit(solution)/shard_map/ppermute | solution.py:320
  61.1 1.3 copy-done.2
  62.3 1.3 act.1
  63.6 0.8 copy-done.3
  64.4 0.1 pad_add_fusion.mine_ref
  64.5 21.7 %all-to-all-done.1 = bf16[8,48,2176]{2,1,0:T(8,128)(2,1)} async-done(((bf16[8,48,2176]{2,1,0:T(8,128)(2,1)}), bf16[8,48,2176]{2,1,0:T(8,128)(2,1)}, u32[]{:S(2)}, u32[]{:S(2)}) %all-to-all-start.1) | async-done | bytes 1671200 | tf_op jit(solution)/shard_map/all_to_all | solution.py:245
  86.2 10.1 %mid.1 = (bf16[384,2176]{1,0:T(8,128)(2,1)}, bf16[384,2048]{1,0:T(8,128)(2,1)}) custom-call(s32[2]{0:T(128)S(1)} %pad_add_fusion.mine_ref, bf16[384,2176]{1,0:T(8,128)(2,1)} %bitcast.8.got_ref, bf16[8,48,2048]{2,1,0:T(8,128)(2,1)} %all-to-all-done.own_ref, bf16[8,48,2048]{2,1,0:T(8,128)(2,1)} %collective-permute-done.other_ref, ...), custom_call_target="tpu_custom_call" | custom-call | flops 3623878656 | bytes 9437184 | tf_op jit(solution)/shard_map/mid/pallas_call | solution.py:336
  96.3 11.8 %all-to-all-start.2 = ((bf16[8,48,2176]{2,1,0:T(8,128)(2,1)}), bf16[8,48,2176]{2,1,0:T(8,128)(2,1)S(1)}, u32[]{:S(2)}, u32[]{:S(2)}) async-start(bf16[8,48,2176]{2,1,0:T(8,128)(2,1)} %bitcast.20), calls=%async_computation.2 | async-start | bytes 3342336 | tf_op jit(solution)/shard_map/all_to_all | solution.py:245
  108.1 0.0 reduce-scatter.2.cloned.1.call-start
  108.2 1.4 copy-done.1
  109.6 2.4 %down.1 = (bf16[384,2048]{1,0:T(8,128)(2,1)S(1)}, bf16[384,2048]{1,0:T(8,128)(2,1)S(1)}) custom-call(s32[2]{0:T(128)S(1)} %pad_add_fusion.mine_ref, bf16[384,2048]{1,0:T(8,128)(2,1)S(1)} %copy-done.1, bf16[768,384]{1,0:T(8,128)(2,1)S(1)} %copy-done.4), custom_call_target="tpu_custom_call" | custom-call | flops 1207959552 | bytes 4718592 | tf_op jit(solution)/shard_map/down/pallas_call | solution.py:358
  111.9 1.9 %collective-permute-start.1 = (bf16[384,2048]{1,0:T(8,128)(2,1)S(1)}, bf16[384,2048]{1,0:T(8,128)(2,1)S(1)}, u32[]{:S(2)}, u32[]{:S(2)}) collective-permute-start(bf16[384,2048]{1,0:T(8,128)(2,1)S(1)} %get-tuple-element.42), channel_id=1, source_target_pairs={{0,32},{32,0},{64,96},{96,64},{128,160},{160,128},{192,224},{224,1... | collective-permute-start | bytes 4718600 | tf_op jit(solution)/shard_map/ppermute | solution.py:367
  113.9 3.4 %collective-permute-done.1 = bf16[384,2048]{1,0:T(8,128)(2,1)S(1)} collective-permute-done((bf16[384,2048]{1,0:T(8,128)(2,1)S(1)}, bf16[384,2048]{1,0:T(8,128)(2,1)S(1)}, u32[]{:S(2)}, u32[]{:S(2)}) %collective-permute-start.1) | collective-permute-done | bytes 1572896 | tf_op jit(solution)/shard_map/ppermute | solution.py:367
  117.3 1.8 add_convert_fusion
  119.0 0.0 reduce-scatter.2.cloned.1.call-update
  119.1 21.6 %all-to-all-done.2 = bf16[8,48,2176]{2,1,0:T(8,128)(2,1)S(1)} async-done(((bf16[8,48,2176]{2,1,0:T(8,128)(2,1)}), bf16[8,48,2176]{2,1,0:T(8,128)(2,1)S(1)}, u32[]{:S(2)}, u32[]{:S(2)}) %all-to-all-start.2) | async-done | bytes 1671200 | tf_op jit(solution)/shard_map/all_to_all | solution.py:245
  140.7 0.6 combine.1
  141.3 1.9 %collective-permute-start.2 = (bf16[32,1152]{1,0:T(8,128)(2,1)S(1)}, bf16[32,1152]{1,0:T(8,128)(2,1)S(1)}, u32[]{:S(2)}, u32[]{:S(2)}) collective-permute-start(bf16[32,1152]{1,0:T(8,128)(2,1)S(1)} %get-tuple-element.46), channel_id=1, source_target_pairs={{0,8},{1,9},{2,10},{3,11},{4,12},{5,13},{6,14},{7,15},{8,16},{9,17... | collective-permute-start | bytes 221192 | tf_op jit(solution)/shard_map/ppermute | solution.py:398
  143.2 7.3 %collective-permute-start.4 = (bf16[32,1024]{1,0:T(8,128)(2,1)S(1)}, bf16[32,1024]{1,0:T(8,128)(2,1)S(1)}, u32[]{:S(2)}, u32[]{:S(2)}) collective-permute-start(bf16[32,1024]{1,0:T(8,128)(2,1)S(1)} %get-tuple-element.48), channel_id=1, source_target_pairs={{0,24},{1,25},{2,26},{3,27},{4,28},{5,29},{6,30},{7,31},{8,0},{9,1... | collective-permute-start | bytes 196616 | tf_op jit(solution)/shard_map/ppermute | solution.py:398
  150.5 2.4 %collective-permute-done.4.more_ref = bf16[32,1024]{1,0:T(8,128)(2,1)S(1)} collective-permute-done((bf16[32,1024]{1,0:T(8,128)(2,1)S(1)}, bf16[32,1024]{1,0:T(8,128)(2,1)S(1)}, u32[]{:S(2)}, u32[]{:S(2)}) %collective-permute-start.4) | collective-permute-done | bytes 65568 | tf_op jit(solution)/shard_map/ppermute | solution.py:398
  153.0 7.5 %collective-permute-start.5 = (bf16[32,2176]{1,0:T(8,128)(2,1)S(1)}, bf16[32,2176]{1,0:T(8,128)(2,1)S(1)}, u32[]{:S(2)}, u32[]{:S(2)}) collective-permute-start(bf16[32,2176]{1,0:T(8,128)(2,1)S(1)} %pass_down.1), channel_id=1, source_target_pairs={{0,24},{1,25},{2,26},{3,27},{4,28},{5,29},{6,30},{7,31},{8,0},{9,1... | collective-permute-start | bytes 417800 | tf_op jit(solution)/shard_map/ppermute | solution.py:398
  160.5 1.9 %collective-permute-start.3 = (bf16[32,2176]{1,0:T(8,128)(2,1)S(1)}, bf16[32,2176]{1,0:T(8,128)(2,1)S(1)}, u32[]{:S(2)}, u32[]{:S(2)}) collective-permute-start(bf16[32,2176]{1,0:T(8,128)(2,1)S(1)} %pass_up.1), channel_id=1, source_target_pairs={{0,8},{1,9},{2,10},{3,11},{4,12},{5,13},{6,14},{7,15},{8,16},{9,17... | collective-permute-start | bytes 417800 | tf_op jit(solution)/shard_map/ppermute | solution.py:398
  162.5 3.8 %collective-permute-done.5.refs_2_ = bf16[32,2176]{1,0:T(8,128)(2,1)S(1)} collective-permute-done((bf16[32,2176]{1,0:T(8,128)(2,1)S(1)}, bf16[32,2176]{1,0:T(8,128)(2,1)S(1)}, u32[]{:S(2)}, u32[]{:S(2)}) %collective-permute-start.5) | collective-permute-done | bytes 139296 | tf_op jit(solution)/shard_map/ppermute | solution.py:398
  166.3 8.9 %collective-permute-done.3.refs_1_ = bf16[32,2176]{1,0:T(8,128)(2,1)S(1)} collective-permute-done((bf16[32,2176]{1,0:T(8,128)(2,1)S(1)}, bf16[32,2176]{1,0:T(8,128)(2,1)S(1)}, u32[]{:S(2)}, u32[]{:S(2)}) %collective-permute-start.3) | collective-permute-done | bytes 139296 | tf_op jit(solution)/shard_map/ppermute | solution.py:398
  175.2 0.9 last.1
  (17 shorter events, 0.1 us)
Async XLA Ops:
  7.2 79.0 %all-gather.3.cloned.1.call-start = ((), (), s32[]{:S(2)}) async-start(), calls=%async_computation.5 | async-start | bytes 6684672 | tf_op jit(solution)/shard_map/all_gather | solution.py:304
  9.7 6.1 %copy-start.5 = (bf16[32,2176]{1,0:T(8,128)(2,1)S(1)}, bf16[32,2176]{1,0:T(8,128)(2,1)}, u32[]{:S(2)}) copy-start(bf16[32,2176]{1,0:T(8,128)(2,1)} %get-tuple-element.27) | copy-start | bytes 417796
  9.7 40.2 %all-to-all-start = ((bf16[8,48,2048]{2,1,0:T(8,128)(2,1)}), bf16[8,48,2048]{2,1,0:T(8,128)(2,1)}, u32[]{:S(2)}, u32[]{:S(2)}) async-start(bf16[8,48,2048]{2,1,0:T(8,128)(2,1)} %get-tuple-element.29), calls=%async_computation | async-start | bytes 3145728 | tf_op jit(solution)/shard_map/all_to_all | solution.py:245
  49.9 36.3 %all-to-all-start.1 = ((bf16[8,48,2176]{2,1,0:T(8,128)(2,1)}), bf16[8,48,2176]{2,1,0:T(8,128)(2,1)}, u32[]{:S(2)}, u32[]{:S(2)}) async-start(bf16[8,48,2176]{2,1,0:T(8,128)(2,1)} %get-tuple-element.31), calls=%async_computation.1 | async-start | bytes 3342336 | tf_op jit(solution)/shard_map/all_to_all | solution.py:245
  54.4 10.1 %collective-permute-start = (bf16[8,48,2048]{2,1,0:T(8,128)(2,1)}, bf16[8,48,2048]{2,1,0:T(8,128)(2,1)}, u32[]{:S(2)}, u32[]{:S(2)}) collective-permute-start(bf16[8,48,2048]{2,1,0:T(8,128)(2,1)} %all-to-all-done.own_ref), channel_id=1, source_target_pairs={{0,32},{32,0},{64,96},{96,64},{128,160},{160,128},{192,224},{224,1... | collective-permute-start | bytes 4718600 | tf_op jit(solution)/shard_map/ppermute | solution.py:320
  61.1 1.3 copy-start.2
  63.6 0.8 copy-start.3
  96.3 11.8 %copy-start.4 = (bf16[768,384]{1,0:T(8,128)(2,1)S(1)}, bf16[768,384]{1,0:T(8,128)(2,1)}, u32[]{:S(2)}) copy-start(bf16[768,384]{1,0:T(8,128)(2,1)} %copy-done.3) | copy-start | bytes 1769476
  96.3 44.4 %all-to-all-start.2 = ((bf16[8,48,2176]{2,1,0:T(8,128)(2,1)}), bf16[8,48,2176]{2,1,0:T(8,128)(2,1)S(1)}, u32[]{:S(2)}, u32[]{:S(2)}) async-start(bf16[8,48,2176]{2,1,0:T(8,128)(2,1)} %bitcast.20), calls=%async_computation.2 | async-start | bytes 3342336 | tf_op jit(solution)/shard_map/all_to_all | solution.py:245
  108.1 68.0 %reduce-scatter.2.cloned.1.call-start = ((), (), s32[]{:S(2)}) async-start(), calls=%async_computation.4 | async-start | bytes 1769472 | tf_op jit(solution)/shard_map/reduce_scatter | solution.py:369
  108.2 1.4 copy-start.1
  111.9 5.3 %collective-permute-start.1 = (bf16[384,2048]{1,0:T(8,128)(2,1)S(1)}, bf16[384,2048]{1,0:T(8,128)(2,1)S(1)}, u32[]{:S(2)}, u32[]{:S(2)}) collective-permute-start(bf16[384,2048]{1,0:T(8,128)(2,1)S(1)} %get-tuple-element.42), channel_id=1, source_target_pairs={{0,32},{32,0},{64,96},{96,64},{128,160},{160,128},{192,224},{224,1... | collective-permute-start | bytes 4718600 | tf_op jit(solution)/shard_map/ppermute | solution.py:367
  119.1 56.2 %copy-start = (s32[32,8]{0,1:T(8,128)S(1)}, s32[32,8]{0,1:T(8,128)}, u32[]{:S(2)}) copy-start(s32[32,8]{0,1:T(8,128)} %param.8) | copy-start | bytes 3076
  141.3 19.2 %collective-permute-start.2 = (bf16[32,1152]{1,0:T(8,128)(2,1)S(1)}, bf16[32,1152]{1,0:T(8,128)(2,1)S(1)}, u32[]{:S(2)}, u32[]{:S(2)}) collective-permute-start(bf16[32,1152]{1,0:T(8,128)(2,1)S(1)} %get-tuple-element.46), channel_id=1, source_target_pairs={{0,8},{1,9},{2,10},{3,11},{4,12},{5,13},{6,14},{7,15},{8,16},{9,17... | collective-permute-start | bytes 221192 | tf_op jit(solution)/shard_map/ppermute | solution.py:398
  143.2 9.7 %collective-permute-start.4 = (bf16[32,1024]{1,0:T(8,128)(2,1)S(1)}, bf16[32,1024]{1,0:T(8,128)(2,1)S(1)}, u32[]{:S(2)}, u32[]{:S(2)}) collective-permute-start(bf16[32,1024]{1,0:T(8,128)(2,1)S(1)} %get-tuple-element.48), channel_id=1, source_target_pairs={{0,24},{1,25},{2,26},{3,27},{4,28},{5,29},{6,30},{7,31},{8,0},{9,1... | collective-permute-start | bytes 196616 | tf_op jit(solution)/shard_map/ppermute | solution.py:398
  153.0 13.3 %collective-permute-start.5 = (bf16[32,2176]{1,0:T(8,128)(2,1)S(1)}, bf16[32,2176]{1,0:T(8,128)(2,1)S(1)}, u32[]{:S(2)}, u32[]{:S(2)}) collective-permute-start(bf16[32,2176]{1,0:T(8,128)(2,1)S(1)} %pass_down.1), channel_id=1, source_target_pairs={{0,24},{1,25},{2,26},{3,27},{4,28},{5,29},{6,30},{7,31},{8,0},{9,1... | collective-permute-start | bytes 417800 | tf_op jit(solution)/shard_map/ppermute | solution.py:398
  160.5 14.7 %collective-permute-start.3 = (bf16[32,2176]{1,0:T(8,128)(2,1)S(1)}, bf16[32,2176]{1,0:T(8,128)(2,1)S(1)}, u32[]{:S(2)}, u32[]{:S(2)}) collective-permute-start(bf16[32,2176]{1,0:T(8,128)(2,1)S(1)} %pass_up.1), channel_id=1, source_target_pairs={{0,8},{1,9},{2,10},{3,11},{4,12},{5,13},{6,14},{7,15},{8,16},{9,17... | collective-permute-start | bytes 417800 | tf_op jit(solution)/shard_map/ppermute | solution.py:398
Sparse Core Ops, SparseCore 0:
  10.1 72.3 all-gather.2
  119.2 41.9 reduce-scatter.1

commit v8 on v7

--- a/solution.py
+++ b/solution.py
@@ -25,9 +25,17 @@
     return values.T[:columns, :rows] if columns < META else values.T[:, :rows]
 
 
+def even_first(hidden, rows):
+    src = lax.broadcasted_iota(jnp.int32, (hidden, hidden), 0)
+    at = lax.broadcasted_iota(jnp.int32, (1, hidden), 1)
+    half = hidden // 2
+    want = (2 * (at % half // rows) + at // half) * rows + at % rows
+    return (src == want).astype(BF16)
+
+
 def prep_kernel(
     rows_ref, ids_ref, weight_ref, gate_ref, up_ref, down_ref, tok_ref, pack_ref, downs_ref,
-    tok_buf, pack_buf, down_buf, ids_buf, weight_buf, in_sems, out_sems,
+    tok_buf, gate_buf, up_buf, pack_buf, down_buf, ids_buf, weight_buf, in_sems, out_sems,
 ):
     tok, width = rows_ref.shape
     topk = ids_ref.shape[0]
@@ -37,8 +45,8 @@
         pltpu.make_async_copy(weight_ref, weight_buf, in_sems.at[1]),
         pltpu.make_async_copy(down_ref, down_buf, in_sems.at[2]),
         pltpu.make_async_copy(rows_ref, tok_buf.at[:, pl.ds(0, width)], in_sems.at[3]),
-        pltpu.make_async_copy(gate_ref, pack_buf.at[:, pl.ds(0, hidden)], in_sems.at[4]),
-        pltpu.make_async_copy(up_ref, pack_buf.at[:, pl.ds(hidden, hidden)], in_sems.at[5]),
+        pltpu.make_async_copy(gate_ref, gate_buf, in_sems.at[4]),
+        pltpu.make_async_copy(up_ref, up_buf, in_sems.at[5]),
     ]
     for copy in copies:
         copy.start()
@@ -56,8 +64,11 @@
     copies[3].wait()
     outs.append(pltpu.make_async_copy(tok_buf, tok_ref, out_sems.at[0]))
     outs[-1].start()
+    order = even_first(hidden, down_ref.shape[0])
     copies[4].wait()
+    pack_buf[:, :hidden] = jnp.dot(gate_buf[...], order, preferred_element_type=F32).astype(BF16)
     copies[5].wait()
+    pack_buf[:, hidden:] = jnp.dot(up_buf[...], order, preferred_element_type=F32).astype(BF16)
     outs.append(pltpu.make_async_copy(pack_buf, pack_ref, out_sems.at[1]))
     outs[-1].start()
     for copy in outs:
@@ -102,16 +113,18 @@
     j, rest = at // (STRIDE * cap), at % (STRIDE * cap)
     k, r = rest // cap, rest % cap
     order = (src == (k * dests + j) * cap + r).astype(BF16)
-    a = jnp.dot(order, pre_ref[:, :hidden], preferred_element_type=F32)
-    u = jnp.dot(order, pre_ref[:, hidden:], preferred_element_type=F32)
+    columns = even_first(hidden, rows)
+    a, u = (
+        jnp.dot(
+            jnp.dot(order, part, preferred_element_type=F32).astype(BF16), columns, preferred_element_type=F32
+        )
+        for part in (pre_ref[:, :hidden], pre_ref[:, hidden:])
+    )
     sig = jax.nn.sigmoid(a)
     silu = a * sig
     hid = (silu * u).astype(BF16)
     hid_ref[...] = hid
-    turned = hid.astype(F32).T.astype(BF16)
-    for block in range(hidden // rows):
-        at = (block % 2) * (hidden // 2) + (block // 2) * rows
-        turned_ref[at : at + rows, :] = turned[block * rows : (block + 1) * rows]
+    turned_ref[...] = hid.astype(F32).T.astype(BF16)
     slope_ref[...] = u * sig * (1.0 + a * (1.0 - sig))
     silu_ref[...] = silu
 
@@ -138,45 +151,35 @@
 
 def mid_kernel(
     mine_ref, got_ref, own_ref, other_ref, hid_ref, slope_ref, silu_ref, pack_ref, out_ref, scaled_ref,
-    out_buf, both_buf, scaled_buf, down_buf, hid_buf, slope_buf, silu_buf, wide_buf, in_sems, out_sems,
+    out_buf, both_buf, scaled_buf, q_buf, wide_buf, in_sem, out_sems,
 ):
     width = got_ref.shape[1] - META
     hidden = hid_ref.shape[1]
+    half = hidden // 2
     devices, wide, both = wide_buf.shape
     core = mine_ref[1]
-    places = (
-        (own_ref, down_buf.at[:, core]),
-        (other_ref, down_buf.at[:, 1 - core]),
-        (hid_ref, hid_buf),
-        (slope_ref, slope_buf),
-        (silu_ref, silu_buf),
-        (pack_ref, wide_buf),
-    )
-    copies = [pltpu.make_async_copy(src, dst, in_sems.at[n]) for n, (src, dst) in enumerate(places)]
-    for copy in copies:
-        copy.start()
+    wide_copy = pltpu.make_async_copy(pack_ref, wide_buf, in_sem)
+    wide_copy.start()
     w = slot_weight(got_ref[:, width:], mine_ref[0])
     scaled_buf[...] = (w * got_ref[:, :width].astype(F32)).astype(BF16)
     steps = out_sems.shape[0] - 1
     backs = [pltpu.make_async_copy(scaled_buf, scaled_ref, out_sems.at[steps])]
     backs[0].start()
-    copies[0].wait()
-    copies[1].wait()
-    q = lax.dot_general(
-        got_ref[:, :width],
-        down_buf[...].reshape(hidden, width),
-        (((1,), (1,)), ((), ())),
-        preferred_element_type=F32,
-    )
-    for copy in copies[2:5]:
-        copy.wait()
-    route = jnp.sum(q * hid_buf[...].astype(F32), axis=1, keepdims=True)
+    for ref, which in ((own_ref, core), (other_ref, 1 - core)):
+        q_buf[:, pl.ds(pl.multiple_of(which * half, half), half)] = lax.dot_general(
+            got_ref[:, :width],
+            ref[...].reshape(half, width),
+            (((1,), (1,)), ((), ())),
+            preferred_element_type=F32,
+        )
+    q = q_buf[...]
+    route = jnp.sum(q * hid_ref[...].astype(F32), axis=1, keepdims=True)
     grad = w * q
-    both_buf[:, :hidden] = (grad * slope_buf[...]).astype(BF16)
-    both_buf[:, hidden:] = (grad * silu_buf[...]).astype(BF16)
+    both_buf[:, :hidden] = (grad * slope_ref[...]).astype(BF16)
+    both_buf[:, hidden:] = (grad * silu_ref[...]).astype(BF16)
     lane = lax.broadcasted_iota(jnp.int32, (got_ref.shape[0], META), 1)
     out_buf[:, width:] = jnp.where(lane == mine_ref[0], route, 0.0).astype(BF16)
-    copies[5].wait()
+    wide_copy.wait()
     group = devices // steps
     for n in range(steps):
         at, size = n * group * wide, group * wide
@@ -291,6 +294,8 @@
         out_specs=(whole(pltpu.HBM),) * 3,
         scratch_shapes=[
             pltpu.VMEM((tok, full), BF16),
+            pltpu.VMEM((wide, hidden), BF16),
+            pltpu.VMEM((wide, hidden), BF16),
             pltpu.VMEM((wide, both), BF16),
             pltpu.VMEM((down_rows, width), BF16),
             pltpu.VMEM((expert_ids.shape[1], tok), jnp.int32),
@@ -336,18 +341,15 @@
     back, scaled = pl.pallas_call(
         mid_kernel,
         out_shape=(shape((slots, full)), shape((slots, width))),
-        in_specs=[whole(pltpu.SMEM), whole()] + [whole(pltpu.HBM)] * 6,
+        in_specs=[whole(pltpu.SMEM)] + [whole()] * 6 + [whole(pltpu.HBM)],
         out_specs=(whole(pltpu.HBM),) * 2,
         scratch_shapes=[
             pltpu.VMEM((slots, full), BF16),
             pltpu.VMEM((slots, both), BF16),
             pltpu.VMEM((slots, width), BF16),
-            pltpu.VMEM((chips, 2, down_rows, width), BF16),
-            pltpu.VMEM((slots, hidden), BF16),
-            pltpu.VMEM((slots, hidden), F32),
             pltpu.VMEM((slots, hidden), F32),
             pltpu.VMEM((n_dp, wide, both), BF16),
-            pltpu.SemaphoreType.DMA((6,)),
+            pltpu.SemaphoreType.DMA,
             pltpu.SemaphoreType.DMA((5,)),
         ],
         compiler_params=params(50),

time: 185 us -> 187 us (1.011)
  Pallas kernels: 20.2 us -> 23.3 us
  transfers between devices with their start and end apart: 11 -> 11, of which waited for: 6 -> 6; matrix products, arithmetic and copies ran while one was open for 1% -> 1% of each run, Pallas kernels for 4% -> 5%
where the time goes in v8:
time: 187 us; the launch traced here: 185 us
  waiting for transfers between devices  60.9 us (33%)
  starting transfers between devices  49.1 us (26%)
  blocking collectives  32 us (17%)
  Pallas kernels  23.3 us (12%)
  between operations  14.2 us (8%)
  local copies, waits for them, and re-layouts  3.49 us (2%)
  other arithmetic  1.88 us (1%)
    all_to_all x3, waiting for transfers between devices, exchange(): lax.all_to_all(value, axes, 0, 0, axis_index_groups=groups, tiled=True)  42.4 us
    all_gather x1, blocking collectives, per_device(): lax.all_gather(rows, axes, axis=0, tiled=True, axis_index_groups=apart)  32 us
    all_to_all x3, starting transfers between devices, exchange(): lax.all_to_all(value, axes, 0, 0, axis_index_groups=groups, tiled=True)  22.1 us
    ppermute x4, starting transfers between devices, hop(): return lax.ppermute(value, 'expert', perm)  18.6 us
    ppermute x4, waiting for transfers between devices, hop(): return lax.ppermute(value, 'expert', perm)  15.1 us
    pallas_call x1, Pallas kernels, per_device(): pl.pallas_call(mid_kernel, out_shape=(shape((slots, full)), shape((slots,...  11.5 us
    ppermute x1, starting transfers between devices, per_device(): other_down = lax.ppermute(own_down, 'dp', swap)  6.41 us
  transfers between devices with their start and end apart: 11, of which 6 were waited for; matrix products, arithmetic and copies ran while one was open for 1% of the time, Pallas kernels for 5%

profile of v8, /device:TPU:1, one launch (start us, length us, event | category | flops | bytes accessed | tf_op | source)
XLA Modules:
  0.0 184.9 jit_solution(11157540037294575575)
XLA Ops:
  7.2 0.0 all-gather.3.cloned.1.call-start
  7.2 3.0 %prep.1 = (bf16[32,2176]{1,0:T(8,128)(2,1)}, bf16[128,1536]{1,0:T(8,128)(2,1)}, bf16[8,48,2048]{2,1,0:T(8,128)(2,1)}) custom-call(bf16[32,2048]{1,0:T(8,128)(2,1)} %rows_ref.1, s32[8,32]{1,0:T(8,128)} %bitcast.16, bf16[8,32]{1,0:T(8,128)(2,1)} %bitcast.24, bf16[128,768]{1,0:T(8,128)(2,1)} %bitcast.21, bf16[128,768]{1,0:T(8,128)(2,1)} %bitcast.22, ...), custom_call_target="tpu_custom_call" | custom-call | tf_op jit(solution)/shard_map/prep/pallas_call | solution.py:290
  10.2 0.0 all-gather.3.cloned.1.call-update
  10.3 6.1 %all-to-all-start = ((bf16[8,48,2048]{2,1,0:T(8,128)(2,1)}), bf16[8,48,2048]{2,1,0:T(8,128)(2,1)}, u32[]{:S(2)}, u32[]{:S(2)}) async-start(bf16[8,48,2048]{2,1,0:T(8,128)(2,1)} %get-tuple-element.29), calls=%async_computation | async-start | bytes 3145728 | tf_op jit(solution)/shard_map/all_to_all | solution.py:248
  16.4 32.0 %all_gather.9.tok_ref = bf16[128,2176]{1,0:T(8,128)(2,1)S(1)} all-gather(bf16[32,2176]{1,0:T(8,128)(2,1)S(1)} %copy-done.5), channel_id=1, replica_groups={{0,8,16,24},{1,9,17,25},{2,10,18,26},{3,11,19,27},{4,12,20,28},{5,13,21..., dimensions={0}, use_global_device_ids=true | all-gather | bytes 696320 | tf_op jit(solution)/shard_map/all_gather | solution.py:315
  48.4 2.6 %select.27 = (bf16[8,48,2176]{2,1,0:T(8,128)(2,1)}, bf16[384,128]{1,0:T(8,128)(2,1)S(1)}) custom-call(s32[8]{0:T(128)S(1)} %fusion.mine_ref, bf16[128,2176]{1,0:T(8,128)(2,1)S(1)} %all_gather.9.tok_ref), custom_call_target="tpu_custom_call" | custom-call | tf_op jit(solution)/shard_map/select/pallas_call | solution.py:316
  50.9 4.3 %all-to-all-start.1 = ((bf16[8,48,2176]{2,1,0:T(8,128)(2,1)}), bf16[8,48,2176]{2,1,0:T(8,128)(2,1)}, u32[]{:S(2)}, u32[]{:S(2)}) async-start(bf16[8,48,2176]{2,1,0:T(8,128)(2,1)} %get-tuple-element.31), calls=%async_computation.1 | async-start | bytes 3342336 | tf_op jit(solution)/shard_map/all_to_all | solution.py:248
  55.2 6.4 %collective-permute-start = (bf16[8,48,2048]{2,1,0:T(8,128)(2,1)}, bf16[8,48,2048]{2,1,0:T(8,128)(2,1)}, u32[]{:S(2)}, u32[]{:S(2)}) collective-permute-start(bf16[8,48,2048]{2,1,0:T(8,128)(2,1)} %all-to-all-done.own_ref), channel_id=1, source_target_pairs={{0,32},{32,0},{64,96},{96,64},{128,160},{160,128},{192,224},{224,1... | collective-permute-start | bytes 4718600 | tf_op jit(solution)/shard_map/ppermute | solution.py:325
  61.7 1.3 copy-done.2
  62.9 2.3 %act.1 = (bf16[384,768]{1,0:T(8,128)(2,1)S(1)}, bf16[768,384]{1,0:T(8,128)(2,1)S(1)}, f32[384,768]{1,0:T(8,128)S(1)}, f32[384,768]{1,0:T(8,128)S(1)}) custom-call(bf16[384,1536]{1,0:T(8,128)(2,1)S(1)} %bitcast.18), custom_call_target="tpu_custom_call" | custom-call | flops 452984832 | bytes 4718592 | tf_op jit(solution)/shard_map/act/pallas_call | solution.py:327
  65.3 0.8 copy-done.3
  66.1 0.1 pad_add_fusion.mine_ref
  66.1 20.8 %all-to-all-done.1 = bf16[8,48,2176]{2,1,0:T(8,128)(2,1)} async-done(((bf16[8,48,2176]{2,1,0:T(8,128)(2,1)}), bf16[8,48,2176]{2,1,0:T(8,128)(2,1)}, u32[]{:S(2)}, u32[]{:S(2)}) %all-to-all-start.1) | async-done | bytes 1671200 | tf_op jit(solution)/shard_map/all_to_all | solution.py:248
  86.9 11.5 %mid.1 = (bf16[384,2176]{1,0:T(8,128)(2,1)}, bf16[384,2048]{1,0:T(8,128)(2,1)}) custom-call(s32[2]{0:T(128)S(1)} %pad_add_fusion.mine_ref, bf16[384,2176]{1,0:T(8,128)(2,1)} %bitcast.8.got_ref, bf16[8,48,2048]{2,1,0:T(8,128)(2,1)} %all-to-all-done.own_ref, bf16[8,48,2048]{2,1,0:T(8,128)(2,1)} %collective-permute-done.other_ref, ...), custom_call_target="tpu_custom_call" | custom-call | flops 3623878656 | bytes 9437184 | tf_op jit(solution)/shard_map/mid/pallas_call | solution.py:341
  98.4 11.7 %all-to-all-start.2 = ((bf16[8,48,2176]{2,1,0:T(8,128)(2,1)}), bf16[8,48,2176]{2,1,0:T(8,128)(2,1)S(1)}, u32[]{:S(2)}, u32[]{:S(2)}) async-start(bf16[8,48,2176]{2,1,0:T(8,128)(2,1)} %bitcast.20), calls=%async_computation.2 | async-start | bytes 3342336 | tf_op jit(solution)/shard_map/all_to_all | solution.py:248
  110.1 0.0 reduce-scatter.2.cloned.1.call-start
  110.2 1.4 copy-done.1
  111.6 2.4 %down.1 = (bf16[384,2048]{1,0:T(8,128)(2,1)S(1)}, bf16[384,2048]{1,0:T(8,128)(2,1)S(1)}) custom-call(s32[2]{0:T(128)S(1)} %pad_add_fusion.mine_ref, bf16[384,2048]{1,0:T(8,128)(2,1)S(1)} %copy-done.1, bf16[768,384]{1,0:T(8,128)(2,1)S(1)} %copy-done.4), custom_call_target="tpu_custom_call" | custom-call | flops 1207959552 | bytes 4718592 | tf_op jit(solution)/shard_map/down/pallas_call | solution.py:360
  114.0 1.9 %collective-permute-start.1 = (bf16[384,2048]{1,0:T(8,128)(2,1)S(1)}, bf16[384,2048]{1,0:T(8,128)(2,1)S(1)}, u32[]{:S(2)}, u32[]{:S(2)}) collective-permute-start(bf16[384,2048]{1,0:T(8,128)(2,1)S(1)} %get-tuple-element.42), channel_id=1, source_target_pairs={{0,32},{32,0},{64,96},{96,64},{128,160},{160,128},{192,224},{224,1... | collective-permute-start | bytes 4718600 | tf_op jit(solution)/shard_map/ppermute | solution.py:369
  115.9 3.4 %collective-permute-done.1 = bf16[384,2048]{1,0:T(8,128)(2,1)S(1)} collective-permute-done((bf16[384,2048]{1,0:T(8,128)(2,1)S(1)}, bf16[384,2048]{1,0:T(8,128)(2,1)S(1)}, u32[]{:S(2)}, u32[]{:S(2)}) %collective-permute-start.1) | collective-permute-done | bytes 1572896 | tf_op jit(solution)/shard_map/ppermute | solution.py:369
  119.3 1.8 add_convert_fusion
  121.1 0.0 reduce-scatter.2.cloned.1.call-update
  121.1 21.6 %all-to-all-done.2 = bf16[8,48,2176]{2,1,0:T(8,128)(2,1)S(1)} async-done(((bf16[8,48,2176]{2,1,0:T(8,128)(2,1)}), bf16[8,48,2176]{2,1,0:T(8,128)(2,1)S(1)}, u32[]{:S(2)}, u32[]{:S(2)}) %all-to-all-start.2) | async-done | bytes 1671200 | tf_op jit(solution)/shard_map/all_to_all | solution.py:248
  142.7 0.6 combine.1
  143.3 1.9 %collective-permute-start.2 = (bf16[32,1152]{1,0:T(8,128)(2,1)S(1)}, bf16[32,1152]{1,0:T(8,128)(2,1)S(1)}, u32[]{:S(2)}, u32[]{:S(2)}) collective-permute-start(bf16[32,1152]{1,0:T(8,128)(2,1)S(1)} %get-tuple-element.46), channel_id=1, source_target_pairs={{0,8},{1,9},{2,10},{3,11},{4,12},{5,13},{6,14},{7,15},{8,16},{9,17... | collective-permute-start | bytes 221192 | tf_op jit(solution)/shard_map/ppermute | solution.py:400
  145.2 7.3 %collective-permute-start.4 = (bf16[32,1024]{1,0:T(8,128)(2,1)S(1)}, bf16[32,1024]{1,0:T(8,128)(2,1)S(1)}, u32[]{:S(2)}, u32[]{:S(2)}) collective-permute-start(bf16[32,1024]{1,0:T(8,128)(2,1)S(1)} %get-tuple-element.48), channel_id=1, source_target_pairs={{0,24},{1,25},{2,26},{3,27},{4,28},{5,29},{6,30},{7,31},{8,0},{9,1... | collective-permute-start | bytes 196616 | tf_op jit(solution)/shard_map/ppermute | solution.py:400
  152.5 2.4 %collective-permute-done.4.more_ref = bf16[32,1024]{1,0:T(8,128)(2,1)S(1)} collective-permute-done((bf16[32,1024]{1,0:T(8,128)(2,1)S(1)}, bf16[32,1024]{1,0:T(8,128)(2,1)S(1)}, u32[]{:S(2)}, u32[]{:S(2)}) %collective-permute-start.4) | collective-permute-done | bytes 65568 | tf_op jit(solution)/shard_map/ppermute | solution.py:400
  155.0 7.5 %collective-permute-start.5 = (bf16[32,2176]{1,0:T(8,128)(2,1)S(1)}, bf16[32,2176]{1,0:T(8,128)(2,1)S(1)}, u32[]{:S(2)}, u32[]{:S(2)}) collective-permute-start(bf16[32,2176]{1,0:T(8,128)(2,1)S(1)} %pass_down.1), channel_id=1, source_target_pairs={{0,24},{1,25},{2,26},{3,27},{4,28},{5,29},{6,30},{7,31},{8,0},{9,1... | collective-permute-start | bytes 417800 | tf_op jit(solution)/shard_map/ppermute | solution.py:400
  162.5 1.9 %collective-permute-start.3 = (bf16[32,2176]{1,0:T(8,128)(2,1)S(1)}, bf16[32,2176]{1,0:T(8,128)(2,1)S(1)}, u32[]{:S(2)}, u32[]{:S(2)}) collective-permute-start(bf16[32,2176]{1,0:T(8,128)(2,1)S(1)} %pass_up.1), channel_id=1, source_target_pairs={{0,8},{1,9},{2,10},{3,11},{4,12},{5,13},{6,14},{7,15},{8,16},{9,17... | collective-permute-start | bytes 417800 | tf_op jit(solution)/shard_map/ppermute | solution.py:400
  164.5 3.9 %collective-permute-done.5.refs_2_ = bf16[32,2176]{1,0:T(8,128)(2,1)S(1)} collective-permute-done((bf16[32,2176]{1,0:T(8,128)(2,1)S(1)}, bf16[32,2176]{1,0:T(8,128)(2,1)S(1)}, u32[]{:S(2)}, u32[]{:S(2)}) %collective-permute-start.5) | collective-permute-done | bytes 139296 | tf_op jit(solution)/shard_map/ppermute | solution.py:400
  168.3 8.8 %collective-permute-done.3.refs_1_ = bf16[32,2176]{1,0:T(8,128)(2,1)S(1)} collective-permute-done((bf16[32,2176]{1,0:T(8,128)(2,1)S(1)}, bf16[32,2176]{1,0:T(8,128)(2,1)S(1)}, u32[]{:S(2)}, u32[]{:S(2)}) %collective-permute-start.3) | collective-permute-done | bytes 139296 | tf_op jit(solution)/shard_map/ppermute | solution.py:400
  177.2 0.9 last.1
  (17 shorter events, 0.1 us)
Async XLA Ops:
  7.2 79.7 %all-gather.3.cloned.1.call-start = ((), (), s32[]{:S(2)}) async-start(), calls=%async_computation.5 | async-start | bytes 6684672 | tf_op jit(solution)/shard_map/all_gather | solution.py:309
  10.3 6.1 %copy-start.5 = (bf16[32,2176]{1,0:T(8,128)(2,1)S(1)}, bf16[32,2176]{1,0:T(8,128)(2,1)}, u32[]{:S(2)}) copy-start(bf16[32,2176]{1,0:T(8,128)(2,1)} %get-tuple-element.27) | copy-start | bytes 417796
  10.3 40.6 %all-to-all-start = ((bf16[8,48,2048]{2,1,0:T(8,128)(2,1)}), bf16[8,48,2048]{2,1,0:T(8,128)(2,1)}, u32[]{:S(2)}, u32[]{:S(2)}) async-start(bf16[8,48,2048]{2,1,0:T(8,128)(2,1)} %get-tuple-element.29), calls=%async_computation | async-start | bytes 3145728 | tf_op jit(solution)/shard_map/all_to_all | solution.py:248
  50.9 36.0 %all-to-all-start.1 = ((bf16[8,48,2176]{2,1,0:T(8,128)(2,1)}), bf16[8,48,2176]{2,1,0:T(8,128)(2,1)}, u32[]{:S(2)}, u32[]{:S(2)}) async-start(bf16[8,48,2176]{2,1,0:T(8,128)(2,1)} %get-tuple-element.31), calls=%async_computation.1 | async-start | bytes 3342336 | tf_op jit(solution)/shard_map/all_to_all | solution.py:248
  55.2 10.9 %collective-permute-start = (bf16[8,48,2048]{2,1,0:T(8,128)(2,1)}, bf16[8,48,2048]{2,1,0:T(8,128)(2,1)}, u32[]{:S(2)}, u32[]{:S(2)}) collective-permute-start(bf16[8,48,2048]{2,1,0:T(8,128)(2,1)} %all-to-all-done.own_ref), channel_id=1, source_target_pairs={{0,32},{32,0},{64,96},{96,64},{128,160},{160,128},{192,224},{224,1... | collective-permute-start | bytes 4718600 | tf_op jit(solution)/shard_map/ppermute | solution.py:325
  61.7 1.3 copy-start.2
  65.3 0.8 copy-start.3
  98.4 11.8 %copy-start.4 = (bf16[768,384]{1,0:T(8,128)(2,1)S(1)}, bf16[768,384]{1,0:T(8,128)(2,1)}, u32[]{:S(2)}) copy-start(bf16[768,384]{1,0:T(8,128)(2,1)} %copy-done.3) | copy-start | bytes 1769476
  98.4 44.3 %all-to-all-start.2 = ((bf16[8,48,2176]{2,1,0:T(8,128)(2,1)}), bf16[8,48,2176]{2,1,0:T(8,128)(2,1)S(1)}, u32[]{:S(2)}, u32[]{:S(2)}) async-start(bf16[8,48,2176]{2,1,0:T(8,128)(2,1)} %bitcast.20), calls=%async_computation.2 | async-start | bytes 3342336 | tf_op jit(solution)/shard_map/all_to_all | solution.py:248
  110.1 67.9 %reduce-scatter.2.cloned.1.call-start = ((), (), s32[]{:S(2)}) async-start(), calls=%async_computation.4 | async-start | bytes 1769472 | tf_op jit(solution)/shard_map/reduce_scatter | solution.py:371
  110.2 1.4 copy-start.1
  114.0 5.3 %collective-permute-start.1 = (bf16[384,2048]{1,0:T(8,128)(2,1)S(1)}, bf16[384,2048]{1,0:T(8,128)(2,1)S(1)}, u32[]{:S(2)}, u32[]{:S(2)}) collective-permute-start(bf16[384,2048]{1,0:T(8,128)(2,1)S(1)} %get-tuple-element.42), channel_id=1, source_target_pairs={{0,32},{32,0},{64,96},{96,64},{128,160},{160,128},{192,224},{224,1... | collective-permute-start | bytes 4718600 | tf_op jit(solution)/shard_map/ppermute | solution.py:369
  121.1 56.1 %copy-start = (s32[32,8]{0,1:T(8,128)S(1)}, s32[32,8]{0,1:T(8,128)}, u32[]{:S(2)}) copy-start(s32[32,8]{0,1:T(8,128)} %param.8) | copy-start | bytes 3076
  143.3 19.2 %collective-permute-start.2 = (bf16[32,1152]{1,0:T(8,128)(2,1)S(1)}, bf16[32,1152]{1,0:T(8,128)(2,1)S(1)}, u32[]{:S(2)}, u32[]{:S(2)}) collective-permute-start(bf16[32,1152]{1,0:T(8,128)(2,1)S(1)} %get-tuple-element.46), channel_id=1, source_target_pairs={{0,8},{1,9},{2,10},{3,11},{4,12},{5,13},{6,14},{7,15},{8,16},{9,17... | collective-permute-start | bytes 221192 | tf_op jit(solution)/shard_map/ppermute | solution.py:400
  145.2 9.7 %collective-permute-start.4 = (bf16[32,1024]{1,0:T(8,128)(2,1)S(1)}, bf16[32,1024]{1,0:T(8,128)(2,1)S(1)}, u32[]{:S(2)}, u32[]{:S(2)}) collective-permute-start(bf16[32,1024]{1,0:T(8,128)(2,1)S(1)} %get-tuple-element.48), channel_id=1, source_target_pairs={{0,24},{1,25},{2,26},{3,27},{4,28},{5,29},{6,30},{7,31},{8,0},{9,1... | collective-permute-start | bytes 196616 | tf_op jit(solution)/shard_map/ppermute | solution.py:400
  155.0 13.4 %collective-permute-start.5 = (bf16[32,2176]{1,0:T(8,128)(2,1)S(1)}, bf16[32,2176]{1,0:T(8,128)(2,1)S(1)}, u32[]{:S(2)}, u32[]{:S(2)}) collective-permute-start(bf16[32,2176]{1,0:T(8,128)(2,1)S(1)} %pass_down.1), channel_id=1, source_target_pairs={{0,24},{1,25},{2,26},{3,27},{4,28},{5,29},{6,30},{7,31},{8,0},{9,1... | collective-permute-start | bytes 417800 | tf_op jit(solution)/shard_map/ppermute | solution.py:400
  162.5 14.6 %collective-permute-start.3 = (bf16[32,2176]{1,0:T(8,128)(2,1)S(1)}, bf16[32,2176]{1,0:T(8,128)(2,1)S(1)}, u32[]{:S(2)}, u32[]{:S(2)}) collective-permute-start(bf16[32,2176]{1,0:T(8,128)(2,1)S(1)} %pass_up.1), channel_id=1, source_target_pairs={{0,8},{1,9},{2,10},{3,11},{4,12},{5,13},{6,14},{7,15},{8,16},{9,17... | collective-permute-start | bytes 417800 | tf_op jit(solution)/shard_map/ppermute | solution.py:400
Sparse Core Ops, SparseCore 0:
  10.4 72.7 all-gather.2
  121.2 42.5 reduce-scatter.1

commit v9 on v7

--- a/solution.py
+++ b/solution.py
@@ -27,44 +27,40 @@
 
 def prep_kernel(
     rows_ref, ids_ref, weight_ref, gate_ref, up_ref, down_ref, tok_ref, pack_ref, downs_ref,
-    tok_buf, pack_buf, down_buf, ids_buf, weight_buf, in_sems, out_sems,
+    tok_buf, pack_buf, down_buf, in_sems, out_sems,
 ):
     tok, width = rows_ref.shape
     topk = ids_ref.shape[0]
     hidden = gate_ref.shape[1]
     copies = [
-        pltpu.make_async_copy(ids_ref, ids_buf, in_sems.at[0]),
-        pltpu.make_async_copy(weight_ref, weight_buf, in_sems.at[1]),
-        pltpu.make_async_copy(down_ref, down_buf, in_sems.at[2]),
-        pltpu.make_async_copy(rows_ref, tok_buf.at[:, pl.ds(0, width)], in_sems.at[3]),
-        pltpu.make_async_copy(gate_ref, pack_buf.at[:, pl.ds(0, hidden)], in_sems.at[4]),
-        pltpu.make_async_copy(up_ref, pack_buf.at[:, pl.ds(hidden, hidden)], in_sems.at[5]),
+        pltpu.make_async_copy(down_ref, down_buf, in_sems.at[0]),
+        pltpu.make_async_copy(rows_ref, tok_buf.at[:, pl.ds(0, width)], in_sems.at[1]),
+        pltpu.make_async_copy(gate_ref, pack_buf.at[:, pl.ds(0, hidden)], in_sems.at[2]),
+        pltpu.make_async_copy(up_ref, pack_buf.at[:, pl.ds(hidden, hidden)], in_sems.at[3]),
     ]
     for copy in copies:
         copy.start()
-    copies[0].wait()
-    copies[1].wait()
-    meta = jnp.concatenate([ids_buf[...].astype(F32), weight_buf[...].astype(F32)], axis=0)
+    meta = jnp.concatenate([ids_ref[...].astype(F32), weight_ref[...].astype(F32)], axis=0)
     meta = jnp.concatenate([meta, jnp.zeros((META - 2 * topk, tok), F32)], axis=0)
     tok_buf[:, width:] = turn(meta).astype(BF16)
-    copies[2].wait()
+    copies[0].wait()
     outs = [
         pltpu.make_async_copy(down_buf, downs_ref.at[i], out_sems.at[2 + i]) for i in range(downs_ref.shape[0])
     ]
     for copy in outs:
         copy.start()
-    copies[3].wait()
+    copies[1].wait()
     outs.append(pltpu.make_async_copy(tok_buf, tok_ref, out_sems.at[0]))
     outs[-1].start()
-    copies[4].wait()
-    copies[5].wait()
+    copies[2].wait()
+    copies[3].wait()
     outs.append(pltpu.make_async_copy(pack_buf, pack_ref, out_sems.at[1]))
     outs[-1].start()
     for copy in outs:
         copy.wait()
 
 
-def select_kernel(cap, mine_ref, tok_ref, send_ref, select_ref):
+def select_kernel(cap, mine_ref, tok_ref, send_ref, select_ref, send_buf, sems):
     rows, full = tok_ref.shape
     width = full - META
     dests, per, _ = send_ref.shape
@@ -89,8 +85,16 @@
     for j in range(dests):
         chosen = (key[j : j + 1, :] == pattern).astype(BF16)
         select_ref[j * per : (j + 1) * per, :] = chosen
-    sent = jnp.dot(select_ref[...], tok_ref[...], preferred_element_type=F32).astype(BF16)
-    send_ref[...] = sent.reshape(send_ref.shape)
+    cuts = [full * n // META // sems.shape[0] * META for n in range(sems.shape[0])] + [full]
+    copies = []
+    for n, (at, end) in enumerate(zip(cuts[:-1], cuts[1:])):
+        sent = jnp.dot(select_ref[...], tok_ref[:, at:end], preferred_element_type=F32).astype(BF16)
+        send_buf[:, :, at:end] = sent.reshape(dests, per, end - at)
+        part = pl.ds(at, end - at)
+        copies.append(pltpu.make_async_copy(send_buf.at[:, :, part], send_ref.at[:, :, part], sems.at[n]))
+        copies[-1].start()
+    for copy in copies:
+        copy.wait()
 
 
 def act_kernel(cap, rows, pre_ref, hid_ref, turned_ref, slope_ref, silu_ref):
@@ -287,15 +291,13 @@
     rows, pack, downs = pl.pallas_call(
         prep_kernel,
         out_shape=(shape((tok, full)), shape((wide, both)), shape((chips, down_rows, width))),
-        in_specs=[whole(pltpu.HBM)] * 6,
+        in_specs=[whole(pltpu.HBM), whole(), whole()] + [whole(pltpu.HBM)] * 3,
         out_specs=(whole(pltpu.HBM),) * 3,
         scratch_shapes=[
             pltpu.VMEM((tok, full), BF16),
             pltpu.VMEM((wide, both), BF16),
             pltpu.VMEM((down_rows, width), BF16),
-            pltpu.VMEM((expert_ids.shape[1], tok), jnp.int32),
-            pltpu.VMEM((expert_ids.shape[1], tok), BF16),
-            pltpu.SemaphoreType.DMA((6,)),
+            pltpu.SemaphoreType.DMA((4,)),
             pltpu.SemaphoreType.DMA((2 + chips,)),
         ],
         compiler_params=params(60),
@@ -312,7 +314,8 @@
         functools.partial(select_kernel, cap),
         out_shape=(shape((dests, per, full)), shape((slots, STRIDE * tok))),
         in_specs=[whole(pltpu.SMEM), whole()],
-        out_specs=(whole(), whole()),
+        out_specs=(whole(pltpu.HBM), whole()),
+        scratch_shapes=[pltpu.VMEM((dests, per, full), BF16), pltpu.SemaphoreType.DMA((3,))],
         compiler_params=params(16),
         name="select",
     )(members, blocks)

time: 185 us -> 187 us (1.011)
  no operation moved by 1% of the time
where the time goes in v9:
time: 187 us; the launch traced here: 184 us
  waiting for transfers between devices  61.9 us (33%)
  starting transfers between devices  49.9 us (27%)
  blocking collectives  31.5 us (17%)
  Pallas kernels  20.6 us (11%)
  between operations  14.3 us (8%)
  local copies, waits for them, and re-layouts  3.49 us (2%)
  other arithmetic  1.88 us (1%)
    all_to_all x3, waiting for transfers between devices, exchange(): lax.all_to_all(value, axes, 0, 0, axis_index_groups=groups, tiled=True)  43.3 us
    all_gather x1, blocking collectives, per_device(): lax.all_gather(rows, axes, axis=0, tiled=True, axis_index_groups=apart)  31.5 us
    all_to_all x3, starting transfers between devices, exchange(): lax.all_to_all(value, axes, 0, 0, axis_index_groups=groups, tiled=True)  22.6 us
    ppermute x4, starting transfers between devices, hop(): return lax.ppermute(value, 'expert', perm)  18.6 us
    ppermute x4, waiting for transfers between devices, hop(): return lax.ppermute(value, 'expert', perm)  15.1 us
    pallas_call x1, Pallas kernels, per_device(): pl.pallas_call(mid_kernel, out_shape=(shape((slots, full)), shape((slots,...  10.1 us
    ppermute x1, starting transfers between devices, per_device(): other_down = lax.ppermute(own_down, 'dp', swap)  6.62 us
  transfers between devices with their start and end apart: 11, of which 6 were waited for; matrix products, arithmetic and copies ran while one was open for 1% of the time, Pallas kernels for 4%

profile of v9, /device:TPU:1, one launch (start us, length us, event | category | flops | bytes accessed | tf_op | source)
XLA Modules:
  0.0 183.5 jit_solution(3054234050372965156)
XLA Ops:
  7.2 0.0 all-gather.3.cloned.1.call-start
  7.2 3.1 %prep.1 = (bf16[32,2176]{1,0:T(8,128)(2,1)}, bf16[128,1536]{1,0:T(8,128)(2,1)}, bf16[8,48,2048]{2,1,0:T(8,128)(2,1)}) custom-call(bf16[32,2048]{1,0:T(8,128)(2,1)} %rows_ref.1, s32[8,32]{1,0:T(8,128)} %bitcast.16, bf16[8,32]{1,0:T(8,128)(2,1)} %bitcast.24, bf16[128,768]{1,0:T(8,128)(2,1)} %bitcast.21, bf16[128,768]{1,0:T(8,128)(2,1)} %bitcast.22, ...), custom_call_target="tpu_custom_call" | custom-call | tf_op jit(solution)/shard_map/prep/pallas_call | solution.py:291
  10.3 0.0 all-gather.3.cloned.1.call-update
  10.3 6.1 %all-to-all-start = ((bf16[8,48,2048]{2,1,0:T(8,128)(2,1)}), bf16[8,48,2048]{2,1,0:T(8,128)(2,1)}, u32[]{:S(2)}, u32[]{:S(2)}) async-start(bf16[8,48,2048]{2,1,0:T(8,128)(2,1)} %get-tuple-element.29), calls=%async_computation | async-start | bytes 3145728 | tf_op jit(solution)/shard_map/all_to_all | solution.py:249
  16.5 31.5 %all_gather.9.tok_ref = bf16[128,2176]{1,0:T(8,128)(2,1)S(1)} all-gather(bf16[32,2176]{1,0:T(8,128)(2,1)S(1)} %copy-done.5), channel_id=1, replica_groups={{0,8,16,24},{1,9,17,25},{2,10,18,26},{3,11,19,27},{4,12,20,28},{5,13,21..., dimensions={0}, use_global_device_ids=true | all-gather | bytes 696320 | tf_op jit(solution)/shard_map/all_gather | solution.py:312
  48.0 2.3 %select.27 = (bf16[8,48,2176]{2,1,0:T(8,128)(2,1)}, bf16[384,128]{1,0:T(8,128)(2,1)S(1)}) custom-call(s32[8]{0:T(128)S(1)} %fusion.mine_ref, bf16[128,2176]{1,0:T(8,128)(2,1)S(1)} %all_gather.9.tok_ref), custom_call_target="tpu_custom_call" | custom-call | tf_op jit(solution)/shard_map/select/pallas_call | solution.py:313
  50.3 4.5 %all-to-all-start.1 = ((bf16[8,48,2176]{2,1,0:T(8,128)(2,1)}), bf16[8,48,2176]{2,1,0:T(8,128)(2,1)}, u32[]{:S(2)}, u32[]{:S(2)}) async-start(bf16[8,48,2176]{2,1,0:T(8,128)(2,1)} %get-tuple-element.31), calls=%async_computation.1 | async-start | bytes 3342336 | tf_op jit(solution)/shard_map/all_to_all | solution.py:249
  54.8 6.6 %collective-permute-start = (bf16[8,48,2048]{2,1,0:T(8,128)(2,1)}, bf16[8,48,2048]{2,1,0:T(8,128)(2,1)}, u32[]{:S(2)}, u32[]{:S(2)}) collective-permute-start(bf16[8,48,2048]{2,1,0:T(8,128)(2,1)} %all-to-all-done.own_ref), channel_id=1, source_target_pairs={{0,32},{32,0},{64,96},{96,64},{128,160},{160,128},{192,224},{224,1... | collective-permute-start | bytes 4718600 | tf_op jit(solution)/shard_map/ppermute | solution.py:323
  61.5 1.3 copy-done.2
  62.7 1.3 act.1
  64.0 0.8 copy-done.3
  64.8 0.1 pad_add_fusion.mine_ref
  64.9 21.7 %all-to-all-done.1 = bf16[8,48,2176]{2,1,0:T(8,128)(2,1)} async-done(((bf16[8,48,2176]{2,1,0:T(8,128)(2,1)}), bf16[8,48,2176]{2,1,0:T(8,128)(2,1)}, u32[]{:S(2)}, u32[]{:S(2)}) %all-to-all-start.1) | async-done | bytes 1671200 | tf_op jit(solution)/shard_map/all_to_all | solution.py:249
  86.6 10.1 %mid.1 = (bf16[384,2176]{1,0:T(8,128)(2,1)}, bf16[384,2048]{1,0:T(8,128)(2,1)}) custom-call(s32[2]{0:T(128)S(1)} %pad_add_fusion.mine_ref, bf16[384,2176]{1,0:T(8,128)(2,1)} %bitcast.8.got_ref, bf16[8,48,2048]{2,1,0:T(8,128)(2,1)} %all-to-all-done.own_ref, bf16[8,48,2048]{2,1,0:T(8,128)(2,1)} %collective-permute-done.other_ref, ...), custom_call_target="tpu_custom_call" | custom-call | flops 3623878656 | bytes 9437184 | tf_op jit(solution)/shard_map/mid/pallas_call | solution.py:339
  96.7 12.0 %all-to-all-start.2 = ((bf16[8,48,2176]{2,1,0:T(8,128)(2,1)}), bf16[8,48,2176]{2,1,0:T(8,128)(2,1)S(1)}, u32[]{:S(2)}, u32[]{:S(2)}) async-start(bf16[8,48,2176]{2,1,0:T(8,128)(2,1)} %bitcast.20), calls=%async_computation.2 | async-start | bytes 3342336 | tf_op jit(solution)/shard_map/all_to_all | solution.py:249
  108.8 0.0 reduce-scatter.2.cloned.1.call-start
  108.8 1.4 copy-done.1
  110.2 2.4 %down.1 = (bf16[384,2048]{1,0:T(8,128)(2,1)S(1)}, bf16[384,2048]{1,0:T(8,128)(2,1)S(1)}) custom-call(s32[2]{0:T(128)S(1)} %pad_add_fusion.mine_ref, bf16[384,2048]{1,0:T(8,128)(2,1)S(1)} %copy-done.1, bf16[768,384]{1,0:T(8,128)(2,1)S(1)} %copy-done.4), custom_call_target="tpu_custom_call" | custom-call | flops 1207959552 | bytes 4718592 | tf_op jit(solution)/shard_map/down/pallas_call | solution.py:361
  112.6 1.9 %collective-permute-start.1 = (bf16[384,2048]{1,0:T(8,128)(2,1)S(1)}, bf16[384,2048]{1,0:T(8,128)(2,1)S(1)}, u32[]{:S(2)}, u32[]{:S(2)}) collective-permute-start(bf16[384,2048]{1,0:T(8,128)(2,1)S(1)} %get-tuple-element.42), channel_id=1, source_target_pairs={{0,32},{32,0},{64,96},{96,64},{128,160},{160,128},{192,224},{224,1... | collective-permute-start | bytes 4718600 | tf_op jit(solution)/shard_map/ppermute | solution.py:370
  114.5 3.4 %collective-permute-done.1 = bf16[384,2048]{1,0:T(8,128)(2,1)S(1)} collective-permute-done((bf16[384,2048]{1,0:T(8,128)(2,1)S(1)}, bf16[384,2048]{1,0:T(8,128)(2,1)S(1)}, u32[]{:S(2)}, u32[]{:S(2)}) %collective-permute-start.1) | collective-permute-done | bytes 1572896 | tf_op jit(solution)/shard_map/ppermute | solution.py:370
  117.9 1.8 add_convert_fusion
  119.7 0.0 reduce-scatter.2.cloned.1.call-update
  119.7 21.6 %all-to-all-done.2 = bf16[8,48,2176]{2,1,0:T(8,128)(2,1)S(1)} async-done(((bf16[8,48,2176]{2,1,0:T(8,128)(2,1)}), bf16[8,48,2176]{2,1,0:T(8,128)(2,1)S(1)}, u32[]{:S(2)}, u32[]{:S(2)}) %all-to-all-start.2) | async-done | bytes 1671200 | tf_op jit(solution)/shard_map/all_to_all | solution.py:249
  141.4 0.6 combine.1
  141.9 1.9 %collective-permute-start.2 = (bf16[32,1152]{1,0:T(8,128)(2,1)S(1)}, bf16[32,1152]{1,0:T(8,128)(2,1)S(1)}, u32[]{:S(2)}, u32[]{:S(2)}) collective-permute-start(bf16[32,1152]{1,0:T(8,128)(2,1)S(1)} %get-tuple-element.46), channel_id=1, source_target_pairs={{0,8},{1,9},{2,10},{3,11},{4,12},{5,13},{6,14},{7,15},{8,16},{9,17... | collective-permute-start | bytes 221192 | tf_op jit(solution)/shard_map/ppermute | solution.py:401
  143.9 7.3 %collective-permute-start.4 = (bf16[32,1024]{1,0:T(8,128)(2,1)S(1)}, bf16[32,1024]{1,0:T(8,128)(2,1)S(1)}, u32[]{:S(2)}, u32[]{:S(2)}) collective-permute-start(bf16[32,1024]{1,0:T(8,128)(2,1)S(1)} %get-tuple-element.48), channel_id=1, source_target_pairs={{0,24},{1,25},{2,26},{3,27},{4,28},{5,29},{6,30},{7,31},{8,0},{9,1... | collective-permute-start | bytes 196616 | tf_op jit(solution)/shard_map/ppermute | solution.py:401
  151.1 2.4 %collective-permute-done.4.more_ref = bf16[32,1024]{1,0:T(8,128)(2,1)S(1)} collective-permute-done((bf16[32,1024]{1,0:T(8,128)(2,1)S(1)}, bf16[32,1024]{1,0:T(8,128)(2,1)S(1)}, u32[]{:S(2)}, u32[]{:S(2)}) %collective-permute-start.4) | collective-permute-done | bytes 65568 | tf_op jit(solution)/shard_map/ppermute | solution.py:401
  153.6 7.5 %collective-permute-start.5 = (bf16[32,2176]{1,0:T(8,128)(2,1)S(1)}, bf16[32,2176]{1,0:T(8,128)(2,1)S(1)}, u32[]{:S(2)}, u32[]{:S(2)}) collective-permute-start(bf16[32,2176]{1,0:T(8,128)(2,1)S(1)} %pass_down.1), channel_id=1, source_target_pairs={{0,24},{1,25},{2,26},{3,27},{4,28},{5,29},{6,30},{7,31},{8,0},{9,1... | collective-permute-start | bytes 417800 | tf_op jit(solution)/shard_map/ppermute | solution.py:401
  161.2 1.9 %collective-permute-start.3 = (bf16[32,2176]{1,0:T(8,128)(2,1)S(1)}, bf16[32,2176]{1,0:T(8,128)(2,1)S(1)}, u32[]{:S(2)}, u32[]{:S(2)}) collective-permute-start(bf16[32,2176]{1,0:T(8,128)(2,1)S(1)} %pass_up.1), channel_id=1, source_target_pairs={{0,8},{1,9},{2,10},{3,11},{4,12},{5,13},{6,14},{7,15},{8,16},{9,17... | collective-permute-start | bytes 417800 | tf_op jit(solution)/shard_map/ppermute | solution.py:401
  163.1 3.8 %collective-permute-done.5.refs_2_ = bf16[32,2176]{1,0:T(8,128)(2,1)S(1)} collective-permute-done((bf16[32,2176]{1,0:T(8,128)(2,1)S(1)}, bf16[32,2176]{1,0:T(8,128)(2,1)S(1)}, u32[]{:S(2)}, u32[]{:S(2)}) %collective-permute-start.5) | collective-permute-done | bytes 139296 | tf_op jit(solution)/shard_map/ppermute | solution.py:401
  166.9 8.9 %collective-permute-done.3.refs_1_ = bf16[32,2176]{1,0:T(8,128)(2,1)S(1)} collective-permute-done((bf16[32,2176]{1,0:T(8,128)(2,1)S(1)}, bf16[32,2176]{1,0:T(8,128)(2,1)S(1)}, u32[]{:S(2)}, u32[]{:S(2)}) %collective-permute-start.3) | collective-permute-done | bytes 139296 | tf_op jit(solution)/shard_map/ppermute | solution.py:401
  175.8 0.9 last.1
  (17 shorter events, 0.1 us)
Async XLA Ops:
  7.2 79.5 %all-gather.3.cloned.1.call-start = ((), (), s32[]{:S(2)}) async-start(), calls=%async_computation.5 | async-start | bytes 6684672 | tf_op jit(solution)/shard_map/all_gather | solution.py:306
  10.3 6.1 %copy-start.5 = (bf16[32,2176]{1,0:T(8,128)(2,1)S(1)}, bf16[32,2176]{1,0:T(8,128)(2,1)}, u32[]{:S(2)}) copy-start(bf16[32,2176]{1,0:T(8,128)(2,1)} %get-tuple-element.27) | copy-start | bytes 417796
  10.3 40.0 %all-to-all-start = ((bf16[8,48,2048]{2,1,0:T(8,128)(2,1)}), bf16[8,48,2048]{2,1,0:T(8,128)(2,1)}, u32[]{:S(2)}, u32[]{:S(2)}) async-start(bf16[8,48,2048]{2,1,0:T(8,128)(2,1)} %get-tuple-element.29), calls=%async_computation | async-start | bytes 3145728 | tf_op jit(solution)/shard_map/all_to_all | solution.py:249
  50.3 36.3 %all-to-all-start.1 = ((bf16[8,48,2176]{2,1,0:T(8,128)(2,1)}), bf16[8,48,2176]{2,1,0:T(8,128)(2,1)}, u32[]{:S(2)}, u32[]{:S(2)}) async-start(bf16[8,48,2176]{2,1,0:T(8,128)(2,1)} %get-tuple-element.31), calls=%async_computation.1 | async-start | bytes 3342336 | tf_op jit(solution)/shard_map/all_to_all | solution.py:249
  54.8 10.1 %collective-permute-start = (bf16[8,48,2048]{2,1,0:T(8,128)(2,1)}, bf16[8,48,2048]{2,1,0:T(8,128)(2,1)}, u32[]{:S(2)}, u32[]{:S(2)}) collective-permute-start(bf16[8,48,2048]{2,1,0:T(8,128)(2,1)} %all-to-all-done.own_ref), channel_id=1, source_target_pairs={{0,32},{32,0},{64,96},{96,64},{128,160},{160,128},{192,224},{224,1... | collective-permute-start | bytes 4718600 | tf_op jit(solution)/shard_map/ppermute | solution.py:323
  61.5 1.3 copy-start.2
  64.0 0.8 copy-start.3
  96.7 12.1 %copy-start.4 = (bf16[768,384]{1,0:T(8,128)(2,1)S(1)}, bf16[768,384]{1,0:T(8,128)(2,1)}, u32[]{:S(2)}) copy-start(bf16[768,384]{1,0:T(8,128)(2,1)} %copy-done.3) | copy-start | bytes 1769476
  96.7 44.6 %all-to-all-start.2 = ((bf16[8,48,2176]{2,1,0:T(8,128)(2,1)}), bf16[8,48,2176]{2,1,0:T(8,128)(2,1)S(1)}, u32[]{:S(2)}, u32[]{:S(2)}) async-start(bf16[8,48,2176]{2,1,0:T(8,128)(2,1)} %bitcast.20), calls=%async_computation.2 | async-start | bytes 3342336 | tf_op jit(solution)/shard_map/all_to_all | solution.py:249
  108.8 67.9 %reduce-scatter.2.cloned.1.call-start = ((), (), s32[]{:S(2)}) async-start(), calls=%async_computation.4 | async-start | bytes 1769472 | tf_op jit(solution)/shard_map/reduce_scatter | solution.py:372
  108.8 1.4 copy-start.1
  112.6 5.3 %collective-permute-start.1 = (bf16[384,2048]{1,0:T(8,128)(2,1)S(1)}, bf16[384,2048]{1,0:T(8,128)(2,1)S(1)}, u32[]{:S(2)}, u32[]{:S(2)}) collective-permute-start(bf16[384,2048]{1,0:T(8,128)(2,1)S(1)} %get-tuple-element.42), channel_id=1, source_target_pairs={{0,32},{32,0},{64,96},{96,64},{128,160},{160,128},{192,224},{224,1... | collective-permute-start | bytes 4718600 | tf_op jit(solution)/shard_map/ppermute | solution.py:370
  119.7 56.1 %copy-start = (s32[32,8]{0,1:T(8,128)S(1)}, s32[32,8]{0,1:T(8,128)}, u32[]{:S(2)}) copy-start(s32[32,8]{0,1:T(8,128)} %param.8) | copy-start | bytes 3076
  141.9 19.2 %collective-permute-start.2 = (bf16[32,1152]{1,0:T(8,128)(2,1)S(1)}, bf16[32,1152]{1,0:T(8,128)(2,1)S(1)}, u32[]{:S(2)}, u32[]{:S(2)}) collective-permute-start(bf16[32,1152]{1,0:T(8,128)(2,1)S(1)} %get-tuple-element.46), channel_id=1, source_target_pairs={{0,8},{1,9},{2,10},{3,11},{4,12},{5,13},{6,14},{7,15},{8,16},{9,17... | collective-permute-start | bytes 221192 | tf_op jit(solution)/shard_map/ppermute | solution.py:401
  143.9 9.7 %collective-permute-start.4 = (bf16[32,1024]{1,0:T(8,128)(2,1)S(1)}, bf16[32,1024]{1,0:T(8,128)(2,1)S(1)}, u32[]{:S(2)}, u32[]{:S(2)}) collective-permute-start(bf16[32,1024]{1,0:T(8,128)(2,1)S(1)} %get-tuple-element.48), channel_id=1, source_target_pairs={{0,24},{1,25},{2,26},{3,27},{4,28},{5,29},{6,30},{7,31},{8,0},{9,1... | collective-permute-start | bytes 196616 | tf_op jit(solution)/shard_map/ppermute | solution.py:401
  153.6 13.3 %collective-permute-start.5 = (bf16[32,2176]{1,0:T(8,128)(2,1)S(1)}, bf16[32,2176]{1,0:T(8,128)(2,1)S(1)}, u32[]{:S(2)}, u32[]{:S(2)}) collective-permute-start(bf16[32,2176]{1,0:T(8,128)(2,1)S(1)} %pass_down.1), channel_id=1, source_target_pairs={{0,24},{1,25},{2,26},{3,27},{4,28},{5,29},{6,30},{7,31},{8,0},{9,1... | collective-permute-start | bytes 417800 | tf_op jit(solution)/shard_map/ppermute | solution.py:401
  161.2 14.6 %collective-permute-start.3 = (bf16[32,2176]{1,0:T(8,128)(2,1)S(1)}, bf16[32,2176]{1,0:T(8,128)(2,1)S(1)}, u32[]{:S(2)}, u32[]{:S(2)}) collective-permute-start(bf16[32,2176]{1,0:T(8,128)(2,1)S(1)} %pass_up.1), channel_id=1, source_target_pairs={{0,8},{1,9},{2,10},{3,11},{4,12},{5,13},{6,14},{7,15},{8,16},{9,17... | collective-permute-start | bytes 417800 | tf_op jit(solution)/shard_map/ppermute | solution.py:401
Sparse Core Ops, SparseCore 0:
  10.4 72.7 all-gather.2
  119.8 42.5 reduce-scatter.1

commit v10 on v7

--- a/solution.py
+++ b/solution.py
@@ -64,7 +64,7 @@
         copy.wait()
 
 
-def select_kernel(cap, mine_ref, tok_ref, send_ref, select_ref):
+def select_kernel(cap, mine_ref, tok_ref, send_ref, select_ref, send_buf, sems):
     rows, full = tok_ref.shape
     width = full - META
     dests, per, _ = send_ref.shape
@@ -89,8 +89,16 @@
     for j in range(dests):
         chosen = (key[j : j + 1, :] == pattern).astype(BF16)
         select_ref[j * per : (j + 1) * per, :] = chosen
-    sent = jnp.dot(select_ref[...], tok_ref[...], preferred_element_type=F32).astype(BF16)
-    send_ref[...] = sent.reshape(send_ref.shape)
+    cuts = [full * n // META // sems.shape[0] * META for n in range(sems.shape[0])] + [full]
+    copies = []
+    for n, (at, end) in enumerate(zip(cuts[:-1], cuts[1:])):
+        sent = jnp.dot(select_ref[...], tok_ref[:, at:end], preferred_element_type=F32).astype(BF16)
+        send_buf[:, :, at:end] = sent.reshape(dests, per, end - at)
+        part = pl.ds(at, end - at)
+        copies.append(pltpu.make_async_copy(send_buf.at[:, :, part], send_ref.at[:, :, part], sems.at[n]))
+        copies[-1].start()
+    for copy in copies:
+        copy.wait()
 
 
 def act_kernel(cap, rows, pre_ref, hid_ref, turned_ref, slope_ref, silu_ref):
@@ -312,7 +320,8 @@
         functools.partial(select_kernel, cap),
         out_shape=(shape((dests, per, full)), shape((slots, STRIDE * tok))),
         in_specs=[whole(pltpu.SMEM), whole()],
-        out_specs=(whole(), whole()),
+        out_specs=(whole(pltpu.HBM), whole()),
+        scratch_shapes=[pltpu.VMEM((dests, per, full), BF16), pltpu.SemaphoreType.DMA((3,))],
         compiler_params=params(16),
         name="select",
     )(members, blocks)

time: 185 us -> 186 us (level)
  no operation moved by 1% of the time
where the time goes in v10:
time: 186 us; the launch traced here: 183 us
  waiting for transfers between devices  62 us (33%)
  starting transfers between devices  49.9 us (27%)
  blocking collectives  31.5 us (17%)
  Pallas kernels  19.9 us (11%)
  between operations  14.3 us (8%)
  local copies, waits for them, and re-layouts  3.49 us (2%)
  other arithmetic  1.88 us (1%)
    all_to_all x3, waiting for transfers between devices, exchange(): lax.all_to_all(value, axes, 0, 0, axis_index_groups=groups, tiled=True)  43.3 us
    all_gather x1, blocking collectives, per_device(): lax.all_gather(rows, axes, axis=0, tiled=True, axis_index_groups=apart)  31.5 us
    all_to_all x3, starting transfers between devices, exchange(): lax.all_to_all(value, axes, 0, 0, axis_index_groups=groups, tiled=True)  22.6 us
    ppermute x4, starting transfers between devices, hop(): return lax.ppermute(value, 'expert', perm)  18.6 us
    ppermute x4, waiting for transfers between devices, hop(): return lax.ppermute(value, 'expert', perm)  15.2 us
    pallas_call x1, Pallas kernels, per_device(): pl.pallas_call(mid_kernel, out_shape=(shape((slots, full)), shape((slots,...  10.1 us
    ppermute x1, starting transfers between devices, per_device(): other_down = lax.ppermute(own_down, 'dp', swap)  6.62 us
  transfers between devices with their start and end apart: 11, of which 6 were waited for; matrix products, arithmetic and copies ran while one was open for 1% of the time, Pallas kernels for 4%

profile of v10, /device:TPU:1, one launch (start us, length us, event | category | flops | bytes accessed | tf_op | source)
XLA Modules:
  0.0 183.0 jit_solution(4870372134640561506)
XLA Ops:
  7.2 0.0 all-gather.3.cloned.1.call-start
  7.2 2.4 %prep.1 = (bf16[32,2176]{1,0:T(8,128)(2,1)}, bf16[128,1536]{1,0:T(8,128)(2,1)}, bf16[8,48,2048]{2,1,0:T(8,128)(2,1)}) custom-call(bf16[32,2048]{1,0:T(8,128)(2,1)} %rows_ref.1, s32[8,32]{1,0:T(8,128)} %bitcast.16, bf16[8,32]{1,0:T(8,128)(2,1)} %bitcast.24, bf16[128,768]{1,0:T(8,128)(2,1)} %bitcast.21, bf16[128,768]{1,0:T(8,128)(2,1)} %bitcast.22, ...), custom_call_target="tpu_custom_call" | custom-call | tf_op jit(solution)/shard_map/prep/pallas_call | solution.py:295
  9.6 0.0 all-gather.3.cloned.1.call-update
  9.7 6.1 %all-to-all-start = ((bf16[8,48,2048]{2,1,0:T(8,128)(2,1)}), bf16[8,48,2048]{2,1,0:T(8,128)(2,1)}, u32[]{:S(2)}, u32[]{:S(2)}) async-start(bf16[8,48,2048]{2,1,0:T(8,128)(2,1)} %get-tuple-element.29), calls=%async_computation | async-start | bytes 3145728 | tf_op jit(solution)/shard_map/all_to_all | solution.py:253
  15.8 31.5 %all_gather.9.tok_ref = bf16[128,2176]{1,0:T(8,128)(2,1)S(1)} all-gather(bf16[32,2176]{1,0:T(8,128)(2,1)S(1)} %copy-done.5), channel_id=1, replica_groups={{0,8,16,24},{1,9,17,25},{2,10,18,26},{3,11,19,27},{4,12,20,28},{5,13,21..., dimensions={0}, use_global_device_ids=true | all-gather | bytes 696320 | tf_op jit(solution)/shard_map/all_gather | solution.py:318
  47.3 2.3 %select.27 = (bf16[8,48,2176]{2,1,0:T(8,128)(2,1)}, bf16[384,128]{1,0:T(8,128)(2,1)S(1)}) custom-call(s32[8]{0:T(128)S(1)} %fusion.mine_ref, bf16[128,2176]{1,0:T(8,128)(2,1)S(1)} %all_gather.9.tok_ref), custom_call_target="tpu_custom_call" | custom-call | tf_op jit(solution)/shard_map/select/pallas_call | solution.py:319
  49.7 4.5 %all-to-all-start.1 = ((bf16[8,48,2176]{2,1,0:T(8,128)(2,1)}), bf16[8,48,2176]{2,1,0:T(8,128)(2,1)}, u32[]{:S(2)}, u32[]{:S(2)}) async-start(bf16[8,48,2176]{2,1,0:T(8,128)(2,1)} %get-tuple-element.31), calls=%async_computation.1 | async-start | bytes 3342336 | tf_op jit(solution)/shard_map/all_to_all | solution.py:253
  54.2 6.6 %collective-permute-start = (bf16[8,48,2048]{2,1,0:T(8,128)(2,1)}, bf16[8,48,2048]{2,1,0:T(8,128)(2,1)}, u32[]{:S(2)}, u32[]{:S(2)}) collective-permute-start(bf16[8,48,2048]{2,1,0:T(8,128)(2,1)} %all-to-all-done.own_ref), channel_id=1, source_target_pairs={{0,32},{32,0},{64,96},{96,64},{128,160},{160,128},{192,224},{224,1... | collective-permute-start | bytes 4718600 | tf_op jit(solution)/shard_map/ppermute | solution.py:329
  60.8 1.3 copy-done.2
  62.1 1.3 act.1
  63.4 0.8 copy-done.3
  64.2 0.1 pad_add_fusion.mine_ref
  64.3 21.7 %all-to-all-done.1 = bf16[8,48,2176]{2,1,0:T(8,128)(2,1)} async-done(((bf16[8,48,2176]{2,1,0:T(8,128)(2,1)}), bf16[8,48,2176]{2,1,0:T(8,128)(2,1)}, u32[]{:S(2)}, u32[]{:S(2)}) %all-to-all-start.1) | async-done | bytes 1671200 | tf_op jit(solution)/shard_map/all_to_all | solution.py:253
  86.0 10.1 %mid.1 = (bf16[384,2176]{1,0:T(8,128)(2,1)}, bf16[384,2048]{1,0:T(8,128)(2,1)}) custom-call(s32[2]{0:T(128)S(1)} %pad_add_fusion.mine_ref, bf16[384,2176]{1,0:T(8,128)(2,1)} %bitcast.8.got_ref, bf16[8,48,2048]{2,1,0:T(8,128)(2,1)} %all-to-all-done.own_ref, bf16[8,48,2048]{2,1,0:T(8,128)(2,1)} %collective-permute-done.other_ref, ...), custom_call_target="tpu_custom_call" | custom-call | flops 3623878656 | bytes 9437184 | tf_op jit(solution)/shard_map/mid/pallas_call | solution.py:345
  96.1 12.0 %all-to-all-start.2 = ((bf16[8,48,2176]{2,1,0:T(8,128)(2,1)}), bf16[8,48,2176]{2,1,0:T(8,128)(2,1)S(1)}, u32[]{:S(2)}, u32[]{:S(2)}) async-start(bf16[8,48,2176]{2,1,0:T(8,128)(2,1)} %bitcast.20), calls=%async_computation.2 | async-start | bytes 3342336 | tf_op jit(solution)/shard_map/all_to_all | solution.py:253
  108.1 0.0 reduce-scatter.2.cloned.1.call-start
  108.2 1.4 copy-done.1
  109.6 2.4 %down.1 = (bf16[384,2048]{1,0:T(8,128)(2,1)S(1)}, bf16[384,2048]{1,0:T(8,128)(2,1)S(1)}) custom-call(s32[2]{0:T(128)S(1)} %pad_add_fusion.mine_ref, bf16[384,2048]{1,0:T(8,128)(2,1)S(1)} %copy-done.1, bf16[768,384]{1,0:T(8,128)(2,1)S(1)} %copy-done.4), custom_call_target="tpu_custom_call" | custom-call | flops 1207959552 | bytes 4718592 | tf_op jit(solution)/shard_map/down/pallas_call | solution.py:367
  111.9 1.9 %collective-permute-start.1 = (bf16[384,2048]{1,0:T(8,128)(2,1)S(1)}, bf16[384,2048]{1,0:T(8,128)(2,1)S(1)}, u32[]{:S(2)}, u32[]{:S(2)}) collective-permute-start(bf16[384,2048]{1,0:T(8,128)(2,1)S(1)} %get-tuple-element.42), channel_id=1, source_target_pairs={{0,32},{32,0},{64,96},{96,64},{128,160},{160,128},{192,224},{224,1... | collective-permute-start | bytes 4718600 | tf_op jit(solution)/shard_map/ppermute | solution.py:376
  113.9 3.4 %collective-permute-done.1 = bf16[384,2048]{1,0:T(8,128)(2,1)S(1)} collective-permute-done((bf16[384,2048]{1,0:T(8,128)(2,1)S(1)}, bf16[384,2048]{1,0:T(8,128)(2,1)S(1)}, u32[]{:S(2)}, u32[]{:S(2)}) %collective-permute-start.1) | collective-permute-done | bytes 1572896 | tf_op jit(solution)/shard_map/ppermute | solution.py:376
  117.3 1.8 add_convert_fusion
  119.0 0.0 reduce-scatter.2.cloned.1.call-update
  119.1 21.6 %all-to-all-done.2 = bf16[8,48,2176]{2,1,0:T(8,128)(2,1)S(1)} async-done(((bf16[8,48,2176]{2,1,0:T(8,128)(2,1)}), bf16[8,48,2176]{2,1,0:T(8,128)(2,1)S(1)}, u32[]{:S(2)}, u32[]{:S(2)}) %all-to-all-start.2) | async-done | bytes 1671200 | tf_op jit(solution)/shard_map/all_to_all | solution.py:253
  140.7 0.6 combine.1
  141.3 1.9 %collective-permute-start.2 = (bf16[32,1152]{1,0:T(8,128)(2,1)S(1)}, bf16[32,1152]{1,0:T(8,128)(2,1)S(1)}, u32[]{:S(2)}, u32[]{:S(2)}) collective-permute-start(bf16[32,1152]{1,0:T(8,128)(2,1)S(1)} %get-tuple-element.46), channel_id=1, source_target_pairs={{0,8},{1,9},{2,10},{3,11},{4,12},{5,13},{6,14},{7,15},{8,16},{9,17... | collective-permute-start | bytes 221192 | tf_op jit(solution)/shard_map/ppermute | solution.py:407
  143.2 7.3 %collective-permute-start.4 = (bf16[32,1024]{1,0:T(8,128)(2,1)S(1)}, bf16[32,1024]{1,0:T(8,128)(2,1)S(1)}, u32[]{:S(2)}, u32[]{:S(2)}) collective-permute-start(bf16[32,1024]{1,0:T(8,128)(2,1)S(1)} %get-tuple-element.48), channel_id=1, source_target_pairs={{0,24},{1,25},{2,26},{3,27},{4,28},{5,29},{6,30},{7,31},{8,0},{9,1... | collective-permute-start | bytes 196616 | tf_op jit(solution)/shard_map/ppermute | solution.py:407
  150.5 2.4 %collective-permute-done.4.more_ref = bf16[32,1024]{1,0:T(8,128)(2,1)S(1)} collective-permute-done((bf16[32,1024]{1,0:T(8,128)(2,1)S(1)}, bf16[32,1024]{1,0:T(8,128)(2,1)S(1)}, u32[]{:S(2)}, u32[]{:S(2)}) %collective-permute-start.4) | collective-permute-done | bytes 65568 | tf_op jit(solution)/shard_map/ppermute | solution.py:407
  153.0 7.5 %collective-permute-start.5 = (bf16[32,2176]{1,0:T(8,128)(2,1)S(1)}, bf16[32,2176]{1,0:T(8,128)(2,1)S(1)}, u32[]{:S(2)}, u32[]{:S(2)}) collective-permute-start(bf16[32,2176]{1,0:T(8,128)(2,1)S(1)} %pass_down.1), channel_id=1, source_target_pairs={{0,24},{1,25},{2,26},{3,27},{4,28},{5,29},{6,30},{7,31},{8,0},{9,1... | collective-permute-start | bytes 417800 | tf_op jit(solution)/shard_map/ppermute | solution.py:407
  160.5 1.9 %collective-permute-start.3 = (bf16[32,2176]{1,0:T(8,128)(2,1)S(1)}, bf16[32,2176]{1,0:T(8,128)(2,1)S(1)}, u32[]{:S(2)}, u32[]{:S(2)}) collective-permute-start(bf16[32,2176]{1,0:T(8,128)(2,1)S(1)} %pass_up.1), channel_id=1, source_target_pairs={{0,8},{1,9},{2,10},{3,11},{4,12},{5,13},{6,14},{7,15},{8,16},{9,17... | collective-permute-start | bytes 417800 | tf_op jit(solution)/shard_map/ppermute | solution.py:407
  162.5 3.8 %collective-permute-done.5.refs_2_ = bf16[32,2176]{1,0:T(8,128)(2,1)S(1)} collective-permute-done((bf16[32,2176]{1,0:T(8,128)(2,1)S(1)}, bf16[32,2176]{1,0:T(8,128)(2,1)S(1)}, u32[]{:S(2)}, u32[]{:S(2)}) %collective-permute-start.5) | collective-permute-done | bytes 139296 | tf_op jit(solution)/shard_map/ppermute | solution.py:407
  166.3 8.9 %collective-permute-done.3.refs_1_ = bf16[32,2176]{1,0:T(8,128)(2,1)S(1)} collective-permute-done((bf16[32,2176]{1,0:T(8,128)(2,1)S(1)}, bf16[32,2176]{1,0:T(8,128)(2,1)S(1)}, u32[]{:S(2)}, u32[]{:S(2)}) %collective-permute-start.3) | collective-permute-done | bytes 139296 | tf_op jit(solution)/shard_map/ppermute | solution.py:407
  175.2 0.9 last.1
  (17 shorter events, 0.1 us)
Async XLA Ops:
  7.2 78.8 %all-gather.3.cloned.1.call-start = ((), (), s32[]{:S(2)}) async-start(), calls=%async_computation.5 | async-start | bytes 6684672 | tf_op jit(solution)/shard_map/all_gather | solution.py:312
  9.7 6.1 %copy-start.5 = (bf16[32,2176]{1,0:T(8,128)(2,1)S(1)}, bf16[32,2176]{1,0:T(8,128)(2,1)}, u32[]{:S(2)}) copy-start(bf16[32,2176]{1,0:T(8,128)(2,1)} %get-tuple-element.27) | copy-start | bytes 417796
  9.7 40.0 %all-to-all-start = ((bf16[8,48,2048]{2,1,0:T(8,128)(2,1)}), bf16[8,48,2048]{2,1,0:T(8,128)(2,1)}, u32[]{:S(2)}, u32[]{:S(2)}) async-start(bf16[8,48,2048]{2,1,0:T(8,128)(2,1)} %get-tuple-element.29), calls=%async_computation | async-start | bytes 3145728 | tf_op jit(solution)/shard_map/all_to_all | solution.py:253
  49.7 36.3 %all-to-all-start.1 = ((bf16[8,48,2176]{2,1,0:T(8,128)(2,1)}), bf16[8,48,2176]{2,1,0:T(8,128)(2,1)}, u32[]{:S(2)}, u32[]{:S(2)}) async-start(bf16[8,48,2176]{2,1,0:T(8,128)(2,1)} %get-tuple-element.31), calls=%async_computation.1 | async-start | bytes 3342336 | tf_op jit(solution)/shard_map/all_to_all | solution.py:253
  54.2 10.1 %collective-permute-start = (bf16[8,48,2048]{2,1,0:T(8,128)(2,1)}, bf16[8,48,2048]{2,1,0:T(8,128)(2,1)}, u32[]{:S(2)}, u32[]{:S(2)}) collective-permute-start(bf16[8,48,2048]{2,1,0:T(8,128)(2,1)} %all-to-all-done.own_ref), channel_id=1, source_target_pairs={{0,32},{32,0},{64,96},{96,64},{128,160},{160,128},{192,224},{224,1... | collective-permute-start | bytes 4718600 | tf_op jit(solution)/shard_map/ppermute | solution.py:329
  60.8 1.3 copy-start.2
  63.4 0.8 copy-start.3
  96.1 12.1 %copy-start.4 = (bf16[768,384]{1,0:T(8,128)(2,1)S(1)}, bf16[768,384]{1,0:T(8,128)(2,1)}, u32[]{:S(2)}) copy-start(bf16[768,384]{1,0:T(8,128)(2,1)} %copy-done.3) | copy-start | bytes 1769476
  96.1 44.6 %all-to-all-start.2 = ((bf16[8,48,2176]{2,1,0:T(8,128)(2,1)}), bf16[8,48,2176]{2,1,0:T(8,128)(2,1)S(1)}, u32[]{:S(2)}, u32[]{:S(2)}) async-start(bf16[8,48,2176]{2,1,0:T(8,128)(2,1)} %bitcast.20), calls=%async_computation.2 | async-start | bytes 3342336 | tf_op jit(solution)/shard_map/all_to_all | solution.py:253
  108.1 68.0 %reduce-scatter.2.cloned.1.call-start = ((), (), s32[]{:S(2)}) async-start(), calls=%async_computation.4 | async-start | bytes 1769472 | tf_op jit(solution)/shard_map/reduce_scatter | solution.py:378
  108.2 1.4 copy-start.1
  111.9 5.3 %collective-permute-start.1 = (bf16[384,2048]{1,0:T(8,128)(2,1)S(1)}, bf16[384,2048]{1,0:T(8,128)(2,1)S(1)}, u32[]{:S(2)}, u32[]{:S(2)}) collective-permute-start(bf16[384,2048]{1,0:T(8,128)(2,1)S(1)} %get-tuple-element.42), channel_id=1, source_target_pairs={{0,32},{32,0},{64,96},{96,64},{128,160},{160,128},{192,224},{224,1... | collective-permute-start | bytes 4718600 | tf_op jit(solution)/shard_map/ppermute | solution.py:376
  119.1 56.2 %copy-start = (s32[32,8]{0,1:T(8,128)S(1)}, s32[32,8]{0,1:T(8,128)}, u32[]{:S(2)}) copy-start(s32[32,8]{0,1:T(8,128)} %param.8) | copy-start | bytes 3076
  141.3 19.2 %collective-permute-start.2 = (bf16[32,1152]{1,0:T(8,128)(2,1)S(1)}, bf16[32,1152]{1,0:T(8,128)(2,1)S(1)}, u32[]{:S(2)}, u32[]{:S(2)}) collective-permute-start(bf16[32,1152]{1,0:T(8,128)(2,1)S(1)} %get-tuple-element.46), channel_id=1, source_target_pairs={{0,8},{1,9},{2,10},{3,11},{4,12},{5,13},{6,14},{7,15},{8,16},{9,17... | collective-permute-start | bytes 221192 | tf_op jit(solution)/shard_map/ppermute | solution.py:407
  143.2 9.7 %collective-permute-start.4 = (bf16[32,1024]{1,0:T(8,128)(2,1)S(1)}, bf16[32,1024]{1,0:T(8,128)(2,1)S(1)}, u32[]{:S(2)}, u32[]{:S(2)}) collective-permute-start(bf16[32,1024]{1,0:T(8,128)(2,1)S(1)} %get-tuple-element.48), channel_id=1, source_target_pairs={{0,24},{1,25},{2,26},{3,27},{4,28},{5,29},{6,30},{7,31},{8,0},{9,1... | collective-permute-start | bytes 196616 | tf_op jit(solution)/shard_map/ppermute | solution.py:407
  153.0 13.3 %collective-permute-start.5 = (bf16[32,2176]{1,0:T(8,128)(2,1)S(1)}, bf16[32,2176]{1,0:T(8,128)(2,1)S(1)}, u32[]{:S(2)}, u32[]{:S(2)}) collective-permute-start(bf16[32,2176]{1,0:T(8,128)(2,1)S(1)} %pass_down.1), channel_id=1, source_target_pairs={{0,24},{1,25},{2,26},{3,27},{4,28},{5,29},{6,30},{7,31},{8,0},{9,1... | collective-permute-start | bytes 417800 | tf_op jit(solution)/shard_map/ppermute | solution.py:407
  160.5 14.7 %collective-permute-start.3 = (bf16[32,2176]{1,0:T(8,128)(2,1)S(1)}, bf16[32,2176]{1,0:T(8,128)(2,1)S(1)}, u32[]{:S(2)}, u32[]{:S(2)}) collective-permute-start(bf16[32,2176]{1,0:T(8,128)(2,1)S(1)} %pass_up.1), channel_id=1, source_target_pairs={{0,8},{1,9},{2,10},{3,11},{4,12},{5,13},{6,14},{7,15},{8,16},{9,17... | collective-permute-start | bytes 417800 | tf_op jit(solution)/shard_map/ppermute | solution.py:407
Sparse Core Ops, SparseCore 0:
  10.1 72.3 all-gather.2
  119.2 41.9 reduce-scatter.1
